TPU v7x, 32 devices: a whole 2x2x4 slice. The times are simulated.
32 devices in a mesh: dp: 4 (over z), ctx: 4 (over y, x), chan: 2 (over core).
Axes of the slice: x: 2, y: 2, z: 4, core: 2. Of those that a mesh axis runs over, the one named last changes fastest.
Arguments:
- layer_input: bfloat16 [4096, 4096], P(('dp', 'chan'), 'ctx'), may hold values from -6 to 6
- grad_output: bfloat16 [4096, 4096], P(('dp', 'chan'), 'ctx'), may hold values from -6 to 6
- filter_taps: float32 [8, 512, 4096], P(('dp', 'chan'), 'ctx'), may hold values from -2 to 2
Outputs:
- grad_input: bfloat16 [4096, 4096], P(('dp', 'chan'), 'ctx')
- grad_filter: float32 [8, 512, 4096], P(('dp', 'chan'), 'ctx')
All inputs are finite; a program needn't handle non-finite values.
Results may differ from a plain program's by a relative error of at most 0.001.
Values may be sent and summed in bfloat16 or wider, within the bound.
No kernel may reach another device: no remote copies, remote signals or barrier semaphores. Data moves between devices by JAX's collectives and lax.ppermute only.
A program may use at most 128 MiB of HBM per device.

v0:
```python
import math

import jax
import jax.numpy as jnp
from jax import lax
from jax.sharding import PartitionSpec as P


def angle_table(count_rows, count_cols, modulus):
    row_index = lax.broadcasted_iota(jnp.int32, (count_rows, count_cols), 0)
    col_index = lax.broadcasted_iota(jnp.int32, (count_rows, count_cols), 1)
    phase_index = row_index * col_index % modulus
    radians = phase_index.astype(jnp.float32) * (2.0 * math.pi / modulus)
    return (jnp.cos(radians), jnp.sin(radians))


def product(pattern, left_operand, right_operand):
    return jnp.einsum(
        pattern,
        left_operand,
        right_operand,
        precision=lax.Precision.HIGHEST,
        preferred_element_type=jnp.float32,
    )


def forward(signal, tables):
    (cos_one, sin_one), (cos_turn, sin_turn), (cos_two, sin_two) = tables
    real_first = product("kn,cnm->ckm", cos_one, signal)
    imag_first = -product("kn,cnm->ckm", sin_one, signal)
    real_turned = real_first * cos_turn + imag_first * sin_turn
    imag_turned = imag_first * cos_turn - real_first * sin_turn
    real_out = product("ckm,mj->ckj", real_turned, cos_two) + product(
        "ckm,mj->ckj", imag_turned, sin_two
    )
    imag_out = product("ckm,mj->ckj", imag_turned, cos_two) - product(
        "ckm,mj->ckj", real_turned, sin_two
    )
    return (real_out, imag_out)


def inverse(real_spec, imag_spec, tables):
    (cos_one, sin_one), (cos_turn, sin_turn), (cos_two, sin_two) = tables
    real_first = product("ckj,mj->ckm", real_spec, cos_two) - product(
        "ckj,mj->ckm", imag_spec, sin_two
    )
    imag_first = product("ckj,mj->ckm", real_spec, sin_two) + product(
        "ckj,mj->ckm", imag_spec, cos_two
    )
    real_turned = real_first * cos_turn - imag_first * sin_turn
    imag_turned = real_first * sin_turn + imag_first * cos_turn
    signal = product("kn,ckm->cnm", cos_one, real_turned) - product(
        "kn,ckm->cnm", sin_one, imag_turned
    )
    return signal / (cos_one.shape[0] * cos_two.shape[0])


def shards(layer_input, grad_output, filter_taps):
    ctx_count = lax.axis_size("ctx")
    pencil = layer_input.shape[0] // ctx_count
    length = layer_input.shape[1] * ctx_count
    inner_size = min(128, length // 2)
    outer_size = 2 * length // inner_size
    half_outer = outer_size // 2
    tables = (
        angle_table(outer_size, half_outer, outer_size),
        angle_table(outer_size, inner_size, outer_size * inner_size),
        angle_table(inner_size, inner_size, inner_size),
    )
    block_shape = (pencil, half_outer, inner_size)
    filter_real, filter_imag = forward(filter_taps.reshape(block_shape), tables)
    moved_input, moved_grad = (
        lax.all_to_all(layer_input, "ctx", split_axis=0, concat_axis=1, tiled=True),
        lax.all_to_all(grad_output, "ctx", split_axis=0, concat_axis=1, tiled=True),
    )
    grad_real, grad_imag = forward(moved_grad.reshape(block_shape).astype(jnp.float32), tables)
    back_real = filter_real * grad_real + filter_imag * grad_imag
    back_imag = filter_real * grad_imag - filter_imag * grad_real
    local_back = inverse(back_real, back_imag, tables).reshape(pencil, length).astype(jnp.bfloat16)
    grad_input = lax.all_to_all(local_back, "ctx", split_axis=1, concat_axis=0, tiled=True)
    input_real, input_imag = forward(moved_input.reshape(block_shape).astype(jnp.float32), tables)
    tap_real = grad_real * input_real + grad_imag * input_imag
    tap_imag = grad_imag * input_real - grad_real * input_imag
    grad_scale = 1.0 / math.sqrt(length)
    local_taps = inverse(tap_real, tap_imag, tables) * grad_scale
    return (grad_input, local_taps.reshape(1, pencil, length))


def solution(mesh):
    in_specs = (P(("dp", "chan"), "ctx"), P(("dp", "chan"), "ctx"), P(("dp", "chan"), "ctx", None))
    out_specs = (P(("dp", "chan"), "ctx"), P(("dp", "chan"), "ctx", None))
    return jax.shard_map(shards, mesh=mesh, in_specs=in_specs, out_specs=out_specs, check_vma=False)
```

profile of v0, /device:TPU:0, one launch (start us, length us, event | category | flops | bytes accessed | tf_op | source)
XLA Modules:
  0.0 233.1 jit_solution(4659365415342247691)
XLA Ops:
  0.6 5.2 %all-to-all-start.2 = ((bf16[4,128,1024]{2,1,0:T(8,128)(2,1)}), bf16[4,128,1024]{2,1,0:T(8,128)(2,1)S(1)}, u32[]{:S(2)}, u32[]{:S(2)}) async-start(bf16[4,128,1024]{2,1,0:T(8,128)(2,1)} %bitcast.116), calls=%async_computation.2 | async-start | bytes 2097152 | tf_op jit(solution)/shard_map/all_to_all | solution.py:73
  5.8 2.0 copy.43
  7.8 5.2 %fusion.124 = f32[64,128,128]{2,0,1:T(8,128)} fusion(f32[128,32,128]{2,1,0:T(8,128)S(1)} %bitcast.110), kind=kOutput, calls=%fused_computation.115 | convolution fusion | flops 402681856 | bytes 6291456 | tf_op jit(solution)/shard_map/kn,cnm->ckm/dot_general | solution.py:18
  12.9 5.2 %fusion.132 = f32[64,128,128]{2,0,1:T(8,128)} fusion(f32[128,32,128]{2,1,0:T(8,128)S(1)} %bitcast.111), kind=kOutput, calls=%fused_computation.123 | convolution fusion | flops 402681856 | bytes 6291456 | tf_op jit(solution)/shard_map/kn,cnm->ckm/dot_general | solution.py:18
  18.1 1.3 all-to-all-done.2
  19.4 3.7 %all-to-all-start = ((bf16[4,128,1024]{2,1,0:T(8,128)(2,1)}), bf16[4,128,1024]{2,1,0:T(8,128)(2,1)S(1)}, u32[]{:S(2)}, u32[]{:S(2)}) async-start(bf16[4,128,1024]{2,1,0:T(8,128)(2,1)} %bitcast.6), calls=%async_computation | async-start | bytes 2097152 | tf_op jit(solution)/shard_map/all_to_all | solution.py:74
  23.1 0.1 fusion.134
  23.3 0.8 copy.36
  24.1 0.4 reshape.58
  24.6 3.9 %fusion.119 = f32[64,128,128]{2,0,1:T(8,128)} fusion(bf16[128,32,128]{2,1,0:T(8,128)(2,1)S(1)} %reshape.58), kind=kOutput, calls=%fused_computation.110 | convolution fusion | flops 402681856 | bytes 5242880 | tf_op jit(solution)/shard_map/kn,cnm->ckm/dot_general | solution.py:18
  28.5 3.9 %fusion.127 = f32[64,128,128]{2,0,1:T(8,128)} fusion(bf16[128,32,128]{2,1,0:T(8,128)(2,1)S(1)} %reshape.58), kind=kOutput, calls=%fused_computation.118 | convolution fusion | flops 402681856 | bytes 5242880 | tf_op jit(solution)/shard_map/kn,cnm->ckm/dot_general | solution.py:18
  32.3 3.9 %all-to-all-done = bf16[4,128,1024]{2,1,0:T(8,128)(2,1)S(1)} async-done(((bf16[4,128,1024]{2,1,0:T(8,128)(2,1)}), bf16[4,128,1024]{2,1,0:T(8,128)(2,1)S(1)}, u32[]{:S(2)}, u32[]{:S(2)}) %all-to-all-start) | async-done | bytes 1048608 | tf_op jit(solution)/shard_map/all_to_all | solution.py:74
  36.2 0.8 copy.26
  37.0 0.4 reshape.57
  37.5 3.9 %fusion.122 = f32[64,128,128]{2,0,1:T(8,128)} fusion(bf16[128,32,128]{2,1,0:T(8,128)(2,1)S(1)} %reshape.57), kind=kOutput, calls=%fused_computation.113 | convolution fusion | flops 402681856 | bytes 5242880 | tf_op jit(solution)/shard_map/kn,cnm->ckm/dot_general | solution.py:18
  41.4 12.2 %add_bitcast_fusion = (f32[128,64,128]{2,1,0:T(8,128)S(1)}, f32[128,64,128]{2,1,0:T(8,128)}, f32[128,64,128]{2,1,0:T(8,128)}, f32[128,64,128]{2,1,0:T(8,128)}, f...) fusion(f32[64,128,128]{2,0,1:T(8,128)} %fusion.127, f32[64,128,128]{2,0,1:T(8,128)} %fusion.119, ...), kind=kOutput, calls=%fused_computation.13 | convolution fusion | flops 424701952 | bytes 47251456 | tf_op jit(solution)/shard_map/kn,cnm->ckm/dot_general | solution.py:18
  53.6 0.0 copy-start.2
  53.6 9.2 %fusion.8 = f32[128,64,128]{2,0,1:T(8,128)S(1)} fusion(f32[128,64,128]{2,1,0:T(8,128)} %get-tuple-element.9), kind=kOutput, calls=%fused_computation.22 | convolution fusion | flops 1610842112 | bytes 8388608 | tf_op jit(solution)/shard_map/ckm,mj->ckj/dot_general | solution.py:18
  62.8 0.0 copy-done.2
  62.8 0.0 copy-start.1
  62.8 7.1 %fusion.10 = f32[128,64,128]{2,0,1:T(8,128)S(1)} fusion(f32[128,64,128]{2,1,0:T(8,128)S(1)} %copy-done.2), kind=kOutput, calls=%fused_computation.24 | convolution fusion | flops 1610842112 | bytes 8388608 | tf_op jit(solution)/shard_map/ckm,mj->ckj/dot_general | solution.py:18
  69.9 0.0 copy-done.1
  69.9 7.2 %fusion.16 = f32[128,64,128]{2,0,1:T(8,128)S(1)} fusion(f32[128,64,128]{2,1,0:T(8,128)S(1)} %copy-done.1), kind=kOutput, calls=%fused_computation.30 | convolution fusion | flops 1610842112 | bytes 8388608 | tf_op jit(solution)/shard_map/ckm,mj->ckj/dot_general | solution.py:18
  77.1 0.0 copy-start
  77.1 8.1 %fusion.18 = f32[128,64,128]{2,0,1:T(8,128)} fusion(f32[128,64,128]{2,1,0:T(8,128)S(1)} %copy-done.1), kind=kOutput, calls=%fused_computation.32 | convolution fusion | flops 1610842112 | bytes 8388608 | tf_op jit(solution)/shard_map/ckm,mj->ckj/dot_general | solution.py:18
  85.2 0.0 copy-done
  85.2 7.0 %fusion.24 = f32[128,64,128]{2,0,1:T(8,128)S(1)} fusion(f32[128,64,128]{2,1,0:T(8,128)S(1)} %copy-done), kind=kOutput, calls=%fused_computation.38 | convolution fusion | flops 1610842112 | bytes 8388608 | tf_op jit(solution)/shard_map/ckm,mj->ckj/dot_general | solution.py:18
  92.2 7.4 %fusion.26 = f32[128,64,128]{2,0,1:T(8,128)S(1)} fusion(f32[128,64,128]{2,1,0:T(8,128)S(1)} %copy-done), kind=kOutput, calls=%fused_computation.40 | convolution fusion | flops 1610842112 | bytes 8388608 | tf_op jit(solution)/shard_map/ckm,mj->ckj/dot_general | solution.py:18
  99.7 8.2 %fusion.44 = f32[128,64,128]{2,0,1:T(8,128)} fusion(f32[128,64,128]{2,0,1:T(8,128)S(1)} %fusion.10, f32[128,64,128]{2,1,0:T(8,128)S(1)} %get-tuple-element.8), kind=kOutput, calls=%fused_computation.50 | convolution fusion | flops 1611890688 | bytes 12582912 | tf_op jit(solution)/shard_map/ckm,mj->ckj/dot_general | solution.py:18
  107.9 8.2 %fusion.47 = f32[128,64,128]{2,0,1:T(8,128)} fusion(f32[128,64,128]{2,0,1:T(8,128)S(1)} %fusion.8, f32[128,64,128]{2,1,0:T(8,128)S(1)} %get-tuple-element.8), kind=kOutput, calls=%fused_computation.51 | convolution fusion | flops 1611890688 | bytes 12582912 | tf_op jit(solution)/shard_map/ckm,mj->ckj/dot_general | solution.py:18
  116.0 8.4 %fusion.32 = f32[128,64,128]{2,0,1:T(8,128)} fusion(f32[128,64,128]{2,0,1:T(8,128)S(1)} %fusion.26, f32[128,64,128]{2,1,0:T(8,128)S(1)} %get-tuple-element.23), kind=kOutput, calls=%fused_computation.46 | convolution fusion | flops 1611890688 | bytes 12582912 | tf_op jit(solution)/shard_map/ckm,mj->ckj/dot_general | solution.py:18
  124.4 0.0 copy-start.3
  124.4 8.2 %fusion.35 = f32[128,64,128]{2,0,1:T(8,128)} fusion(f32[128,64,128]{2,0,1:T(8,128)S(1)} %fusion.24, f32[128,64,128]{2,1,0:T(8,128)S(1)} %get-tuple-element.23), kind=kOutput, calls=%fused_computation.47 | convolution fusion | flops 1611890688 | bytes 12582912 | tf_op jit(solution)/shard_map/ckm,mj->ckj/dot_general | solution.py:18
  132.6 0.0 copy-done.3
  132.6 8.2 %fusion.41 = f32[128,64,128]{2,0,1:T(8,128)} fusion(f32[128,64,128]{2,0,1:T(8,128)S(1)} %fusion.16, f32[128,64,128]{2,1,0:T(8,128)S(1)} %copy-done.3), kind=kOutput, calls=%fused_computation.49 | convolution fusion | flops 1611890688 | bytes 12582912 | tf_op jit(solution)/shard_map/ckm,mj->ckj/dot_general | solution.py:18
  140.8 16.4 %multiply_subtract_fusion.1 = (f32[128,64,128]{2,0,1:T(8,128)}, f32[128,64,128]{2,0,1:T(8,128)}, f32[128,64,128]{2,0,1:T(8,128)}, f32[128,64,128]{2,0,1:T(8,128)}) fusion(f32[128,64,128]{2,0,1:T(8,128)} %fusion.47, f32[128,64,128]{2,0,1:T(8,128)} %fusion.41, f32[128,64,128]{2,0,1:T(8,128)} %fusion.44, f32[128,64,128]{2,0,1:T(8,128)} %fusion.35, ...), kind=kOutput, calls=%fused_computation.10 | convolution fusion | flops 1624473600 | bytes 46137344 | tf_op jit(solution)/shard_map/ckm,mj->ckj/dot_general | solution.py:18
  157.2 7.6 %fusion.60 = f32[128,64,128]{2,0,1:T(8,128)} fusion(f32[128,64,128]{2,0,1:T(8,128)} %get-tuple-element.3), kind=kOutput, calls=%fused_computation.65 | convolution fusion | flops 1610842112 | bytes 8388608 | tf_op jit(solution)/shard_map/ckj,mj->ckm/dot_general | solution.py:18
  164.8 0.0 copy-done.7
  164.8 0.0 copy-start.6
  164.8 3.8 %fusion.73 = f32[128,64,128]{2,0,1:T(8,128)S(1)} fusion(f32[128,64,128]{2,0,1:T(8,128)S(1)} %copy-done.7), kind=kOutput, calls=%fused_computation.78 | convolution fusion | flops 1610842112 | bytes 8388608 | tf_op jit(solution)/shard_map/ckj,mj->ckm/dot_general | solution.py:18
  168.6 0.0 copy-done.6
  168.6 3.8 %fusion.65 = f32[128,64,128]{2,0,1:T(8,128)S(1)} fusion(f32[128,64,128]{2,0,1:T(8,128)S(1)} %copy-done.6), kind=kOutput, calls=%fused_computation.70 | convolution fusion | flops 1610842112 | bytes 8388608 | tf_op jit(solution)/shard_map/ckj,mj->ckm/dot_general | solution.py:18
  172.4 0.0 copy-start.5
  172.5 3.8 %fusion.78 = f32[128,64,128]{2,0,1:T(8,128)S(1)} fusion(f32[128,64,128]{2,0,1:T(8,128)S(1)} %copy-done.6), kind=kOutput, calls=%fused_computation.83 | convolution fusion | flops 1610842112 | bytes 8388608 | tf_op jit(solution)/shard_map/ckj,mj->ckm/dot_general | solution.py:18
  176.3 0.0 copy-done.5
  176.3 4.0 %convolution_subtract_fusion.1 = f32[128,64,128]{2,0,1:T(8,128)S(1)} fusion(f32[128,64,128]{2,0,1:T(8,128)S(1)} %fusion.78, f32[128,64,128]{2,0,1:T(8,128)S(1)} %copy-done.5), kind=kOutput, calls=%fused_computation.55 | convolution fusion | flops 1611890688 | bytes 12582912 | tf_op jit(solution)/shard_map/ckj,mj->ckm/dot_general | solution.py:18
  180.2 0.0 copy-start.4
  180.3 3.8 %convolution_add_fusion.1 = f32[128,64,128]{2,0,1:T(8,128)S(1)} fusion(f32[128,64,128]{2,0,1:T(8,128)S(1)} %fusion.65, f32[128,64,128]{2,0,1:T(8,128)S(1)} %copy-done.5), kind=kOutput, calls=%fused_computation.54 | convolution fusion | flops 1611890688 | bytes 12582912 | tf_op jit(solution)/shard_map/ckj,mj->ckm/dot_general | solution.py:18
  184.0 0.0 copy-done.4
  184.1 5.5 %convolution_subtract_fusion = f32[128,64,128]{2,0,1:T(8,128)} fusion(f32[128,64,128]{2,0,1:T(8,128)S(1)} %fusion.73, f32[128,64,128]{2,0,1:T(8,128)S(1)} %copy-done.4), kind=kOutput, calls=%fused_computation.53 | convolution fusion | flops 1611890688 | bytes 12582912 | tf_op jit(solution)/shard_map/ckj,mj->ckm/dot_general | solution.py:18
  189.6 11.2 %multiply_subtract_fusion = (f32[128,64,128]{2,0,1:T(8,128)}, f32[128,64,128]{2,0,1:T(8,128)}, f32[128,64,128]{2,0,1:T(8,128)}, f32[128,64,128]{2,0,1:T(8,128)}) fusion(f32[128,64,128]{2,0,1:T(8,128)} %convolution_subtract_fusion, f32[64,128]{1,0:T(8,128)S(1)} %get-tuple-element.24, f32[64,128]{1,0:T(8,128)S(1)} %get-tuple-element.25, ...), kind=kOutput, calls=%fused_computation.9 | convolution fusion | flops 1624473600 | bytes 37814272 | tf_op jit(solution)/shard_map/ckj,mj->ckm/dot_general | solution.py:18
  200.8 7.1 %fusion.4 = f32[128,128,32]{1,2,0:T(8,128)S(1)} fusion(f32[128,64,128]{2,0,1:T(8,128)} %get-tuple-element.18), kind=kOutput, calls=%fused_computation.4 | convolution fusion | flops 402681856 | bytes 6291456 | tf_op jit(solution)/shard_map/kn,ckm->cnm/dot_general | solution.py:18
  207.8 0.0 copy-done.8
  207.8 5.0 %fusion.54 = bf16[128,32,128]{2,1,0:T(8,128)(2,1)S(1)} fusion(f32[128,128,32]{1,2,0:T(8,128)S(1)} %fusion.4, f32[128,64,128]{2,0,1:T(8,128)S(1)} %copy-done.8), kind=kOutput, calls=%fused_computation.58 | convolution fusion | flops 404254720 | bytes 7340032 | tf_op jit(solution)/shard_map/kn,ckm->cnm/dot_general | solution.py:18
  212.8 0.3 convert_element_type.127
  213.1 1.3 copy.35
  214.4 3.8 %all-to-all-start.1 = ((bf16[128,4,1024]{2,0,1:T(8,128)(2,1)}), bf16[128,4,1024]{2,0,1:T(8,128)(2,1)S(1)}, u32[]{:S(2)}, u32[]{:S(2)}) async-start(bf16[128,4,1024]{2,0,1:T(8,128)(2,1)} %copy.35), calls=%async_computation.1 | async-start | bytes 2097152 | tf_op jit(solution)/shard_map/all_to_all | solution.py:80
  218.2 0.0 copy-start.9
  218.2 7.1 %fusion = f32[128,128,32]{1,2,0:T(8,128)S(1)} fusion(f32[128,64,128]{2,0,1:T(8,128)} %get-tuple-element.7), kind=kOutput, calls=%fused_computation | convolution fusion | flops 402681856 | bytes 6291456 | tf_op jit(solution)/shard_map/kn,ckm->cnm/dot_general | solution.py:18
  225.3 0.0 copy-done.9
  225.3 5.0 %multiply_bitcast_fusion = f32[128,32,128]{2,1,0:T(8,128)S(1)} fusion(f32[128,128,32]{1,2,0:T(8,128)S(1)} %fusion, f32[128,64,128]{2,0,1:T(8,128)S(1)} %copy-done.9), kind=kOutput, calls=%fused_computation.56 | convolution fusion | flops 403730432 | bytes 8388608 | tf_op jit(solution)/shard_map/kn,ckm->cnm/dot_general | solution.py:18
  230.3 1.5 reshape.59
  231.8 0.0 all-to-all-done.1
  231.8 1.0 copy.97
  (2 shorter events, 0.0 us)
Async XLA Ops:
  0.6 18.8 %all-to-all-start.2 = ((bf16[4,128,1024]{2,1,0:T(8,128)(2,1)}), bf16[4,128,1024]{2,1,0:T(8,128)(2,1)S(1)}, u32[]{:S(2)}, u32[]{:S(2)}) async-start(bf16[4,128,1024]{2,1,0:T(8,128)(2,1)} %bitcast.116), calls=%async_computation.2 | async-start | bytes 2097152 | tf_op jit(solution)/shard_map/all_to_all | solution.py:73
  19.4 16.8 %all-to-all-start = ((bf16[4,128,1024]{2,1,0:T(8,128)(2,1)}), bf16[4,128,1024]{2,1,0:T(8,128)(2,1)S(1)}, u32[]{:S(2)}, u32[]{:S(2)}) async-start(bf16[4,128,1024]{2,1,0:T(8,128)(2,1)} %bitcast.6), calls=%async_computation | async-start | bytes 2097152 | tf_op jit(solution)/shard_map/all_to_all | solution.py:74
  53.6 9.2 %copy-start.2 = (f32[128,64,128]{2,1,0:T(8,128)S(1)}, f32[128,64,128]{2,1,0:T(8,128)}, u32[]{:S(2)}) copy-start(f32[128,64,128]{2,1,0:T(8,128)} %get-tuple-element.9) | copy-start | bytes 12582916
  62.8 7.1 %copy-start.1 = (f32[128,64,128]{2,1,0:T(8,128)S(1)}, f32[128,64,128]{2,1,0:T(8,128)}, u32[]{:S(2)}) copy-start(f32[128,64,128]{2,1,0:T(8,128)} %get-tuple-element.20) | copy-start | bytes 12582916
  77.1 8.2 %copy-start = (f32[128,64,128]{2,1,0:T(8,128)S(1)}, f32[128,64,128]{2,1,0:T(8,128)}, u32[]{:S(2)}) copy-start(f32[128,64,128]{2,1,0:T(8,128)} %get-tuple-element.22) | copy-start | bytes 12582916
  124.4 8.2 %copy-start.3 = (f32[128,64,128]{2,1,0:T(8,128)S(1)}, f32[128,64,128]{2,1,0:T(8,128)}, u32[]{:S(2)}) copy-start(f32[128,64,128]{2,1,0:T(8,128)} %get-tuple-element.21) | copy-start | bytes 12582916
  157.2 7.6 %copy-start.7 = (f32[128,64,128]{2,0,1:T(8,128)S(1)}, f32[128,64,128]{2,0,1:T(8,128)}, u32[]{:S(2)}) copy-start(f32[128,64,128]{2,0,1:T(8,128)} %get-tuple-element.3) | copy-start | bytes 12582916
  164.8 3.8 %copy-start.6 = (f32[128,64,128]{2,0,1:T(8,128)S(1)}, f32[128,64,128]{2,0,1:T(8,128)}, u32[]{:S(2)}) copy-start(f32[128,64,128]{2,0,1:T(8,128)} %get-tuple-element.16) | copy-start | bytes 12582916
  172.4 3.8 %copy-start.5 = (f32[128,64,128]{2,0,1:T(8,128)S(1)}, f32[128,64,128]{2,0,1:T(8,128)}, u32[]{:S(2)}) copy-start(f32[128,64,128]{2,0,1:T(8,128)} %get-tuple-element.17) | copy-start | bytes 12582916
  180.2 3.8 %copy-start.4 = (f32[128,64,128]{2,0,1:T(8,128)S(1)}, f32[128,64,128]{2,0,1:T(8,128)}, u32[]{:S(2)}) copy-start(f32[128,64,128]{2,0,1:T(8,128)} %get-tuple-element.2) | copy-start | bytes 12582916
  200.8 7.1 %copy-start.8 = (f32[128,64,128]{2,0,1:T(8,128)S(1)}, f32[128,64,128]{2,0,1:T(8,128)}, u32[]{:S(2)}) copy-start(f32[128,64,128]{2,0,1:T(8,128)} %get-tuple-element.19) | copy-start | bytes 12582916
  214.4 17.4 %all-to-all-start.1 = ((bf16[128,4,1024]{2,0,1:T(8,128)(2,1)}), bf16[128,4,1024]{2,0,1:T(8,128)(2,1)S(1)}, u32[]{:S(2)}, u32[]{:S(2)}) async-start(bf16[128,4,1024]{2,0,1:T(8,128)(2,1)} %copy.35), calls=%async_computation.1 | async-start | bytes 2097152 | tf_op jit(solution)/shard_map/all_to_all | solution.py:80
  218.2 7.1 %copy-start.9 = (f32[128,64,128]{2,0,1:T(8,128)S(1)}, f32[128,64,128]{2,0,1:T(8,128)}, u32[]{:S(2)}) copy-start(f32[128,64,128]{2,0,1:T(8,128)} %get-tuple-element.6) | copy-start | bytes 12582916
where the time goes:
time: 237 us; the launch traced here: 233 us
  matrix products  205 us (86%)
  starting transfers between devices  12.6 us (5%)
  local copies, waits for them, and re-layouts  8.57 us (4%)
  waiting for transfers between devices  5.21 us (2%)
    dot_general x30, matrix products, product(): jnp.einsum(pattern, left_operand, right_operand, precision=lax.Precision....  205 us
    all_to_all x1, starting transfers between devices, shards(): lax.all_to_all(layer_input, 'ctx', split_axis=0, concat_axis=1, tiled=True)  5.18 us
  transfers between devices with their start and end apart: 3, of which 2 were waited for; matrix products, arithmetic and copies ran while one was open for 15% of the time, Pallas kernels for 0%

commit v1 on v0

v1 whole, which is shorter than its diff:
```python
import functools
import math

import jax
import jax.numpy as jnp
import ml_dtypes
import numpy as np
from jax import lax
from jax.experimental import pallas as pl
from jax.experimental.pallas import tpu as pltpu
from jax.sharding import PartitionSpec as P

LANES = 128
TILE = 16
HALF_TILE = 8


def split_table(table):
    high = table.astype(ml_dtypes.bfloat16)
    low = (table - high.astype(np.float64)).astype(ml_dtypes.bfloat16)
    return high, low


def dft_tables(length):
    index = np.arange(LANES)
    angle = 2.0 * np.pi * (np.outer(index, index) % LANES) / LANES
    cos, sin = np.cos(angle), np.sin(angle)
    ahead = np.block([[cos, -sin], [sin, cos]])
    back = np.block([[cos, sin], [-sin, cos]]) / length
    outer = length // LANES
    order = np.concatenate([np.arange(0, outer, 2), np.arange(1, outer, 2)])
    turn = 2.0 * np.pi * np.outer(order + 0.25, index) / length
    twiddle = np.stack([np.cos(turn), np.sin(turn)], axis=1).astype(np.float32)
    return split_table(ahead), split_table(back), split_table(back / math.sqrt(length)), twiddle


def add(a, b):
    return (a[0] + b[0], a[1] + b[1])


def sub(a, b):
    return (a[0] - b[0], a[1] - b[1])


def turn_quarter(a, sign):
    return (-a[1], a[0]) if sign > 0 else (a[1], -a[0])


def turn_by(a, numerator, denominator, sign):
    numerator = numerator % denominator
    if numerator == 0:
        return a
    if 4 * numerator == denominator:
        return turn_quarter(a, sign)
    if 2 * numerator == denominator:
        return (-a[0], -a[1])
    if 4 * numerator == 3 * denominator:
        return turn_quarter(a, -sign)
    angle = sign * 2.0 * math.pi * numerator / denominator
    cos, sin = math.cos(angle), math.sin(angle)
    if 8 * numerator % denominator == 0:
        root = math.sqrt(0.5)
        re, im = a
        if cos * sin > 0:
            re, im = re - im, re + im
        else:
            re, im = re + im, im - re
        return (re * (root if cos > 0 else -root), im * (root if cos > 0 else -root))
    return (a[0] * cos - a[1] * sin, a[0] * sin + a[1] * cos)


def fft(points, sign):
    count = len(points)
    if count == 1:
        return points
    if count == 2:
        return [add(points[0], points[1]), sub(points[0], points[1])]
    if count % 4:
        evens, odds = fft(points[0::2], sign), fft(points[1::2], sign)
        turned = [turn_by(odds[k], k, count, sign) for k in range(count // 2)]
        return [add(a, b) for a, b in zip(evens, turned)] + [sub(a, b) for a, b in zip(evens, turned)]
    quarter = count // 4
    parts = [fft(points[r::4], sign) for r in range(4)]
    out = [None] * count
    for k in range(quarter):
        p0, p1, p2, p3 = (turn_by(parts[r][k], r * k, count, sign) for r in range(4))
        s02, d02, s13, d13 = add(p0, p2), sub(p0, p2), add(p1, p3), sub(p1, p3)
        out[k] = add(s02, s13)
        out[k + 2 * quarter] = sub(s02, s13)
        if sign > 0:
            out[k + quarter] = (d02[0] - d13[1], d02[1] + d13[0])
            out[k + 3 * quarter] = (d02[0] + d13[1], d02[1] - d13[0])
        else:
            out[k + quarter] = (d02[0] + d13[1], d02[1] - d13[0])
            out[k + 3 * quarter] = (d02[0] - d13[1], d02[1] + d13[0])
    return out


def outer_forward(load, store, twiddle_ref, outer, half):
    count = outer // 2
    for row in range(0, TILE, HALF_TILE):
        points = []
        for n in range(count):
            near = -2.0 * math.pi * n * (half + 0.25) / outer
            far = -2.0 * math.pi * (n + count) * (half + 0.25) / outer
            a, b = load(n, row), load(n + count, row)
            if n == 0:
                points.append((a + b * math.cos(far), b * math.sin(far)))
            else:
                points.append((a * math.cos(near) + b * math.cos(far), a * math.sin(near) + b * math.sin(far)))
        for k, (re, im) in enumerate(fft(points, -1)):
            at = half * count + k
            cos, sin = twiddle_ref[at, 0:1, :], twiddle_ref[at, 1:2, :]
            store(at, row, re * cos + im * sin, im * cos - re * sin)


def outer_inverse(spec_ref, twiddle_ref, out_ref, outer, half):
    count = outer // 2
    for row in range(0, TILE, HALF_TILE):
        points = []
        for k in range(count):
            at = half * count + k
            rows = pl.ds(at * TILE + row, HALF_TILE)
            re, im = spec_ref[rows, 0:LANES], spec_ref[rows, LANES : 2 * LANES]
            cos, sin = twiddle_ref[at, 0:1, :], twiddle_ref[at, 1:2, :]
            points.append((re * cos - im * sin, re * sin + im * cos))
        for n, (re, im) in enumerate(fft(points, 1)):
            for place in (n, n + count):
                angle = 2.0 * math.pi * place * (half + 0.25) / outer
                value = re if place == 0 else re * math.cos(angle) - im * math.sin(angle)
                if half == 0:
                    out_ref[place, row : row + HALF_TILE, :] = value
                else:
                    out_ref[place, row : row + HALF_TILE, :] += value


def matmul(values, high_ref, low_ref):
    high = values.astype(jnp.bfloat16)
    low = (values - high.astype(jnp.float32)).astype(jnp.bfloat16)
    dot = functools.partial(jnp.dot, preferred_element_type=jnp.float32)
    return dot(high, high_ref[...]) + dot(low, high_ref[...]) + dot(high, low_ref[...])


def spectrum_kernel(taps_ref, ahead_high, ahead_low, twiddle_ref, spec_ref, work_ref, *, outer):
    count = outer // 2

    def load(n, row):
        return taps_ref[row : row + HALF_TILE, n * LANES : (n + 1) * LANES]

    def store(at, row, re, im):
        rows = pl.ds(at * TILE + row, HALF_TILE)
        work_ref[rows, 0:LANES] = re
        work_ref[rows, LANES : 2 * LANES] = im

    for half in range(2):
        outer_forward(load, store, twiddle_ref, outer, half)
    for half in range(2):
        rows = pl.ds(half * count * TILE, count * TILE)
        spec_ref[0, rows, :] = matmul(work_ref[rows, :], ahead_high, ahead_low)


def correlate(piece_refs, me, mate_ref, keep_ref, signal_is_grad, tables, fill_ref, work_ref, out_ref, outer):
    ahead_high, ahead_low, back_high, back_low, twiddle_ref = tables
    count = outer // 2
    per_piece = outer // len(piece_refs)
    for k, ref in enumerate(piece_refs):
        first = (me ^ k) * per_piece
        for i in range(per_piece):
            fill_ref[first + i] = ref[:, i * LANES : (i + 1) * LANES].astype(jnp.float32)

    def load(n, row):
        return fill_ref[n, row : row + HALF_TILE, :]

    def store(at, row, re, im):
        rows = pl.ds(at * TILE + row, HALF_TILE)
        work_ref[rows, 0:LANES] = re
        work_ref[rows, LANES : 2 * LANES] = im

    for half in range(2):
        outer_forward(load, store, twiddle_ref, outer, half)
    for half in range(2):
        rows = pl.ds(half * count * TILE, count * TILE)
        own = matmul(work_ref[rows, :], ahead_high, ahead_low)
        if keep_ref is not None:
            keep_ref[0, rows, :] = own
        mate = mate_ref[0, rows, :]
        grad, other = (own, mate) if signal_is_grad else (mate, own)
        grad_re, grad_im = grad[:, :LANES], grad[:, LANES:]
        other_re, other_im = other[:, :LANES], other[:, LANES:]
        both = jnp.concatenate(
            [other_re * grad_re + other_im * grad_im, other_re * grad_im - other_im * grad_re], axis=1
        )
        work_ref[rows, :] = matmul(both, back_high, back_low)
    for half in range(2):
        outer_inverse(work_ref, twiddle_ref, out_ref, outer, half)


def input_kernel(me_ref, *refs, outer, parts):
    pieces, (mate_ref, *tables) = refs[:parts], refs[parts : parts + 6]
    keep_ref, *sends = refs[parts + 6 : 2 * parts + 7]
    fill_ref, work_ref, out_ref = refs[2 * parts + 7 :]
    me = me_ref[0]
    correlate(pieces, me, mate_ref, keep_ref, True, tables, fill_ref, work_ref, out_ref, outer)
    per_piece = outer // parts
    for k, ref in enumerate(sends):
        first = (me ^ k) * per_piece
        for i in range(per_piece):
            ref[:, i * LANES : (i + 1) * LANES] = out_ref[first + i].astype(jnp.bfloat16)


def filter_kernel(me_ref, *refs, outer, parts):
    pieces, (mate_ref, *tables) = refs[:parts], refs[parts : parts + 6]
    result_ref, fill_ref, work_ref, out_ref = refs[parts + 6 :]
    correlate(pieces, me_ref[0], mate_ref, None, False, tables, fill_ref, work_ref, out_ref, outer)
    for n in range(outer):
        result_ref[:, n * LANES : (n + 1) * LANES] = out_ref[n]


def gather_kernel(me_ref, *refs, pencil):
    *pieces, out_ref, sems = refs
    copies = []
    for k, ref in enumerate(pieces):
        rows = pl.ds((me_ref[0] ^ k) * pencil, pencil)
        copies.append(pltpu.make_async_copy(ref, out_ref.at[rows, :], sems.at[k]))
    for copy in copies:
        copy.start()
    for copy in copies:
        copy.wait()


def shards(layer_input, grad_output, filter_taps):
    parts = lax.axis_size("ctx")
    me = lax.axis_index("ctx")
    pencil, piece = layer_input.shape[0] // parts, layer_input.shape[1]
    length = piece * parts
    outer = length // LANES
    aligned = pencil % TILE == 0
    rows = -(-pencil // TILE) * TILE
    steps = rows // TILE
    ahead, back, back_scaled, twiddle = dft_tables(length)
    me_array = me.astype(jnp.int32).reshape(1)

    def swap(block, k):
        return lax.ppermute(block, "ctx", [(i, i ^ k) for i in range(parts)])

    def pick(array, k):
        blocks = array.reshape(parts, pencil, piece)
        return lax.dynamic_index_in_dim(blocks, me ^ k, 0, keepdims=False)

    def pad(block):
        return block if aligned else jnp.pad(block, ((0, rows - pencil), (0, 0)))

    whole = lambda array: pl.BlockSpec(array.shape, lambda s, *_: (0,) * array.ndim)
    piece_spec = pl.BlockSpec((TILE, piece), lambda s, *_: (s, 0))
    own_spec = pl.BlockSpec((TILE, piece), lambda s, at: (at[0] * steps + s, 0)) if aligned else piece_spec
    full_spec = pl.BlockSpec((TILE, length), lambda s, *_: (s, 0))
    spec_spec = pl.BlockSpec((1, outer * TILE, 2 * LANES), lambda s, *_: (s, 0, 0))
    spec_shape = jax.ShapeDtypeStruct((steps, outer * TILE, 2 * LANES), jnp.float32)
    work = pltpu.VMEM((outer * TILE, 2 * LANES), jnp.float32)
    lane_tiles = pltpu.VMEM((outer, TILE, LANES), jnp.float32)
    params = pltpu.CompilerParams(vmem_limit_bytes=32 * 1024 * 1024)
    stage_flops = 2 * 3 * rows * outer * (2 * LANES) ** 2
    spec_bytes = 4 * rows * length * 2

    def cost(stages, moved):
        return pl.CostEstimate(flops=stages * stage_flops, bytes_accessed=moved, transcendentals=0)

    def own_of(array):
        return array if aligned else pad(pick(array, 0))

    grad_pieces = [swap(pick(grad_output, k), k) for k in range(1, parts)]
    input_pieces = [swap(pick(layer_input, k), k) for k in range(1, parts)]

    taps = pad(filter_taps.reshape(pencil, length))
    taps_spectrum = pl.pallas_call(
        functools.partial(spectrum_kernel, outer=outer),
        grid=(steps,),
        in_specs=[full_spec, whole(ahead[0]), whole(ahead[1]), whole(twiddle)],
        out_specs=spec_spec,
        out_shape=spec_shape,
        scratch_shapes=[work],
        compiler_params=params,
        cost_estimate=cost(1, 2 * spec_bytes),
        name="taps_spectrum",
    )(taps, *ahead, twiddle)

    tables = [*ahead, *back, twiddle]
    grad_spectrum, *outgoing = pl.pallas_call(
        functools.partial(input_kernel, outer=outer, parts=parts),
        grid_spec=pltpu.PrefetchScalarGridSpec(
            num_scalar_prefetch=1,
            grid=(steps,),
            in_specs=[own_spec, *[piece_spec] * (parts - 1), spec_spec, *map(whole, tables)],
            out_specs=[spec_spec, *[piece_spec] * parts],
            scratch_shapes=[lane_tiles, work, lane_tiles],
        ),
        out_shape=[spec_shape, *[jax.ShapeDtypeStruct((rows, piece), jnp.bfloat16)] * parts],
        compiler_params=params,
        cost_estimate=cost(2, 2 * spec_bytes),
        name="grad_input",
    )(me_array, own_of(grad_output), *map(pad, grad_pieces), taps_spectrum, *tables)

    incoming = [outgoing[0][:pencil]] + [swap(outgoing[k][:pencil], k) for k in range(1, parts)]

    tables = [*ahead, *back_scaled, twiddle]
    grad_filter = pl.pallas_call(
        functools.partial(filter_kernel, outer=outer, parts=parts),
        grid_spec=pltpu.PrefetchScalarGridSpec(
            num_scalar_prefetch=1,
            grid=(steps,),
            in_specs=[own_spec, *[piece_spec] * (parts - 1), spec_spec, *map(whole, tables)],
            out_specs=full_spec,
            scratch_shapes=[lane_tiles, work, lane_tiles],
        ),
        out_shape=jax.ShapeDtypeStruct((rows, length), jnp.float32),
        compiler_params=params,
        cost_estimate=cost(2, 2 * spec_bytes),
        name="grad_filter",
    )(me_array, own_of(layer_input), *map(pad, input_pieces), grad_spectrum, *tables)

    if aligned:
        grad_input = pl.pallas_call(
            functools.partial(gather_kernel, pencil=pencil),
            in_specs=[pl.BlockSpec(memory_space=pltpu.SMEM), *[pl.BlockSpec(memory_space=pl.ANY)] * parts],
            out_specs=pl.BlockSpec(memory_space=pl.ANY),
            out_shape=jax.ShapeDtypeStruct((parts * pencil, piece), jnp.bfloat16),
            scratch_shapes=[pltpu.SemaphoreType.DMA((parts,))],
            name="gather_pieces",
        )(me_array, *incoming)
    else:
        slots = jnp.zeros((parts, pencil, piece), jnp.bfloat16)
        for k, block in enumerate(incoming):
            slots = lax.dynamic_update_index_in_dim(slots, block, me ^ k, 0)
        grad_input = slots.reshape(parts * pencil, piece)
    return (grad_input, grad_filter[:pencil].reshape(1, pencil, length))


def solution(mesh):
    in_specs = (P(("dp", "chan"), "ctx"), P(("dp", "chan"), "ctx"), P(("dp", "chan"), "ctx", None))
    out_specs = (P(("dp", "chan"), "ctx"), P(("dp", "chan"), "ctx", None))
    return jax.shard_map(shards, mesh=mesh, in_specs=in_specs, out_specs=out_specs, check_vma=False)
```

time: 237 us -> 75.6 us (0.32); the launches traced: 233 us -> 75.3 us
  matrix products: 205 us -> 0 us
  Pallas kernels: 0 us -> 54 us
  waiting for transfers between devices: 5.21 us -> 1.4 us
    dot_general x30 -> x0, matrix products: 205 us -> none  [product(): jnp.einsum(pattern, left_operand, right_operand, precision=lax.Precision....]
    pallas_call x0 -> x4, Pallas kernels: none -> 54 us  [the longest x1 32.9 us: shards(): pl.pallas_call(functools.partial(gather_kernel, pencil=pencil), in_specs=...]
    all_to_all x3 -> x0, starting transfers between devices: 12.6 us -> none  [the longest x1 5.18 us: shards(): lax.all_to_all(layer_input, 'ctx', split_axis=0, concat_axis=1, tiled=True)]
    ppermute x0 -> x9, starting transfers between devices: none -> 11.7 us  [swap(): return lax.ppermute(block, 'ctx', [(i, i ^ k) for i in range(parts)])]
    all_to_all x3 -> x0, waiting for transfers between devices: 5.21 us -> none  [the longest x1 3.87 us: shards(): lax.all_to_all(grad_output, 'ctx', split_axis=0, concat_axis=1, tiled=True)]
    reshape x3 -> x0, local copies, waits for them, and re-layouts: 2.41 us -> none  [the longest x1 1.53 us: shards(): return (grad_input, local_taps.reshape(1, pencil, length))]
    unnamed x22 -> x34, local copies, waits for them, and re-layouts: 2.97 us -> 5.03 us
  transfers between devices with their start and end apart: 3 -> 9, of which waited for: 2 -> 2; matrix products, arithmetic and copies ran while one was open for 15% -> 2% of each run, Pallas kernels for 0% -> 28%
where the time goes in v1:
time: 75.6 us; the launch traced here: 75.3 us
  Pallas kernels  54 us (71%)
  starting transfers between devices  11.7 us (15%)
  local copies, waits for them, and re-layouts  7.36 us (10%)
  waiting for transfers between devices  1.4 us (2%)
  between operations  0.84 us (1%)
    pallas_call x1, Pallas kernels, shards(): pl.pallas_call(functools.partial(gather_kernel, pencil=pencil), in_specs=...  32.9 us
    ppermute x9, starting transfers between devices, swap(): return lax.ppermute(block, 'ctx', [(i, i ^ k) for i in range(parts)])  11.7 us
    pallas_call x1, Pallas kernels, shards(): pl.pallas_call(functools.partial(filter_kernel, outer=outer, parts=parts)...  8.72 us
    pallas_call x1, Pallas kernels, shards(): pl.pallas_call(functools.partial(input_kernel, outer=outer, parts=parts),...  8.1 us
    unnamed x34, local copies, waits for them, and re-layouts  5.03 us
    pallas_call x1, Pallas kernels, shards(): pl.pallas_call(functools.partial(spectrum_kernel, outer=outer), grid=(ste...  4.29 us
    squeeze x2, local copies, waits for them, and re-layouts, pick(): return lax.dynamic_index_in_dim(blocks, me ^ k, 0, keepdims=False)  2.33 us
  transfers between devices with their start and end apart: 9, of which 2 were waited for; matrix products, arithmetic and copies ran while one was open for 2% of the time, Pallas kernels for 28%

profile of v1, /device:TPU:0, one launch (start us, length us, event | category | flops | bytes accessed | tf_op | source)
XLA Modules:
  0.0 75.3 jit_solution(18115768018534077392)
XLA Ops:
  0.6 1.2 %dynamic-slice_bitcast_fusion.3 = (bf16[128,1024]{1,0:T(8,128)(2,1)S(1)}, bf16[128,1024]{1,0:T(8,128)(2,1)S(1)}, bf16[128,1024]{1,0:T(8,128)(2,1)S(1)}) fusion(bf16[4,128,1024]{2,1,0:T(8,128)(2,1)} %bitcast.18, s32[]{:T(128)S(6)} %select_n.15, s32[]{:T(128)S(6)} %select_n.14, s32[]{:T(128)S(6)} %select_n.13), kind=kLoop, calls=%fused_computation.3 | loop fusion | bytes 1572876 | tf_op jit(solution)/shard_map/jit(dynamic_index_in_dim)/squeeze | solution.py:248
  1.8 0.0 copy-start.1
  1.8 0.0 copy-start.12
  1.8 0.0 copy-start.13
  1.9 3.0 %collective-permute-start = (bf16[128,1024]{1,0:T(8,128)(2,1)S(1)}, bf16[128,1024]{1,0:T(8,128)(2,1)S(1)}, u32[]{:S(2)}, u32[]{:S(2)}) collective-permute-start(bf16[128,1024]{1,0:T(8,128)(2,1)S(1)} %get-tuple-element.17), channel_id=1, source_target_pairs={{0,2},{2,0},{4,6},{6,4},{1,3},{3,1},{5,7},{7,5},{8,10},{10,8},{12,... | collective-permute-start | bytes 786440 | tf_op jit(solution)/shard_map/ppermute | solution.py:244
  4.9 1.5 %collective-permute-start.1 = (bf16[128,1024]{1,0:T(8,128)(2,1)S(1)}, bf16[128,1024]{1,0:T(8,128)(2,1)S(1)}, u32[]{:S(2)}, u32[]{:S(2)}) collective-permute-start(bf16[128,1024]{1,0:T(8,128)(2,1)S(1)} %get-tuple-element.16), channel_id=1, source_target_pairs={{0,4},{2,6},{4,0},{6,2},{1,5},{3,7},{5,1},{7,3},{8,12},{10,14},{12... | collective-permute-start | bytes 786440 | tf_op jit(solution)/shard_map/ppermute | solution.py:244
  6.4 0.0 collective-permute-start.2
  6.4 1.2 %dynamic-slice_bitcast_fusion = (bf16[128,1024]{1,0:T(8,128)(2,1)S(1)}, bf16[128,1024]{1,0:T(8,128)(2,1)S(1)}, bf16[128,1024]{1,0:T(8,128)(2,1)S(1)}) fusion(bf16[4,128,1024]{2,1,0:T(8,128)(2,1)} %bitcast.19, s32[]{:T(128)S(6)} %select_n.15, s32[]{:T(128)S(6)} %select_n.14, s32[]{:T(128)S(6)} %select_n.13), kind=kLoop, calls=%fused_computation | loop fusion | bytes 1572876 | tf_op jit(solution)/shard_map/jit(dynamic_index_in_dim)/squeeze | solution.py:248
  7.6 2.0 %collective-permute-start.6 = (bf16[128,1024]{1,0:T(8,128)(2,1)S(1)}, bf16[128,1024]{1,0:T(8,128)(2,1)S(1)}, u32[]{:S(2)}, u32[]{:S(2)}) collective-permute-start(bf16[128,1024]{1,0:T(8,128)(2,1)S(1)} %get-tuple-element.14), channel_id=1, source_target_pairs={{0,2},{2,0},{4,6},{6,4},{1,3},{3,1},{5,7},{7,5},{8,10},{10,8},{12,... | collective-permute-start | bytes 786440 | tf_op jit(solution)/shard_map/ppermute | solution.py:244
  9.6 1.5 %collective-permute-start.7 = (bf16[128,1024]{1,0:T(8,128)(2,1)S(1)}, bf16[128,1024]{1,0:T(8,128)(2,1)S(1)}, u32[]{:S(2)}, u32[]{:S(2)}) collective-permute-start(bf16[128,1024]{1,0:T(8,128)(2,1)S(1)} %get-tuple-element.13), channel_id=1, source_target_pairs={{0,4},{2,6},{4,0},{6,2},{1,5},{3,7},{5,1},{7,3},{8,12},{10,14},{12... | collective-permute-start | bytes 786440 | tf_op jit(solution)/shard_map/ppermute | solution.py:244
  11.1 0.0 copy-start
  11.1 1.6 %copy-done = f32[1,128,4096]{2,1,0:T(8,128)S(1)} copy-done((f32[1,128,4096]{2,1,0:T(8,128)S(1)}, f32[1,128,4096]{2,1,0:T(8,128)}, u32[]{:S(2)}) %copy-start) | copy-done | bytes 2097176
  12.7 0.0 copy-start.4
  12.7 0.9 %copy-done.4 = bf16[256,256]{1,0:T(8,128)(2,1)S(1)} copy-done((bf16[256,256]{1,0:T(8,128)(2,1)S(1)}, bf16[256,256]{1,0:T(8,128)(2,1)}, u32[]{:S(2)}) %copy-start.4) | copy-done | bytes 131096
  13.6 0.0 copy-start.6
  13.6 0.9 %copy-done.6 = bf16[256,256]{1,0:T(8,128)(2,1)S(1)} copy-done((bf16[256,256]{1,0:T(8,128)(2,1)S(1)}, bf16[256,256]{1,0:T(8,128)(2,1)}, u32[]{:S(2)}) %copy-start.6) | copy-done | bytes 131096
  14.5 0.0 copy-start.8
  14.5 0.8 %copy-done.8 = f32[32,2,128]{2,1,0:T(2,128)S(1)} copy-done((f32[32,2,128]{2,1,0:T(2,128)S(1)}, f32[32,2,128]{2,1,0:T(2,128)}, u32[]{:S(2)}) %copy-start.8) | copy-done | bytes 32792
  15.3 4.3 %taps_spectrum.1.refs_4_ = f32[8,512,256]{2,1,0:T(8,128)S(1)} custom-call(f32[128,4096]{1,0:T(8,128)S(1)} %bitcast.17, bf16[256,256]{1,0:T(8,128)(2,1)S(1)} %copy-done.4, bf16[256,256]{1,0:T(8,128)(2,1)S(1)} %copy-done.6, f32[32,2,128]{2,1,0:T(2,128)S(1)} %copy-done.8), custom_call_target="tpu_custom_call" | custom-call | flops 1610612736 | bytes 8388608 | tf_op jit(solution)/shard_map/taps_spectrum/pallas_call | solution.py:275
  19.6 0.0 collective-permute-done.refs_1_
  19.6 0.1 collective-permute-start.8
  19.7 0.1 collective-permute-done.1.refs_2_
  19.7 0.0 collective-permute-done.2.refs_3_
  19.7 0.0 copy-done.1
  19.7 0.0 copy-done.12
  19.7 0.0 copy-done.13
  19.7 0.0 copy-start.2
  19.7 0.0 copy-start.5
  19.8 0.0 copy-start.7
  19.8 0.0 copy-start.9
  19.8 0.0 copy-start.10
  19.8 0.0 copy-start.11
  19.8 8.1 %grad_input.1 = (f32[8,512,256]{2,1,0:T(8,128)S(1)}, bf16[128,1024]{1,0:T(8,128)(2,1)S(1)}, bf16[128,1024]{1,0:T(8,128)(2,1)S(1)}, bf16[128,1024]{1,0:T(8,128)(2,1)S(1)}, bf16[128,1024]{1,0:T(8,128)(2,1)S(1)}) custom-call(s32[1]{0:T(128)} %bitcast.me_ref, bf16[512,1024]{1,0:T(8,128)(2,1)S(1)} %copy-done.1, ...), custom_call_target="tpu_custom_call" | custom-call | flops 3221225472 | bytes 8388608 | tf_op jit(solution)/shard_map/grad_input/pallas_call | solution.py:288
  27.9 0.0 copy-start.3
  27.9 2.0 %collective-permute-start.3 = (bf16[128,1024]{1,0:T(8,128)(2,1)S(1)}, bf16[128,1024]{1,0:T(8,128)(2,1)S(1)}, u32[]{:S(2)}, u32[]{:S(2)}) collective-permute-start(bf16[128,1024]{1,0:T(8,128)(2,1)S(1)} %get-tuple-element.8), channel_id=1, source_target_pairs={{0,2},{2,0},{4,6},{6,4},{1,3},{3,1},{5,7},{7,5},{8,10},{10,8},{12,... | collective-permute-start | bytes 786440 | tf_op jit(solution)/shard_map/ppermute | solution.py:244
  29.9 1.5 %collective-permute-start.4 = (bf16[128,1024]{1,0:T(8,128)(2,1)S(1)}, bf16[128,1024]{1,0:T(8,128)(2,1)S(1)}, u32[]{:S(2)}, u32[]{:S(2)}) collective-permute-start(bf16[128,1024]{1,0:T(8,128)(2,1)S(1)} %get-tuple-element.9), channel_id=1, source_target_pairs={{0,4},{2,6},{4,0},{6,2},{1,5},{3,7},{5,1},{7,3},{8,12},{10,14},{12... | collective-permute-start | bytes 786440 | tf_op jit(solution)/shard_map/ppermute | solution.py:244
  31.4 0.0 collective-permute-done.6.refs_1_
  31.4 0.1 collective-permute-start.5
  31.5 0.0 collective-permute-done.7.refs_2_
  31.5 0.0 collective-permute-done.8.refs_3_
  31.5 0.0 copy-done.2
  31.5 0.0 copy-done.5
  31.5 0.0 copy-done.7
  31.5 0.0 copy-done.9
  31.5 0.0 copy-done.10
  31.5 0.0 copy-done.11
  31.5 8.7 %grad_filter.1 = f32[128,4096]{1,0:T(8,128)} custom-call(s32[1]{0:T(128)} %bitcast.me_ref, bf16[512,1024]{1,0:T(8,128)(2,1)S(1)} %copy-done.2, bf16[128,1024]{1,0:T(8,128)(2,1)S(1)} %collective-permute-done.6.refs_1_, bf16[128,1024]{1,0:T(8,128)(2,1)S(1)} %collective-permute-done.7.refs_2_, bf16[128,1024]{1,0:T(8,128)(2,1)S(1)} %collective-permute-done.8.refs_3_, ...), custom_call_target="tpu_custom_call" | custom-call | flops 3221225472 | bytes 8388608 | tf_op jit(solution)/shard_map/grad_filter/pallas_call | solution.py:306
  40.3 0.0 copy-done.3
  40.3 0.0 collective-permute-done.3.refs_1_
  40.3 0.0 copy-start.14
  40.3 1.3 %collective-permute-done.4.refs_2_ = bf16[128,1024]{1,0:T(8,128)(2,1)S(1)} collective-permute-done((bf16[128,1024]{1,0:T(8,128)(2,1)S(1)}, bf16[128,1024]{1,0:T(8,128)(2,1)S(1)}, u32[]{:S(2)}, u32[]{:S(2)}) %collective-permute-start.4) | collective-permute-done | bytes 262176 | tf_op jit(solution)/shard_map/ppermute | solution.py:244
  41.6 0.0 copy-start.15
  41.6 0.0 collective-permute-done.5.refs_3_
  41.6 0.0 copy-start.16
  41.6 0.0 copy-done.14
  41.6 0.7 copy-done.15
  42.3 0.1 copy-done.16
  42.4 32.9 %gather_pieces.1 = bf16[512,1024]{1,0:T(8,128)(2,1)} custom-call(s32[1]{0:T(128)} %bitcast.me_ref, bf16[128,1024]{1,0:T(8,128)(2,1)} %copy-done.3, bf16[128,1024]{1,0:T(8,128)(2,1)} %copy-done.14, bf16[128,1024]{1,0:T(8,128)(2,1)} %copy-done.15, bf16[128,1024]{1,0:T(8,128)(2,1)} %copy-done.16), custom_call_target="tpu_custom_call" | custom-call | tf_op jit(solution)/shard_map/gather_pieces/pallas_call | solution.py:322
Async XLA Ops:
  1.8 17.9 %copy-start.1 = (bf16[512,1024]{1,0:T(8,128)(2,1)S(1)}, bf16[512,1024]{1,0:T(8,128)(2,1)}, u32[]{:S(2)}) copy-start(bf16[512,1024]{1,0:T(8,128)(2,1)} %refs_0_.2) | copy-start | bytes 3145732
  1.8 17.9 %copy-start.12 = (bf16[256,256]{1,0:T(8,128)(2,1)S(1)}, bf16[256,256]{1,0:T(8,128)(2,1)}, u32[]{:S(2)}) copy-start(bf16[256,256]{1,0:T(8,128)(2,1)} %constant.45.clone.refs_7_) | copy-start | bytes 393220
  1.8 17.9 %copy-start.13 = (bf16[256,256]{1,0:T(8,128)(2,1)S(1)}, bf16[256,256]{1,0:T(8,128)(2,1)}, u32[]{:S(2)}) copy-start(bf16[256,256]{1,0:T(8,128)(2,1)} %constant.46.clone.refs_8_) | copy-start | bytes 393220
  1.9 17.7 %collective-permute-start = (bf16[128,1024]{1,0:T(8,128)(2,1)S(1)}, bf16[128,1024]{1,0:T(8,128)(2,1)S(1)}, u32[]{:S(2)}, u32[]{:S(2)}) collective-permute-start(bf16[128,1024]{1,0:T(8,128)(2,1)S(1)} %get-tuple-element.17), channel_id=1, source_target_pairs={{0,2},{2,0},{4,6},{6,4},{1,3},{3,1},{5,7},{7,5},{8,10},{10,8},{12,... | collective-permute-start | bytes 786440 | tf_op jit(solution)/shard_map/ppermute | solution.py:244
  4.9 14.8 %collective-permute-start.1 = (bf16[128,1024]{1,0:T(8,128)(2,1)S(1)}, bf16[128,1024]{1,0:T(8,128)(2,1)S(1)}, u32[]{:S(2)}, u32[]{:S(2)}) collective-permute-start(bf16[128,1024]{1,0:T(8,128)(2,1)S(1)} %get-tuple-element.16), channel_id=1, source_target_pairs={{0,4},{2,6},{4,0},{6,2},{1,5},{3,7},{5,1},{7,3},{8,12},{10,14},{12... | collective-permute-start | bytes 786440 | tf_op jit(solution)/shard_map/ppermute | solution.py:244
  6.4 13.3 %collective-permute-start.2 = (bf16[128,1024]{1,0:T(8,128)(2,1)S(1)}, bf16[128,1024]{1,0:T(8,128)(2,1)S(1)}, u32[]{:S(2)}, u32[]{:S(2)}) collective-permute-start(bf16[128,1024]{1,0:T(8,128)(2,1)S(1)} %get-tuple-element.15), channel_id=1, source_target_pairs={{0,6},{2,4},{4,2},{6,0},{1,7},{3,5},{5,3},{7,1},{8,14},{10,12},{12... | collective-permute-start | bytes 786440 | tf_op jit(solution)/shard_map/ppermute | solution.py:244
  7.6 23.9 %collective-permute-start.6 = (bf16[128,1024]{1,0:T(8,128)(2,1)S(1)}, bf16[128,1024]{1,0:T(8,128)(2,1)S(1)}, u32[]{:S(2)}, u32[]{:S(2)}) collective-permute-start(bf16[128,1024]{1,0:T(8,128)(2,1)S(1)} %get-tuple-element.14), channel_id=1, source_target_pairs={{0,2},{2,0},{4,6},{6,4},{1,3},{3,1},{5,7},{7,5},{8,10},{10,8},{12,... | collective-permute-start | bytes 786440 | tf_op jit(solution)/shard_map/ppermute | solution.py:244
  9.6 21.9 %collective-permute-start.7 = (bf16[128,1024]{1,0:T(8,128)(2,1)S(1)}, bf16[128,1024]{1,0:T(8,128)(2,1)S(1)}, u32[]{:S(2)}, u32[]{:S(2)}) collective-permute-start(bf16[128,1024]{1,0:T(8,128)(2,1)S(1)} %get-tuple-element.13), channel_id=1, source_target_pairs={{0,4},{2,6},{4,0},{6,2},{1,5},{3,7},{5,1},{7,3},{8,12},{10,14},{12... | collective-permute-start | bytes 786440 | tf_op jit(solution)/shard_map/ppermute | solution.py:244
  11.1 1.6 %copy-start = (f32[1,128,4096]{2,1,0:T(8,128)S(1)}, f32[1,128,4096]{2,1,0:T(8,128)}, u32[]{:S(2)}) copy-start(f32[1,128,4096]{2,1,0:T(8,128)} %param.12) | copy-start | bytes 6291460
  12.7 0.9 %copy-start.4 = (bf16[256,256]{1,0:T(8,128)(2,1)S(1)}, bf16[256,256]{1,0:T(8,128)(2,1)}, u32[]{:S(2)}) copy-start(bf16[256,256]{1,0:T(8,128)(2,1)} %constant.42.clone.ahead_high.refs_5_) | copy-start | bytes 393220
  13.6 0.9 %copy-start.6 = (bf16[256,256]{1,0:T(8,128)(2,1)S(1)}, bf16[256,256]{1,0:T(8,128)(2,1)}, u32[]{:S(2)}) copy-start(bf16[256,256]{1,0:T(8,128)(2,1)} %constant.43.clone.ahead_low.refs_6_) | copy-start | bytes 393220
  14.5 0.8 %copy-start.8 = (f32[32,2,128]{2,1,0:T(2,128)S(1)}, f32[32,2,128]{2,1,0:T(2,128)}, u32[]{:S(2)}) copy-start(f32[32,2,128]{2,1,0:T(2,128)} %constant.44.clone.twiddle_ref.refs_9_) | copy-start | bytes 98308
  19.6 11.9 %collective-permute-start.8 = (bf16[128,1024]{1,0:T(8,128)(2,1)S(1)}, bf16[128,1024]{1,0:T(8,128)(2,1)S(1)}, u32[]{:S(2)}, u32[]{:S(2)}) collective-permute-start(bf16[128,1024]{1,0:T(8,128)(2,1)S(1)} %get-tuple-element.12), channel_id=1, source_target_pairs={{0,6},{2,4},{4,2},{6,0},{1,7},{3,5},{5,3},{7,1},{8,14},{10,12},{12... | collective-permute-start | bytes 786440 | tf_op jit(solution)/shard_map/ppermute | solution.py:244
  19.7 11.8 %copy-start.2 = (bf16[512,1024]{1,0:T(8,128)(2,1)S(1)}, bf16[512,1024]{1,0:T(8,128)(2,1)}, u32[]{:S(2)}) copy-start(bf16[512,1024]{1,0:T(8,128)(2,1)} %refs_0_.3) | copy-start | bytes 3145732
  19.7 11.8 %copy-start.5 = (bf16[256,256]{1,0:T(8,128)(2,1)S(1)}, bf16[256,256]{1,0:T(8,128)(2,1)}, u32[]{:S(2)}) copy-start(bf16[256,256]{1,0:T(8,128)(2,1)} %constant.42.clone.ahead_high.refs_5_) | copy-start | bytes 393220
  19.8 11.8 %copy-start.7 = (bf16[256,256]{1,0:T(8,128)(2,1)S(1)}, bf16[256,256]{1,0:T(8,128)(2,1)}, u32[]{:S(2)}) copy-start(bf16[256,256]{1,0:T(8,128)(2,1)} %constant.43.clone.ahead_low.refs_6_) | copy-start | bytes 393220
  19.8 11.7 %copy-start.9 = (f32[32,2,128]{2,1,0:T(2,128)S(1)}, f32[32,2,128]{2,1,0:T(2,128)}, u32[]{:S(2)}) copy-start(f32[32,2,128]{2,1,0:T(2,128)} %constant.44.clone.twiddle_ref.refs_9_) | copy-start | bytes 98308
  19.8 11.7 %copy-start.10 = (bf16[256,256]{1,0:T(8,128)(2,1)S(1)}, bf16[256,256]{1,0:T(8,128)(2,1)}, u32[]{:S(2)}) copy-start(bf16[256,256]{1,0:T(8,128)(2,1)} %constant.47.clone.refs_7_) | copy-start | bytes 393220
  19.8 11.7 %copy-start.11 = (bf16[256,256]{1,0:T(8,128)(2,1)S(1)}, bf16[256,256]{1,0:T(8,128)(2,1)}, u32[]{:S(2)}) copy-start(bf16[256,256]{1,0:T(8,128)(2,1)} %constant.48.clone.refs_8_) | copy-start | bytes 393220
  27.9 12.4 %copy-start.3 = (bf16[128,1024]{1,0:T(8,128)(2,1)}, bf16[128,1024]{1,0:T(8,128)(2,1)S(1)}, u32[]{:S(2)}) copy-start(bf16[128,1024]{1,0:T(8,128)(2,1)S(1)} %get-tuple-element.7.refs_0_) | copy-start | bytes 786436
  27.9 12.3 %collective-permute-start.3 = (bf16[128,1024]{1,0:T(8,128)(2,1)S(1)}, bf16[128,1024]{1,0:T(8,128)(2,1)S(1)}, u32[]{:S(2)}, u32[]{:S(2)}) collective-permute-start(bf16[128,1024]{1,0:T(8,128)(2,1)S(1)} %get-tuple-element.8), channel_id=1, source_target_pairs={{0,2},{2,0},{4,6},{6,4},{1,3},{3,1},{5,7},{7,5},{8,10},{10,8},{12,... | collective-permute-start | bytes 786440 | tf_op jit(solution)/shard_map/ppermute | solution.py:244
  29.9 11.7 %collective-permute-start.4 = (bf16[128,1024]{1,0:T(8,128)(2,1)S(1)}, bf16[128,1024]{1,0:T(8,128)(2,1)S(1)}, u32[]{:S(2)}, u32[]{:S(2)}) collective-permute-start(bf16[128,1024]{1,0:T(8,128)(2,1)S(1)} %get-tuple-element.9), channel_id=1, source_target_pairs={{0,4},{2,6},{4,0},{6,2},{1,5},{3,7},{5,1},{7,3},{8,12},{10,14},{12... | collective-permute-start | bytes 786440 | tf_op jit(solution)/shard_map/ppermute | solution.py:244
  31.4 10.2 %collective-permute-start.5 = (bf16[128,1024]{1,0:T(8,128)(2,1)S(1)}, bf16[128,1024]{1,0:T(8,128)(2,1)S(1)}, u32[]{:S(2)}, u32[]{:S(2)}) collective-permute-start(bf16[128,1024]{1,0:T(8,128)(2,1)S(1)} %get-tuple-element.10), channel_id=1, source_target_pairs={{0,6},{2,4},{4,2},{6,0},{1,7},{3,5},{5,3},{7,1},{8,14},{10,12},{12... | collective-permute-start | bytes 786440 | tf_op jit(solution)/shard_map/ppermute | solution.py:244
  40.3 1.3 %copy-start.14 = (bf16[128,1024]{1,0:T(8,128)(2,1)}, bf16[128,1024]{1,0:T(8,128)(2,1)S(1)}, u32[]{:S(2)}) copy-start(bf16[128,1024]{1,0:T(8,128)(2,1)S(1)} %collective-permute-done.3.refs_1_) | copy-start | bytes 786436
  41.6 0.7 copy-start.15
  41.6 0.8 %copy-start.16 = (bf16[128,1024]{1,0:T(8,128)(2,1)}, bf16[128,1024]{1,0:T(8,128)(2,1)S(1)}, u32[]{:S(2)}) copy-start(bf16[128,1024]{1,0:T(8,128)(2,1)S(1)} %collective-permute-done.5.refs_3_) | copy-start | bytes 786436

commit v2 on v1

--- a/solution.py
+++ b/solution.py
@@ -321,7 +321,7 @@
     if aligned:
         grad_input = pl.pallas_call(
             functools.partial(gather_kernel, pencil=pencil),
-            in_specs=[pl.BlockSpec(memory_space=pltpu.SMEM), *[pl.BlockSpec(memory_space=pl.ANY)] * parts],
+            in_specs=[pl.BlockSpec(memory_space=pltpu.SMEM), *[pl.BlockSpec(memory_space=pltpu.VMEM)] * parts],
             out_specs=pl.BlockSpec(memory_space=pl.ANY),
             out_shape=jax.ShapeDtypeStruct((parts * pencil, piece), jnp.bfloat16),
             scratch_shapes=[pltpu.SemaphoreType.DMA((parts,))],

time: 75.6 us -> 44.9 us (0.59)
  Pallas kernels: 54 us -> 23.3 us
    pallas_call x1, Pallas kernels: 32.9 us -> 2.18 us  [shards(): pl.pallas_call(functools.partial(gather_kernel, pencil=pencil), in_specs=...]
  transfers between devices with their start and end apart: 9 -> 9, of which waited for: 2 -> 2; matrix products, arithmetic and copies ran while one was open for 2% -> 3% of each run, Pallas kernels for 28% -> 47%
where the time goes in v2:
time: 44.9 us; the launch traced here: 44.6 us
  Pallas kernels  23.3 us (52%)
  starting transfers between devices  11.7 us (26%)
  local copies, waits for them, and re-layouts  7.36 us (16%)
  waiting for transfers between devices  1.4 us (3%)
  between operations  0.84 us (2%)
    ppermute x9, starting transfers between devices, swap(): return lax.ppermute(block, 'ctx', [(i, i ^ k) for i in range(parts)])  11.7 us
    pallas_call x1, Pallas kernels, shards(): pl.pallas_call(functools.partial(filter_kernel, outer=outer, parts=parts)...  8.72 us
    pallas_call x1, Pallas kernels, shards(): pl.pallas_call(functools.partial(input_kernel, outer=outer, parts=parts),...  8.1 us
    unnamed x34, local copies, waits for them, and re-layouts  5.03 us
    pallas_call x1, Pallas kernels, shards(): pl.pallas_call(functools.partial(spectrum_kernel, outer=outer), grid=(ste...  4.29 us
    squeeze x2, local copies, waits for them, and re-layouts, pick(): return lax.dynamic_index_in_dim(blocks, me ^ k, 0, keepdims=False)  2.33 us
    pallas_call x1, Pallas kernels, shards(): pl.pallas_call(functools.partial(gather_kernel, pencil=pencil), in_specs=...  2.18 us
    ppermute x9, waiting for transfers between devices, swap(): return lax.ppermute(block, 'ctx', [(i, i ^ k) for i in range(parts)])  1.4 us
  transfers between devices with their start and end apart: 9, of which 2 were waited for; matrix products, arithmetic and copies ran while one was open for 3% of the time, Pallas kernels for 47%

profile of v2, /device:TPU:0, one launch (start us, length us, event | category | flops | bytes accessed | tf_op | source)
XLA Modules:
  0.0 44.6 jit_solution(13028171258037914721)
XLA Ops:
  0.6 1.2 %dynamic-slice_bitcast_fusion.3 = (bf16[128,1024]{1,0:T(8,128)(2,1)S(1)}, bf16[128,1024]{1,0:T(8,128)(2,1)S(1)}, bf16[128,1024]{1,0:T(8,128)(2,1)S(1)}) fusion(bf16[4,128,1024]{2,1,0:T(8,128)(2,1)} %bitcast.18, s32[]{:T(128)S(6)} %select_n.15, s32[]{:T(128)S(6)} %select_n.14, s32[]{:T(128)S(6)} %select_n.13), kind=kLoop, calls=%fused_computation.3 | loop fusion | bytes 1572876 | tf_op jit(solution)/shard_map/jit(dynamic_index_in_dim)/squeeze | solution.py:248
  1.8 0.0 copy-start.1
  1.8 0.0 copy-start.12
  1.8 0.0 copy-start.13
  1.9 3.0 %collective-permute-start = (bf16[128,1024]{1,0:T(8,128)(2,1)S(1)}, bf16[128,1024]{1,0:T(8,128)(2,1)S(1)}, u32[]{:S(2)}, u32[]{:S(2)}) collective-permute-start(bf16[128,1024]{1,0:T(8,128)(2,1)S(1)} %get-tuple-element.17), channel_id=1, source_target_pairs={{0,2},{2,0},{4,6},{6,4},{1,3},{3,1},{5,7},{7,5},{8,10},{10,8},{12,... | collective-permute-start | bytes 786440 | tf_op jit(solution)/shard_map/ppermute | solution.py:244
  4.9 1.5 %collective-permute-start.1 = (bf16[128,1024]{1,0:T(8,128)(2,1)S(1)}, bf16[128,1024]{1,0:T(8,128)(2,1)S(1)}, u32[]{:S(2)}, u32[]{:S(2)}) collective-permute-start(bf16[128,1024]{1,0:T(8,128)(2,1)S(1)} %get-tuple-element.16), channel_id=1, source_target_pairs={{0,4},{2,6},{4,0},{6,2},{1,5},{3,7},{5,1},{7,3},{8,12},{10,14},{12... | collective-permute-start | bytes 786440 | tf_op jit(solution)/shard_map/ppermute | solution.py:244
  6.4 0.0 collective-permute-start.2
  6.4 1.2 %dynamic-slice_bitcast_fusion = (bf16[128,1024]{1,0:T(8,128)(2,1)S(1)}, bf16[128,1024]{1,0:T(8,128)(2,1)S(1)}, bf16[128,1024]{1,0:T(8,128)(2,1)S(1)}) fusion(bf16[4,128,1024]{2,1,0:T(8,128)(2,1)} %bitcast.19, s32[]{:T(128)S(6)} %select_n.15, s32[]{:T(128)S(6)} %select_n.14, s32[]{:T(128)S(6)} %select_n.13), kind=kLoop, calls=%fused_computation | loop fusion | bytes 1572876 | tf_op jit(solution)/shard_map/jit(dynamic_index_in_dim)/squeeze | solution.py:248
  7.6 2.0 %collective-permute-start.6 = (bf16[128,1024]{1,0:T(8,128)(2,1)S(1)}, bf16[128,1024]{1,0:T(8,128)(2,1)S(1)}, u32[]{:S(2)}, u32[]{:S(2)}) collective-permute-start(bf16[128,1024]{1,0:T(8,128)(2,1)S(1)} %get-tuple-element.14), channel_id=1, source_target_pairs={{0,2},{2,0},{4,6},{6,4},{1,3},{3,1},{5,7},{7,5},{8,10},{10,8},{12,... | collective-permute-start | bytes 786440 | tf_op jit(solution)/shard_map/ppermute | solution.py:244
  9.6 1.5 %collective-permute-start.7 = (bf16[128,1024]{1,0:T(8,128)(2,1)S(1)}, bf16[128,1024]{1,0:T(8,128)(2,1)S(1)}, u32[]{:S(2)}, u32[]{:S(2)}) collective-permute-start(bf16[128,1024]{1,0:T(8,128)(2,1)S(1)} %get-tuple-element.13), channel_id=1, source_target_pairs={{0,4},{2,6},{4,0},{6,2},{1,5},{3,7},{5,1},{7,3},{8,12},{10,14},{12... | collective-permute-start | bytes 786440 | tf_op jit(solution)/shard_map/ppermute | solution.py:244
  11.1 0.0 copy-start
  11.1 1.6 %copy-done = f32[1,128,4096]{2,1,0:T(8,128)S(1)} copy-done((f32[1,128,4096]{2,1,0:T(8,128)S(1)}, f32[1,128,4096]{2,1,0:T(8,128)}, u32[]{:S(2)}) %copy-start) | copy-done | bytes 2097176
  12.7 0.0 copy-start.4
  12.7 0.9 %copy-done.4 = bf16[256,256]{1,0:T(8,128)(2,1)S(1)} copy-done((bf16[256,256]{1,0:T(8,128)(2,1)S(1)}, bf16[256,256]{1,0:T(8,128)(2,1)}, u32[]{:S(2)}) %copy-start.4) | copy-done | bytes 131096
  13.6 0.0 copy-start.6
  13.6 0.9 %copy-done.6 = bf16[256,256]{1,0:T(8,128)(2,1)S(1)} copy-done((bf16[256,256]{1,0:T(8,128)(2,1)S(1)}, bf16[256,256]{1,0:T(8,128)(2,1)}, u32[]{:S(2)}) %copy-start.6) | copy-done | bytes 131096
  14.5 0.0 copy-start.8
  14.5 0.8 %copy-done.8 = f32[32,2,128]{2,1,0:T(2,128)S(1)} copy-done((f32[32,2,128]{2,1,0:T(2,128)S(1)}, f32[32,2,128]{2,1,0:T(2,128)}, u32[]{:S(2)}) %copy-start.8) | copy-done | bytes 32792
  15.3 4.3 %taps_spectrum.1.refs_4_ = f32[8,512,256]{2,1,0:T(8,128)S(1)} custom-call(f32[128,4096]{1,0:T(8,128)S(1)} %bitcast.17, bf16[256,256]{1,0:T(8,128)(2,1)S(1)} %copy-done.4, bf16[256,256]{1,0:T(8,128)(2,1)S(1)} %copy-done.6, f32[32,2,128]{2,1,0:T(2,128)S(1)} %copy-done.8), custom_call_target="tpu_custom_call" | custom-call | flops 1610612736 | bytes 8388608 | tf_op jit(solution)/shard_map/taps_spectrum/pallas_call | solution.py:275
  19.6 0.0 collective-permute-done.refs_1_
  19.6 0.1 collective-permute-start.8
  19.7 0.1 collective-permute-done.1.refs_2_
  19.7 0.0 collective-permute-done.2.refs_3_
  19.7 0.0 copy-done.1
  19.7 0.0 copy-done.12
  19.7 0.0 copy-done.13
  19.7 0.0 copy-start.2
  19.7 0.0 copy-start.5
  19.8 0.0 copy-start.7
  19.8 0.0 copy-start.9
  19.8 0.0 copy-start.10
  19.8 0.0 copy-start.11
  19.8 8.1 %grad_input.1 = (f32[8,512,256]{2,1,0:T(8,128)S(1)}, bf16[128,1024]{1,0:T(8,128)(2,1)S(1)}, bf16[128,1024]{1,0:T(8,128)(2,1)S(1)}, bf16[128,1024]{1,0:T(8,128)(2,1)S(1)}, bf16[128,1024]{1,0:T(8,128)(2,1)S(1)}) custom-call(s32[1]{0:T(128)} %bitcast.me_ref, bf16[512,1024]{1,0:T(8,128)(2,1)S(1)} %copy-done.1, ...), custom_call_target="tpu_custom_call" | custom-call | flops 3221225472 | bytes 8388608 | tf_op jit(solution)/shard_map/grad_input/pallas_call | solution.py:288
  27.9 0.0 copy-start.3
  27.9 2.0 %collective-permute-start.3 = (bf16[128,1024]{1,0:T(8,128)(2,1)S(1)}, bf16[128,1024]{1,0:T(8,128)(2,1)S(1)}, u32[]{:S(2)}, u32[]{:S(2)}) collective-permute-start(bf16[128,1024]{1,0:T(8,128)(2,1)S(1)} %get-tuple-element.8), channel_id=1, source_target_pairs={{0,2},{2,0},{4,6},{6,4},{1,3},{3,1},{5,7},{7,5},{8,10},{10,8},{12,... | collective-permute-start | bytes 786440 | tf_op jit(solution)/shard_map/ppermute | solution.py:244
  29.9 1.5 %collective-permute-start.4 = (bf16[128,1024]{1,0:T(8,128)(2,1)S(1)}, bf16[128,1024]{1,0:T(8,128)(2,1)S(1)}, u32[]{:S(2)}, u32[]{:S(2)}) collective-permute-start(bf16[128,1024]{1,0:T(8,128)(2,1)S(1)} %get-tuple-element.9), channel_id=1, source_target_pairs={{0,4},{2,6},{4,0},{6,2},{1,5},{3,7},{5,1},{7,3},{8,12},{10,14},{12... | collective-permute-start | bytes 786440 | tf_op jit(solution)/shard_map/ppermute | solution.py:244
  31.4 0.0 collective-permute-done.6.refs_1_
  31.4 0.1 collective-permute-start.5
  31.5 0.0 collective-permute-done.7.refs_2_
  31.5 0.0 collective-permute-done.8.refs_3_
  31.5 0.0 copy-done.2
  31.5 0.0 copy-done.5
  31.5 0.0 copy-done.7
  31.5 0.0 copy-done.9
  31.5 0.0 copy-done.10
  31.5 0.0 copy-done.11
  31.5 8.7 %grad_filter.1 = f32[128,4096]{1,0:T(8,128)} custom-call(s32[1]{0:T(128)} %bitcast.me_ref, bf16[512,1024]{1,0:T(8,128)(2,1)S(1)} %copy-done.2, bf16[128,1024]{1,0:T(8,128)(2,1)S(1)} %collective-permute-done.6.refs_1_, bf16[128,1024]{1,0:T(8,128)(2,1)S(1)} %collective-permute-done.7.refs_2_, bf16[128,1024]{1,0:T(8,128)(2,1)S(1)} %collective-permute-done.8.refs_3_, ...), custom_call_target="tpu_custom_call" | custom-call | flops 3221225472 | bytes 8388608 | tf_op jit(solution)/shard_map/grad_filter/pallas_call | solution.py:306
  40.3 0.0 copy-done.3
  40.3 0.0 collective-permute-done.3.refs_1_
  40.3 0.0 copy-start.14
  40.3 1.3 %collective-permute-done.4.refs_2_ = bf16[128,1024]{1,0:T(8,128)(2,1)S(1)} collective-permute-done((bf16[128,1024]{1,0:T(8,128)(2,1)S(1)}, bf16[128,1024]{1,0:T(8,128)(2,1)S(1)}, u32[]{:S(2)}, u32[]{:S(2)}) %collective-permute-start.4) | collective-permute-done | bytes 262176 | tf_op jit(solution)/shard_map/ppermute | solution.py:244
  41.6 0.0 copy-start.15
  41.6 0.0 collective-permute-done.5.refs_3_
  41.6 0.0 copy-start.16
  41.6 0.0 copy-done.14
  41.6 0.7 %copy-done.15 = bf16[128,1024]{1,0:T(8,128)(2,1)} copy-done((bf16[128,1024]{1,0:T(8,128)(2,1)}, bf16[128,1024]{1,0:T(8,128)(2,1)S(1)}, u32[]{:S(2)}) %copy-start.15) | copy-done | bytes 262168
  42.3 0.1 copy-done.16
  42.4 2.2 %gather_pieces.1 = bf16[512,1024]{1,0:T(8,128)(2,1)} custom-call(s32[1]{0:T(128)} %bitcast.me_ref, bf16[128,1024]{1,0:T(8,128)(2,1)} %copy-done.3, bf16[128,1024]{1,0:T(8,128)(2,1)} %copy-done.14, bf16[128,1024]{1,0:T(8,128)(2,1)} %copy-done.15, bf16[128,1024]{1,0:T(8,128)(2,1)} %copy-done.16), custom_call_target="tpu_custom_call" | custom-call | tf_op jit(solution)/shard_map/gather_pieces/pallas_call | solution.py:322
Async XLA Ops:
  1.8 17.9 %copy-start.1 = (bf16[512,1024]{1,0:T(8,128)(2,1)S(1)}, bf16[512,1024]{1,0:T(8,128)(2,1)}, u32[]{:S(2)}) copy-start(bf16[512,1024]{1,0:T(8,128)(2,1)} %refs_0_.2) | copy-start | bytes 3145732
  1.8 17.9 %copy-start.12 = (bf16[256,256]{1,0:T(8,128)(2,1)S(1)}, bf16[256,256]{1,0:T(8,128)(2,1)}, u32[]{:S(2)}) copy-start(bf16[256,256]{1,0:T(8,128)(2,1)} %constant.45.clone.refs_7_) | copy-start | bytes 393220
  1.8 17.9 %copy-start.13 = (bf16[256,256]{1,0:T(8,128)(2,1)S(1)}, bf16[256,256]{1,0:T(8,128)(2,1)}, u32[]{:S(2)}) copy-start(bf16[256,256]{1,0:T(8,128)(2,1)} %constant.46.clone.refs_8_) | copy-start | bytes 393220
  1.9 17.7 %collective-permute-start = (bf16[128,1024]{1,0:T(8,128)(2,1)S(1)}, bf16[128,1024]{1,0:T(8,128)(2,1)S(1)}, u32[]{:S(2)}, u32[]{:S(2)}) collective-permute-start(bf16[128,1024]{1,0:T(8,128)(2,1)S(1)} %get-tuple-element.17), channel_id=1, source_target_pairs={{0,2},{2,0},{4,6},{6,4},{1,3},{3,1},{5,7},{7,5},{8,10},{10,8},{12,... | collective-permute-start | bytes 786440 | tf_op jit(solution)/shard_map/ppermute | solution.py:244
  4.9 14.8 %collective-permute-start.1 = (bf16[128,1024]{1,0:T(8,128)(2,1)S(1)}, bf16[128,1024]{1,0:T(8,128)(2,1)S(1)}, u32[]{:S(2)}, u32[]{:S(2)}) collective-permute-start(bf16[128,1024]{1,0:T(8,128)(2,1)S(1)} %get-tuple-element.16), channel_id=1, source_target_pairs={{0,4},{2,6},{4,0},{6,2},{1,5},{3,7},{5,1},{7,3},{8,12},{10,14},{12... | collective-permute-start | bytes 786440 | tf_op jit(solution)/shard_map/ppermute | solution.py:244
  6.4 13.3 %collective-permute-start.2 = (bf16[128,1024]{1,0:T(8,128)(2,1)S(1)}, bf16[128,1024]{1,0:T(8,128)(2,1)S(1)}, u32[]{:S(2)}, u32[]{:S(2)}) collective-permute-start(bf16[128,1024]{1,0:T(8,128)(2,1)S(1)} %get-tuple-element.15), channel_id=1, source_target_pairs={{0,6},{2,4},{4,2},{6,0},{1,7},{3,5},{5,3},{7,1},{8,14},{10,12},{12... | collective-permute-start | bytes 786440 | tf_op jit(solution)/shard_map/ppermute | solution.py:244
  7.6 23.9 %collective-permute-start.6 = (bf16[128,1024]{1,0:T(8,128)(2,1)S(1)}, bf16[128,1024]{1,0:T(8,128)(2,1)S(1)}, u32[]{:S(2)}, u32[]{:S(2)}) collective-permute-start(bf16[128,1024]{1,0:T(8,128)(2,1)S(1)} %get-tuple-element.14), channel_id=1, source_target_pairs={{0,2},{2,0},{4,6},{6,4},{1,3},{3,1},{5,7},{7,5},{8,10},{10,8},{12,... | collective-permute-start | bytes 786440 | tf_op jit(solution)/shard_map/ppermute | solution.py:244
  9.6 21.9 %collective-permute-start.7 = (bf16[128,1024]{1,0:T(8,128)(2,1)S(1)}, bf16[128,1024]{1,0:T(8,128)(2,1)S(1)}, u32[]{:S(2)}, u32[]{:S(2)}) collective-permute-start(bf16[128,1024]{1,0:T(8,128)(2,1)S(1)} %get-tuple-element.13), channel_id=1, source_target_pairs={{0,4},{2,6},{4,0},{6,2},{1,5},{3,7},{5,1},{7,3},{8,12},{10,14},{12... | collective-permute-start | bytes 786440 | tf_op jit(solution)/shard_map/ppermute | solution.py:244
  11.1 1.6 %copy-start = (f32[1,128,4096]{2,1,0:T(8,128)S(1)}, f32[1,128,4096]{2,1,0:T(8,128)}, u32[]{:S(2)}) copy-start(f32[1,128,4096]{2,1,0:T(8,128)} %param.12) | copy-start | bytes 6291460
  12.7 0.9 %copy-start.4 = (bf16[256,256]{1,0:T(8,128)(2,1)S(1)}, bf16[256,256]{1,0:T(8,128)(2,1)}, u32[]{:S(2)}) copy-start(bf16[256,256]{1,0:T(8,128)(2,1)} %constant.42.clone.ahead_high.refs_5_) | copy-start | bytes 393220
  13.6 0.9 %copy-start.6 = (bf16[256,256]{1,0:T(8,128)(2,1)S(1)}, bf16[256,256]{1,0:T(8,128)(2,1)}, u32[]{:S(2)}) copy-start(bf16[256,256]{1,0:T(8,128)(2,1)} %constant.43.clone.ahead_low.refs_6_) | copy-start | bytes 393220
  14.5 0.8 %copy-start.8 = (f32[32,2,128]{2,1,0:T(2,128)S(1)}, f32[32,2,128]{2,1,0:T(2,128)}, u32[]{:S(2)}) copy-start(f32[32,2,128]{2,1,0:T(2,128)} %constant.44.clone.twiddle_ref.refs_9_) | copy-start | bytes 98308
  19.6 11.9 %collective-permute-start.8 = (bf16[128,1024]{1,0:T(8,128)(2,1)S(1)}, bf16[128,1024]{1,0:T(8,128)(2,1)S(1)}, u32[]{:S(2)}, u32[]{:S(2)}) collective-permute-start(bf16[128,1024]{1,0:T(8,128)(2,1)S(1)} %get-tuple-element.12), channel_id=1, source_target_pairs={{0,6},{2,4},{4,2},{6,0},{1,7},{3,5},{5,3},{7,1},{8,14},{10,12},{12... | collective-permute-start | bytes 786440 | tf_op jit(solution)/shard_map/ppermute | solution.py:244
  19.7 11.8 %copy-start.2 = (bf16[512,1024]{1,0:T(8,128)(2,1)S(1)}, bf16[512,1024]{1,0:T(8,128)(2,1)}, u32[]{:S(2)}) copy-start(bf16[512,1024]{1,0:T(8,128)(2,1)} %refs_0_.3) | copy-start | bytes 3145732
  19.7 11.8 %copy-start.5 = (bf16[256,256]{1,0:T(8,128)(2,1)S(1)}, bf16[256,256]{1,0:T(8,128)(2,1)}, u32[]{:S(2)}) copy-start(bf16[256,256]{1,0:T(8,128)(2,1)} %constant.42.clone.ahead_high.refs_5_) | copy-start | bytes 393220
  19.8 11.8 %copy-start.7 = (bf16[256,256]{1,0:T(8,128)(2,1)S(1)}, bf16[256,256]{1,0:T(8,128)(2,1)}, u32[]{:S(2)}) copy-start(bf16[256,256]{1,0:T(8,128)(2,1)} %constant.43.clone.ahead_low.refs_6_) | copy-start | bytes 393220
  19.8 11.7 %copy-start.9 = (f32[32,2,128]{2,1,0:T(2,128)S(1)}, f32[32,2,128]{2,1,0:T(2,128)}, u32[]{:S(2)}) copy-start(f32[32,2,128]{2,1,0:T(2,128)} %constant.44.clone.twiddle_ref.refs_9_) | copy-start | bytes 98308
  19.8 11.7 %copy-start.10 = (bf16[256,256]{1,0:T(8,128)(2,1)S(1)}, bf16[256,256]{1,0:T(8,128)(2,1)}, u32[]{:S(2)}) copy-start(bf16[256,256]{1,0:T(8,128)(2,1)} %constant.47.clone.refs_7_) | copy-start | bytes 393220
  19.8 11.7 %copy-start.11 = (bf16[256,256]{1,0:T(8,128)(2,1)S(1)}, bf16[256,256]{1,0:T(8,128)(2,1)}, u32[]{:S(2)}) copy-start(bf16[256,256]{1,0:T(8,128)(2,1)} %constant.48.clone.refs_8_) | copy-start | bytes 393220
  27.9 12.4 %copy-start.3 = (bf16[128,1024]{1,0:T(8,128)(2,1)}, bf16[128,1024]{1,0:T(8,128)(2,1)S(1)}, u32[]{:S(2)}) copy-start(bf16[128,1024]{1,0:T(8,128)(2,1)S(1)} %get-tuple-element.7.refs_0_) | copy-start | bytes 786436
  27.9 12.3 %collective-permute-start.3 = (bf16[128,1024]{1,0:T(8,128)(2,1)S(1)}, bf16[128,1024]{1,0:T(8,128)(2,1)S(1)}, u32[]{:S(2)}, u32[]{:S(2)}) collective-permute-start(bf16[128,1024]{1,0:T(8,128)(2,1)S(1)} %get-tuple-element.8), channel_id=1, source_target_pairs={{0,2},{2,0},{4,6},{6,4},{1,3},{3,1},{5,7},{7,5},{8,10},{10,8},{12,... | collective-permute-start | bytes 786440 | tf_op jit(solution)/shard_map/ppermute | solution.py:244
  29.9 11.7 %collective-permute-start.4 = (bf16[128,1024]{1,0:T(8,128)(2,1)S(1)}, bf16[128,1024]{1,0:T(8,128)(2,1)S(1)}, u32[]{:S(2)}, u32[]{:S(2)}) collective-permute-start(bf16[128,1024]{1,0:T(8,128)(2,1)S(1)} %get-tuple-element.9), channel_id=1, source_target_pairs={{0,4},{2,6},{4,0},{6,2},{1,5},{3,7},{5,1},{7,3},{8,12},{10,14},{12... | collective-permute-start | bytes 786440 | tf_op jit(solution)/shard_map/ppermute | solution.py:244
  31.4 10.2 %collective-permute-start.5 = (bf16[128,1024]{1,0:T(8,128)(2,1)S(1)}, bf16[128,1024]{1,0:T(8,128)(2,1)S(1)}, u32[]{:S(2)}, u32[]{:S(2)}) collective-permute-start(bf16[128,1024]{1,0:T(8,128)(2,1)S(1)} %get-tuple-element.10), channel_id=1, source_target_pairs={{0,6},{2,4},{4,2},{6,0},{1,7},{3,5},{5,3},{7,1},{8,14},{10,12},{12... | collective-permute-start | bytes 786440 | tf_op jit(solution)/shard_map/ppermute | solution.py:244
  40.3 1.3 %copy-start.14 = (bf16[128,1024]{1,0:T(8,128)(2,1)}, bf16[128,1024]{1,0:T(8,128)(2,1)S(1)}, u32[]{:S(2)}) copy-start(bf16[128,1024]{1,0:T(8,128)(2,1)S(1)} %collective-permute-done.3.refs_1_) | copy-start | bytes 786436
  41.6 0.7 %copy-start.15 = (bf16[128,1024]{1,0:T(8,128)(2,1)}, bf16[128,1024]{1,0:T(8,128)(2,1)S(1)}, u32[]{:S(2)}) copy-start(bf16[128,1024]{1,0:T(8,128)(2,1)S(1)} %collective-permute-done.4.refs_2_) | copy-start | bytes 786436
  41.6 0.8 %copy-start.16 = (bf16[128,1024]{1,0:T(8,128)(2,1)}, bf16[128,1024]{1,0:T(8,128)(2,1)S(1)}, u32[]{:S(2)}) copy-start(bf16[128,1024]{1,0:T(8,128)(2,1)S(1)} %collective-permute-done.5.refs_3_) | copy-start | bytes 786436

commit v3 on v2

--- a/solution.py
+++ b/solution.py
@@ -141,49 +141,82 @@
     return dot(high, high_ref[...]) + dot(low, high_ref[...]) + dot(high, low_ref[...])
 
 
-def spectrum_kernel(taps_ref, ahead_high, ahead_low, twiddle_ref, spec_ref, work_ref, *, outer):
+def put(work_ref, at, row, re, im):
+    rows = pl.ds(at * TILE + row, HALF_TILE)
+    work_ref[rows, 0:LANES] = re
+    work_ref[rows, LANES : 2 * LANES] = im
+
+
+def spectrum_kernel(me_ref, taps_ref, ahead_high, ahead_low, twiddle_ref, *refs, outer, parts, pencil):
+    *moved, spec_ref = refs[:-6]
+    taps_here, high_here, low_here, twiddle_here, work_ref, sems = refs[-6:]
     count = outer // 2
-
-    def load(n, row):
-        return taps_ref[row : row + HALF_TILE, n * LANES : (n + 1) * LANES]
-
-    def store(at, row, re, im):
-        rows = pl.ds(at * TILE + row, HALF_TILE)
-        work_ref[rows, 0:LANES] = re
-        work_ref[rows, LANES : 2 * LANES] = im
-
-    for half in range(2):
-        outer_forward(load, store, twiddle_ref, outer, half)
-    for half in range(2):
-        rows = pl.ds(half * count * TILE, count * TILE)
-        spec_ref[0, rows, :] = matmul(work_ref[rows, :], ahead_high, ahead_low)
-
-
-def correlate(piece_refs, me, mate_ref, keep_ref, signal_is_grad, tables, fill_ref, work_ref, out_ref, outer):
+    steps = taps_ref.shape[0] // TILE
+
+    def fetch(step):
+        rows = pl.ds(step * TILE, TILE)
+        return pltpu.make_async_copy(taps_ref.at[rows, :], taps_here.at[rows, :], sems.at[step])
+
+    copies = [
+        pltpu.make_async_copy(ahead_high, high_here, sems.at[steps]),
+        pltpu.make_async_copy(ahead_low, low_here, sems.at[steps + 1]),
+        pltpu.make_async_copy(twiddle_ref, twiddle_here, sems.at[steps + 2]),
+    ]
+    later = []
+    if moved:
+        input_ref, grad_ref, *slices, own_grad = moved
+        moves = [(input_ref, k, ref) for k, ref in enumerate(slices)] + [(grad_ref, 0, own_grad)]
+        for at, (source, k, ref) in enumerate(moves):
+            rows = pl.ds((me_ref[0] ^ k) * pencil, pencil)
+            later.append(pltpu.make_async_copy(source.at[rows, :], ref, sems.at[steps + 3 + at]))
+    fetch(0).start()
+    for copy in reversed(copies):
+        copy.start()
+    for step in range(1, steps):
+        fetch(step).start()
+    for copy in later:
+        copy.start()
+    for copy in copies:
+        copy.wait()
+
+    @pl.loop(0, steps)
+    def _(step):
+        fetch(step).wait()
+
+        def load(n, row):
+            return taps_here[pl.ds(pl.multiple_of(step * TILE + row, HALF_TILE), HALF_TILE), n * LANES : (n + 1) * LANES]
+
+        for half in range(2):
+            outer_forward(load, functools.partial(put, work_ref), twiddle_here, outer, half)
+        for half in range(2):
+            rows = pl.ds(half * count * TILE, count * TILE)
+            spec_ref[step, rows, :] = matmul(work_ref[rows, :], high_here, low_here)
+
+    for copy in later:
+        copy.wait()
+
+
+def correlate(step, piece_refs, me, mate_ref, keep_ref, signal_is_grad, tables, fill_ref, work_ref, out_ref, outer):
     ahead_high, ahead_low, back_high, back_low, twiddle_ref = tables
     count = outer // 2
     per_piece = outer // len(piece_refs)
+    rows = pl.ds(pl.multiple_of(step * TILE, TILE), TILE)
     for k, ref in enumerate(piece_refs):
         first = (me ^ k) * per_piece
         for i in range(per_piece):
-            fill_ref[first + i] = ref[:, i * LANES : (i + 1) * LANES].astype(jnp.float32)
+            fill_ref[first + i] = ref[rows, i * LANES : (i + 1) * LANES].astype(jnp.float32)
 
     def load(n, row):
         return fill_ref[n, row : row + HALF_TILE, :]
 
-    def store(at, row, re, im):
-        rows = pl.ds(at * TILE + row, HALF_TILE)
-        work_ref[rows, 0:LANES] = re
-        work_ref[rows, LANES : 2 * LANES] = im
-
     for half in range(2):
-        outer_forward(load, store, twiddle_ref, outer, half)
+        outer_forward(load, functools.partial(put, work_ref), twiddle_ref, outer, half)
     for half in range(2):
         rows = pl.ds(half * count * TILE, count * TILE)
         own = matmul(work_ref[rows, :], ahead_high, ahead_low)
         if keep_ref is not None:
-            keep_ref[0, rows, :] = own
-        mate = mate_ref[0, rows, :]
+            keep_ref[step, rows, :] = own
+        mate = mate_ref[step, rows, :]
         grad, other = (own, mate) if signal_is_grad else (mate, own)
         grad_re, grad_im = grad[:, :LANES], grad[:, LANES:]
         other_re, other_im = other[:, :LANES], other[:, LANES:]
@@ -200,27 +233,46 @@
     keep_ref, *sends = refs[parts + 6 : 2 * parts + 7]
     fill_ref, work_ref, out_ref = refs[2 * parts + 7 :]
     me = me_ref[0]
-    correlate(pieces, me, mate_ref, keep_ref, True, tables, fill_ref, work_ref, out_ref, outer)
     per_piece = outer // parts
-    for k, ref in enumerate(sends):
-        first = (me ^ k) * per_piece
-        for i in range(per_piece):
-            ref[:, i * LANES : (i + 1) * LANES] = out_ref[first + i].astype(jnp.bfloat16)
+
+    @pl.loop(0, pieces[0].shape[0] // TILE)
+    def _(step):
+        correlate(step, pieces, me, mate_ref, keep_ref, True, tables, fill_ref, work_ref, out_ref, outer)
+        rows = pl.ds(pl.multiple_of(step * TILE, TILE), TILE)
+        for k, ref in enumerate(sends):
+            first = (me ^ k) * per_piece
+            for i in range(per_piece):
+                ref[rows, i * LANES : (i + 1) * LANES] = out_ref[first + i].astype(jnp.bfloat16)
 
 
 def filter_kernel(me_ref, *refs, outer, parts):
     pieces, (mate_ref, *tables) = refs[:parts], refs[parts : parts + 6]
-    result_ref, fill_ref, work_ref, out_ref = refs[parts + 6 :]
-    correlate(pieces, me_ref[0], mate_ref, None, False, tables, fill_ref, work_ref, out_ref, outer)
-    for n in range(outer):
-        result_ref[:, n * LANES : (n + 1) * LANES] = out_ref[n]
-
-
-def gather_kernel(me_ref, *refs, pencil):
+    result_ref, fill_ref, work_ref, out_ref, result_here, sems = refs[parts + 6 :]
+    steps = pieces[0].shape[0] // TILE
+
+    def flush(step):
+        rows = pl.ds(pl.multiple_of(step * TILE, TILE), TILE)
+        return pltpu.make_async_copy(result_here.at[rows, :], result_ref.at[rows, :], sems.at[step])
+
+    @pl.loop(0, steps)
+    def _(step):
+        correlate(step, pieces, me_ref[0], mate_ref, None, False, tables, fill_ref, work_ref, out_ref, outer)
+        rows = pl.ds(pl.multiple_of(step * TILE, TILE), TILE)
+        for n in range(outer):
+            result_here[rows, n * LANES : (n + 1) * LANES] = out_ref[n]
+        flush(step).start()
+
+    @pl.loop(0, steps)
+    def _(step):
+        flush(step).wait()
+
+
+def gather_kernel(*refs, pencil):
     *pieces, out_ref, sems = refs
+    me = lax.axis_index("ctx")
     copies = []
     for k, ref in enumerate(pieces):
-        rows = pl.ds((me_ref[0] ^ k) * pencil, pencil)
+        rows = pl.ds((me ^ k) * pencil, pencil)
         copies.append(pltpu.make_async_copy(ref, out_ref.at[rows, :], sems.at[k]))
     for copy in copies:
         copy.start()
@@ -239,6 +291,7 @@
     steps = rows // TILE
     ahead, back, back_scaled, twiddle = dft_tables(length)
     me_array = me.astype(jnp.int32).reshape(1)
+    others = sorted(range(1, parts), reverse=True)
 
     def swap(block, k):
         return lax.ppermute(block, "ctx", [(i, i ^ k) for i in range(parts)])
@@ -250,83 +303,95 @@
     def pad(block):
         return block if aligned else jnp.pad(block, ((0, rows - pencil), (0, 0)))
 
-    whole = lambda array: pl.BlockSpec(array.shape, lambda s, *_: (0,) * array.ndim)
-    piece_spec = pl.BlockSpec((TILE, piece), lambda s, *_: (s, 0))
-    own_spec = pl.BlockSpec((TILE, piece), lambda s, at: (at[0] * steps + s, 0)) if aligned else piece_spec
-    full_spec = pl.BlockSpec((TILE, length), lambda s, *_: (s, 0))
-    spec_spec = pl.BlockSpec((1, outer * TILE, 2 * LANES), lambda s, *_: (s, 0, 0))
+    scalar = pl.BlockSpec(memory_space=pltpu.SMEM)
+    here = pl.BlockSpec(memory_space=pltpu.VMEM)
+    there = pl.BlockSpec(memory_space=pl.ANY)
     spec_shape = jax.ShapeDtypeStruct((steps, outer * TILE, 2 * LANES), jnp.float32)
+    slice_shape = jax.ShapeDtypeStruct((rows, piece), jnp.bfloat16)
     work = pltpu.VMEM((outer * TILE, 2 * LANES), jnp.float32)
     lane_tiles = pltpu.VMEM((outer, TILE, LANES), jnp.float32)
-    params = pltpu.CompilerParams(vmem_limit_bytes=32 * 1024 * 1024)
+    params = pltpu.CompilerParams(vmem_limit_bytes=16 * 1024 * 1024)
     stage_flops = 2 * 3 * rows * outer * (2 * LANES) ** 2
     spec_bytes = 4 * rows * length * 2
 
     def cost(stages, moved):
         return pl.CostEstimate(flops=stages * stage_flops, bytes_accessed=moved, transcendentals=0)
 
-    def own_of(array):
-        return array if aligned else pad(pick(array, 0))
-
-    grad_pieces = [swap(pick(grad_output, k), k) for k in range(1, parts)]
-    input_pieces = [swap(pick(layer_input, k), k) for k in range(1, parts)]
-
-    taps = pad(filter_taps.reshape(pencil, length))
-    taps_spectrum = pl.pallas_call(
-        functools.partial(spectrum_kernel, outer=outer),
-        grid=(steps,),
-        in_specs=[full_spec, whole(ahead[0]), whole(ahead[1]), whole(twiddle)],
-        out_specs=spec_spec,
-        out_shape=spec_shape,
-        scratch_shapes=[work],
+    def in_hbm(array):
+        return pltpu.with_memory_space_constraint(array, pltpu.HBM)
+
+    grad_pieces = [None] * parts
+    for k in others:
+        grad_pieces[k] = swap(pick(grad_output, k), k)
+
+    taps = filter_taps.reshape(pencil, length)
+    tables = [*ahead, twiddle]
+    slices = parts + 1 if aligned else 0
+    results = pl.pallas_call(
+        functools.partial(spectrum_kernel, outer=outer, parts=parts, pencil=pencil),
+        in_specs=[scalar] + [there] * (6 if aligned else 4),
+        out_specs=[here] * (slices + 1),
+        out_shape=[slice_shape] * slices + [spec_shape],
+        scratch_shapes=[
+            pltpu.VMEM((rows, length), jnp.float32),
+            *[pltpu.VMEM(table.shape, table.dtype) for table in tables],
+            work,
+            pltpu.SemaphoreType.DMA((steps + 3 + slices,)),
+        ],
         compiler_params=params,
         cost_estimate=cost(1, 2 * spec_bytes),
         name="taps_spectrum",
-    )(taps, *ahead, twiddle)
+    )(me_array, in_hbm(pad(taps)), *map(in_hbm, map(jnp.asarray, tables)), *map(in_hbm, [layer_input, grad_output] if aligned else []))
+    taps_spectrum = results[-1]
+    blocks = results[:parts] if aligned else [pick(layer_input, k) for k in range(parts)]
+    grad_pieces[0] = results[parts] if aligned else pick(grad_output, 0)
+    input_pieces = [blocks[0]] + [None] * (parts - 1)
+    for k in others:
+        input_pieces[k] = swap(blocks[k], k)
 
     tables = [*ahead, *back, twiddle]
     grad_spectrum, *outgoing = pl.pallas_call(
         functools.partial(input_kernel, outer=outer, parts=parts),
-        grid_spec=pltpu.PrefetchScalarGridSpec(
-            num_scalar_prefetch=1,
-            grid=(steps,),
-            in_specs=[own_spec, *[piece_spec] * (parts - 1), spec_spec, *map(whole, tables)],
-            out_specs=[spec_spec, *[piece_spec] * parts],
-            scratch_shapes=[lane_tiles, work, lane_tiles],
-        ),
-        out_shape=[spec_shape, *[jax.ShapeDtypeStruct((rows, piece), jnp.bfloat16)] * parts],
+        in_specs=[scalar] + [here] * (parts + 1 + len(tables)),
+        out_specs=[here] * (parts + 1),
+        out_shape=[spec_shape, *[slice_shape] * parts],
+        scratch_shapes=[lane_tiles, work, lane_tiles],
         compiler_params=params,
         cost_estimate=cost(2, 2 * spec_bytes),
         name="grad_input",
-    )(me_array, own_of(grad_output), *map(pad, grad_pieces), taps_spectrum, *tables)
-
-    incoming = [outgoing[0][:pencil]] + [swap(outgoing[k][:pencil], k) for k in range(1, parts)]
+    )(me_array, *map(pad, grad_pieces), taps_spectrum, *tables)
+
+    incoming = [outgoing[0][:pencil]] + [None] * (parts - 1)
+    for k in others:
+        incoming[k] = swap(outgoing[k][:pencil], k)
 
     tables = [*ahead, *back_scaled, twiddle]
     grad_filter = pl.pallas_call(
         functools.partial(filter_kernel, outer=outer, parts=parts),
-        grid_spec=pltpu.PrefetchScalarGridSpec(
-            num_scalar_prefetch=1,
-            grid=(steps,),
-            in_specs=[own_spec, *[piece_spec] * (parts - 1), spec_spec, *map(whole, tables)],
-            out_specs=full_spec,
-            scratch_shapes=[lane_tiles, work, lane_tiles],
-        ),
+        in_specs=[scalar] + [here] * (parts + 1 + len(tables)),
+        out_specs=there,
         out_shape=jax.ShapeDtypeStruct((rows, length), jnp.float32),
+        scratch_shapes=[
+            lane_tiles,
+            work,
+            lane_tiles,
+            pltpu.VMEM((rows, length), jnp.float32),
+            pltpu.SemaphoreType.DMA((steps,)),
+        ],
         compiler_params=params,
         cost_estimate=cost(2, 2 * spec_bytes),
         name="grad_filter",
-    )(me_array, own_of(layer_input), *map(pad, input_pieces), grad_spectrum, *tables)
+    )(me_array, *map(pad, input_pieces), grad_spectrum, *tables)
 
     if aligned:
         grad_input = pl.pallas_call(
             functools.partial(gather_kernel, pencil=pencil),
-            in_specs=[pl.BlockSpec(memory_space=pltpu.SMEM), *[pl.BlockSpec(memory_space=pltpu.VMEM)] * parts],
-            out_specs=pl.BlockSpec(memory_space=pl.ANY),
+            in_specs=[there] * parts,
+            out_specs=there,
             out_shape=jax.ShapeDtypeStruct((parts * pencil, piece), jnp.bfloat16),
             scratch_shapes=[pltpu.SemaphoreType.DMA((parts,))],
             name="gather_pieces",
-        )(me_array, *incoming)
+        )(*[pltpu.with_memory_space_constraint(block, pltpu.VMEM) for block in incoming])
     else:
         slots = jnp.zeros((parts, pencil, piece), jnp.bfloat16)
         for k, block in enumerate(incoming):

time: 44.9 us -> 42.3 us (0.942)
  local copies, waits for them, and re-layouts: 7.36 us -> 1.32 us
  waiting for transfers between devices: 1.4 us -> 4.93 us
    unnamed x34 -> x14, local copies, waits for them, and re-layouts: 5.03 us -> 0.05 us
    ppermute x9, waiting for transfers between devices: 1.4 us -> 4.93 us  [swap(): return lax.ppermute(block, 'ctx', [(i, i ^ k) for i in range(parts)])]
    pallas_call x1, Pallas kernels: 4.29 us -> 5.52 us  [shards(): pl.pallas_call(functools.partial(spectrum_kernel, outer=outer, parts=part...]
    pallas_call x1, Pallas kernels: 2.18 us -> 1 us  [shards(): pl.pallas_call(functools.partial(gather_kernel, pencil=pencil), in_specs=...]
    squeeze x2 -> x1, local copies, waits for them, and re-layouts: 2.33 us -> 1.27 us  [pick(): return lax.dynamic_index_in_dim(blocks, me ^ k, 0, keepdims=False)]
  transfers between devices with their start and end apart: 9 -> 9, of which waited for: 2 -> 3; matrix products, arithmetic and copies ran while one was open for 3% -> 0% of each run, Pallas kernels for 47% -> 52%
where the time goes in v3:
time: 42.3 us; the launch traced here: 42.2 us
  Pallas kernels  23.1 us (55%)
  starting transfers between devices  12.1 us (29%)
  waiting for transfers between devices  4.93 us (12%)
  local copies, waits for them, and re-layouts  1.32 us (3%)
  between operations  0.78 us (2%)
    ppermute x9, starting transfers between devices, swap(): return lax.ppermute(block, 'ctx', [(i, i ^ k) for i in range(parts)])  12.1 us
    pallas_call x1, Pallas kernels, shards(): pl.pallas_call(functools.partial(filter_kernel, outer=outer, parts=parts)...  8.65 us
    pallas_call x1, Pallas kernels, shards(): pl.pallas_call(functools.partial(input_kernel, outer=outer, parts=parts),...  7.93 us
    pallas_call x1, Pallas kernels, shards(): pl.pallas_call(functools.partial(spectrum_kernel, outer=outer, parts=part...  5.52 us
    ppermute x9, waiting for transfers between devices, swap(): return lax.ppermute(block, 'ctx', [(i, i ^ k) for i in range(parts)])  4.93 us
    squeeze x1, local copies, waits for them, and re-layouts, pick(): return lax.dynamic_index_in_dim(blocks, me ^ k, 0, keepdims=False)  1.27 us
    pallas_call x1, Pallas kernels, shards(): pl.pallas_call(functools.partial(gather_kernel, pencil=pencil), in_specs=...  1 us
  transfers between devices with their start and end apart: 9, of which 3 were waited for; matrix products, arithmetic and copies ran while one was open for 0% of the time, Pallas kernels for 52%

profile of v3, /device:TPU:0, one launch (start us, length us, event | category | flops | bytes accessed | tf_op | source)
XLA Modules:
  0.0 42.2 jit_solution(2856000473245207288)
XLA Ops:
  0.6 0.0 copy-start.6
  0.6 0.0 copy-start
  0.7 0.0 copy-start.1
  0.7 0.0 copy-start.4
  0.7 0.0 copy-start.5
  0.7 1.3 %dynamic-slice_bitcast_fusion = (bf16[128,1024]{1,0:T(8,128)(2,1)S(1)}, bf16[128,1024]{1,0:T(8,128)(2,1)S(1)}, bf16[128,1024]{1,0:T(8,128)(2,1)S(1)}) fusion(bf16[4,128,1024]{2,1,0:T(8,128)(2,1)} %bitcast.10, s32[]{:T(128)S(6)} %select_n.12, s32[]{:T(128)S(6)} %select_n.11, s32[]{:T(128)S(6)} %select_n.10), kind=kLoop, calls=%fused_computation | loop fusion | bytes 1572876 | tf_op jit(solution)/shard_map/jit(dynamic_index_in_dim)/squeeze | solution.py:301
  2.0 4.0 %collective-permute-start.2 = (bf16[128,1024]{1,0:T(8,128)(2,1)S(1)}, bf16[128,1024]{1,0:T(8,128)(2,1)S(1)}, u32[]{:S(2)}, u32[]{:S(2)}) collective-permute-start(bf16[128,1024]{1,0:T(8,128)(2,1)S(1)} %get-tuple-element.24), channel_id=1, source_target_pairs={{0,6},{2,4},{4,2},{6,0},{1,7},{3,5},{5,3},{7,1},{8,14},{10,12},{12... | collective-permute-start | bytes 786440 | tf_op jit(solution)/shard_map/ppermute | solution.py:297
  5.9 0.5 %collective-permute-start.1 = (bf16[128,1024]{1,0:T(8,128)(2,1)S(1)}, bf16[128,1024]{1,0:T(8,128)(2,1)S(1)}, u32[]{:S(2)}, u32[]{:S(2)}) collective-permute-start(bf16[128,1024]{1,0:T(8,128)(2,1)S(1)} %get-tuple-element.25), channel_id=1, source_target_pairs={{0,4},{2,6},{4,0},{6,2},{1,5},{3,7},{5,1},{7,3},{8,12},{10,14},{12... | collective-permute-start | bytes 786440 | tf_op jit(solution)/shard_map/ppermute | solution.py:297
  6.5 0.1 collective-permute-start
  6.6 5.5 %taps_spectrum.1 = (bf16[128,1024]{1,0:T(8,128)(2,1)S(1)}, bf16[128,1024]{1,0:T(8,128)(2,1)S(1)}, bf16[128,1024]{1,0:T(8,128)(2,1)S(1)}, bf16[128,1024]{1,0:T(8,...) custom-call(s32[1]{0:T(128)} %bitcast.me_ref, f32[128,4096]{1,0:T(8,128)} %bitcast.11, ...), custom_call_target="tpu_custom_call" | custom-call | flops 1610612736 | bytes 8388608 | tf_op jit(solution)/shard_map/taps_spectrum/pallas_call | solution.py:330
  12.1 2.0 %collective-permute-start.6 = (bf16[128,1024]{1,0:T(8,128)(2,1)S(1)}, bf16[128,1024]{1,0:T(8,128)(2,1)S(1)}, u32[]{:S(2)}, u32[]{:S(2)}) collective-permute-start(bf16[128,1024]{1,0:T(8,128)(2,1)S(1)} %get-tuple-element.20), channel_id=1, source_target_pairs={{0,2},{2,0},{4,6},{6,4},{1,3},{3,1},{5,7},{7,5},{8,10},{10,8},{12,... | collective-permute-start | bytes 786440 | tf_op jit(solution)/shard_map/ppermute | solution.py:297
  14.1 1.5 %collective-permute-start.7 = (bf16[128,1024]{1,0:T(8,128)(2,1)S(1)}, bf16[128,1024]{1,0:T(8,128)(2,1)S(1)}, u32[]{:S(2)}, u32[]{:S(2)}) collective-permute-start(bf16[128,1024]{1,0:T(8,128)(2,1)S(1)} %get-tuple-element.21), channel_id=1, source_target_pairs={{0,4},{2,6},{4,0},{6,2},{1,5},{3,7},{5,1},{7,3},{8,12},{10,14},{12... | collective-permute-start | bytes 786440 | tf_op jit(solution)/shard_map/ppermute | solution.py:297
  15.6 0.0 collective-permute-done.2.refs_3_
  15.6 0.4 %collective-permute-start.8 = (bf16[128,1024]{1,0:T(8,128)(2,1)S(1)}, bf16[128,1024]{1,0:T(8,128)(2,1)S(1)}, u32[]{:S(2)}, u32[]{:S(2)}) collective-permute-start(bf16[128,1024]{1,0:T(8,128)(2,1)S(1)} %get-tuple-element.22), channel_id=1, source_target_pairs={{0,6},{2,4},{4,2},{6,0},{1,7},{3,5},{5,3},{7,1},{8,14},{10,12},{12... | collective-permute-start | bytes 786440 | tf_op jit(solution)/shard_map/ppermute | solution.py:297
  16.0 1.9 %collective-permute-done.1.refs_2_ = bf16[128,1024]{1,0:T(8,128)(2,1)S(1)} collective-permute-done((bf16[128,1024]{1,0:T(8,128)(2,1)S(1)}, bf16[128,1024]{1,0:T(8,128)(2,1)S(1)}, u32[]{:S(2)}, u32[]{:S(2)}) %collective-permute-start.1) | collective-permute-done | bytes 262176 | tf_op jit(solution)/shard_map/ppermute | solution.py:297
  18.0 1.3 %collective-permute-done.refs_1_ = bf16[128,1024]{1,0:T(8,128)(2,1)S(1)} collective-permute-done((bf16[128,1024]{1,0:T(8,128)(2,1)S(1)}, bf16[128,1024]{1,0:T(8,128)(2,1)S(1)}, u32[]{:S(2)}, u32[]{:S(2)}) %collective-permute-start) | collective-permute-done | bytes 262176 | tf_op jit(solution)/shard_map/ppermute | solution.py:297
  19.3 0.0 copy-done.6
  19.3 0.0 copy-done
  19.3 0.0 copy-done.1
  19.3 0.0 copy-done.4
  19.3 0.0 copy-done.5
  19.3 0.0 copy-start.2
  19.4 0.0 copy-start.3
  19.4 7.9 %grad_input.1 = (f32[8,512,256]{2,1,0:T(8,128)S(1)}, bf16[128,1024]{1,0:T(8,128)(2,1)S(1)}, bf16[128,1024]{1,0:T(8,128)(2,1)S(1)}, bf16[128,1024]{1,0:T(8,128)(2,1)S(1)}, bf16[128,1024]{1,0:T(8,128)(2,1)S(1)}) custom-call(s32[1]{0:T(128)} %bitcast.me_ref, bf16[128,1024]{1,0:T(8,128)(2,1)S(1)} %get-tuple-element.13.refs_0_, ...), custom_call_target="tpu_custom_call" | custom-call | flops 3221225472 | bytes 8388608 | tf_op jit(solution)/shard_map/grad_input/pallas_call | solution.py:353
  27.3 1.5 %collective-permute-start.3 = (bf16[128,1024]{1,0:T(8,128)(2,1)S(1)}, bf16[128,1024]{1,0:T(8,128)(2,1)S(1)}, u32[]{:S(2)}, u32[]{:S(2)}) collective-permute-start(bf16[128,1024]{1,0:T(8,128)(2,1)S(1)} %get-tuple-element.16), channel_id=1, source_target_pairs={{0,2},{2,0},{4,6},{6,4},{1,3},{3,1},{5,7},{7,5},{8,10},{10,8},{12,... | collective-permute-start | bytes 786440 | tf_op jit(solution)/shard_map/ppermute | solution.py:297
  28.8 0.6 %collective-permute-start.4 = (bf16[128,1024]{1,0:T(8,128)(2,1)S(1)}, bf16[128,1024]{1,0:T(8,128)(2,1)S(1)}, u32[]{:S(2)}, u32[]{:S(2)}) collective-permute-start(bf16[128,1024]{1,0:T(8,128)(2,1)S(1)} %get-tuple-element.17), channel_id=1, source_target_pairs={{0,4},{2,6},{4,0},{6,2},{1,5},{3,7},{5,1},{7,3},{8,12},{10,14},{12... | collective-permute-start | bytes 786440 | tf_op jit(solution)/shard_map/ppermute | solution.py:297
  29.4 0.0 collective-permute-done.6.refs_1_
  29.4 1.5 %collective-permute-start.5 = (bf16[128,1024]{1,0:T(8,128)(2,1)S(1)}, bf16[128,1024]{1,0:T(8,128)(2,1)S(1)}, u32[]{:S(2)}, u32[]{:S(2)}) collective-permute-start(bf16[128,1024]{1,0:T(8,128)(2,1)S(1)} %get-tuple-element.18), channel_id=1, source_target_pairs={{0,6},{2,4},{4,2},{6,0},{1,7},{3,5},{5,3},{7,1},{8,14},{10,12},{12... | collective-permute-start | bytes 786440 | tf_op jit(solution)/shard_map/ppermute | solution.py:297
  30.9 0.0 collective-permute-done.7.refs_2_
  30.9 0.0 collective-permute-done.8.refs_3_
  30.9 0.0 copy-done.2
  30.9 0.0 copy-done.3
  30.9 8.6 %grad_filter.1 = f32[128,4096]{1,0:T(8,128)} custom-call(s32[1]{0:T(128)} %bitcast.me_ref, bf16[128,1024]{1,0:T(8,128)(2,1)S(1)} %get-tuple-element.19.refs_0_, bf16[128,1024]{1,0:T(8,128)(2,1)S(1)} %collective-permute-done.6.refs_1_, bf16[128,1024]{1,0:T(8,128)(2,1)S(1)} %collective-permute-done.7.refs_2_, ...), custom_call_target="tpu_custom_call" | custom-call | flops 3221225472 | bytes 8388608 | tf_op jit(solution)/shard_map/grad_filter/pallas_call | solution.py:369
  39.5 0.0 collective-permute-done.3.refs_1_
  39.5 1.6 %collective-permute-done.4.refs_2_ = bf16[128,1024]{1,0:T(8,128)(2,1)S(1)} collective-permute-done((bf16[128,1024]{1,0:T(8,128)(2,1)S(1)}, bf16[128,1024]{1,0:T(8,128)(2,1)S(1)}, u32[]{:S(2)}, u32[]{:S(2)}) %collective-permute-start.4) | collective-permute-done | bytes 262176 | tf_op jit(solution)/shard_map/ppermute | solution.py:297
  41.2 0.0 collective-permute-done.5.refs_3_
  41.2 1.0 %gather_pieces.1 = bf16[512,1024]{1,0:T(8,128)(2,1)} custom-call(bf16[128,1024]{1,0:T(8,128)(2,1)S(1)} %get-tuple-element.15.refs_0_, bf16[128,1024]{1,0:T(8,128)(2,1)S(1)} %collective-permute-done.3.refs_1_, bf16[128,1024]{1,0:T(8,128)(2,1)S(1)} %collective-permute-done.4.refs_2_, bf16[128,1024]{1,0:T(8,128)(2,1)S(1)} %collective-permute-done.5.refs_3_), custom_call_target="tpu_custom_call" | custom-call | tf_op jit(solution)/shard_map/gather_pieces/pallas_call | solution.py:387
Async XLA Ops:
  0.6 18.7 %copy-start.6 = (f32[32,2,128]{2,1,0:T(2,128)S(1)}, f32[32,2,128]{2,1,0:T(2,128)}, u32[]{:S(2)}) copy-start(f32[32,2,128]{2,1,0:T(2,128)} %constant.38.clone.twiddle_ref.refs_9_) | copy-start | bytes 98308
  0.6 18.7 %copy-start = (bf16[256,256]{1,0:T(8,128)(2,1)S(1)}, bf16[256,256]{1,0:T(8,128)(2,1)}, u32[]{:S(2)}) copy-start(bf16[256,256]{1,0:T(8,128)(2,1)} %constant.37.clone.ahead_low.refs_6_) | copy-start | bytes 393220
  0.7 18.7 %copy-start.1 = (bf16[256,256]{1,0:T(8,128)(2,1)S(1)}, bf16[256,256]{1,0:T(8,128)(2,1)}, u32[]{:S(2)}) copy-start(bf16[256,256]{1,0:T(8,128)(2,1)} %constant.36.clone.ahead_high.refs_5_) | copy-start | bytes 393220
  0.7 18.7 %copy-start.4 = (bf16[256,256]{1,0:T(8,128)(2,1)S(1)}, bf16[256,256]{1,0:T(8,128)(2,1)}, u32[]{:S(2)}) copy-start(bf16[256,256]{1,0:T(8,128)(2,1)} %constant.40.clone.refs_8_) | copy-start | bytes 393220
  0.7 18.7 %copy-start.5 = (bf16[256,256]{1,0:T(8,128)(2,1)S(1)}, bf16[256,256]{1,0:T(8,128)(2,1)}, u32[]{:S(2)}) copy-start(bf16[256,256]{1,0:T(8,128)(2,1)} %constant.39.clone.refs_7_) | copy-start | bytes 393220
  2.0 13.6 %collective-permute-start.2 = (bf16[128,1024]{1,0:T(8,128)(2,1)S(1)}, bf16[128,1024]{1,0:T(8,128)(2,1)S(1)}, u32[]{:S(2)}, u32[]{:S(2)}) collective-permute-start(bf16[128,1024]{1,0:T(8,128)(2,1)S(1)} %get-tuple-element.24), channel_id=1, source_target_pairs={{0,6},{2,4},{4,2},{6,0},{1,7},{3,5},{5,3},{7,1},{8,14},{10,12},{12... | collective-permute-start | bytes 786440 | tf_op jit(solution)/shard_map/ppermute | solution.py:297
  5.9 12.0 %collective-permute-start.1 = (bf16[128,1024]{1,0:T(8,128)(2,1)S(1)}, bf16[128,1024]{1,0:T(8,128)(2,1)S(1)}, u32[]{:S(2)}, u32[]{:S(2)}) collective-permute-start(bf16[128,1024]{1,0:T(8,128)(2,1)S(1)} %get-tuple-element.25), channel_id=1, source_target_pairs={{0,4},{2,6},{4,0},{6,2},{1,5},{3,7},{5,1},{7,3},{8,12},{10,14},{12... | collective-permute-start | bytes 786440 | tf_op jit(solution)/shard_map/ppermute | solution.py:297
  6.5 12.9 %collective-permute-start = (bf16[128,1024]{1,0:T(8,128)(2,1)S(1)}, bf16[128,1024]{1,0:T(8,128)(2,1)S(1)}, u32[]{:S(2)}, u32[]{:S(2)}) collective-permute-start(bf16[128,1024]{1,0:T(8,128)(2,1)S(1)} %get-tuple-element.26), channel_id=1, source_target_pairs={{0,2},{2,0},{4,6},{6,4},{1,3},{3,1},{5,7},{7,5},{8,10},{10,8},{12,... | collective-permute-start | bytes 786440 | tf_op jit(solution)/shard_map/ppermute | solution.py:297
  12.1 17.3 %collective-permute-start.6 = (bf16[128,1024]{1,0:T(8,128)(2,1)S(1)}, bf16[128,1024]{1,0:T(8,128)(2,1)S(1)}, u32[]{:S(2)}, u32[]{:S(2)}) collective-permute-start(bf16[128,1024]{1,0:T(8,128)(2,1)S(1)} %get-tuple-element.20), channel_id=1, source_target_pairs={{0,2},{2,0},{4,6},{6,4},{1,3},{3,1},{5,7},{7,5},{8,10},{10,8},{12,... | collective-permute-start | bytes 786440 | tf_op jit(solution)/shard_map/ppermute | solution.py:297
  14.1 16.8 %collective-permute-start.7 = (bf16[128,1024]{1,0:T(8,128)(2,1)S(1)}, bf16[128,1024]{1,0:T(8,128)(2,1)S(1)}, u32[]{:S(2)}, u32[]{:S(2)}) collective-permute-start(bf16[128,1024]{1,0:T(8,128)(2,1)S(1)} %get-tuple-element.21), channel_id=1, source_target_pairs={{0,4},{2,6},{4,0},{6,2},{1,5},{3,7},{5,1},{7,3},{8,12},{10,14},{12... | collective-permute-start | bytes 786440 | tf_op jit(solution)/shard_map/ppermute | solution.py:297
  15.6 15.3 %collective-permute-start.8 = (bf16[128,1024]{1,0:T(8,128)(2,1)S(1)}, bf16[128,1024]{1,0:T(8,128)(2,1)S(1)}, u32[]{:S(2)}, u32[]{:S(2)}) collective-permute-start(bf16[128,1024]{1,0:T(8,128)(2,1)S(1)} %get-tuple-element.22), channel_id=1, source_target_pairs={{0,6},{2,4},{4,2},{6,0},{1,7},{3,5},{5,3},{7,1},{8,14},{10,12},{12... | collective-permute-start | bytes 786440 | tf_op jit(solution)/shard_map/ppermute | solution.py:297
  19.3 11.5 %copy-start.2 = (bf16[256,256]{1,0:T(8,128)(2,1)S(1)}, bf16[256,256]{1,0:T(8,128)(2,1)}, u32[]{:S(2)}) copy-start(bf16[256,256]{1,0:T(8,128)(2,1)} %constant.42.clone.refs_8_) | copy-start | bytes 393220
  19.4 11.5 %copy-start.3 = (bf16[256,256]{1,0:T(8,128)(2,1)S(1)}, bf16[256,256]{1,0:T(8,128)(2,1)}, u32[]{:S(2)}) copy-start(bf16[256,256]{1,0:T(8,128)(2,1)} %constant.41.clone.refs_7_) | copy-start | bytes 393220
  27.3 12.2 %collective-permute-start.3 = (bf16[128,1024]{1,0:T(8,128)(2,1)S(1)}, bf16[128,1024]{1,0:T(8,128)(2,1)S(1)}, u32[]{:S(2)}, u32[]{:S(2)}) collective-permute-start(bf16[128,1024]{1,0:T(8,128)(2,1)S(1)} %get-tuple-element.16), channel_id=1, source_target_pairs={{0,2},{2,0},{4,6},{6,4},{1,3},{3,1},{5,7},{7,5},{8,10},{10,8},{12,... | collective-permute-start | bytes 786440 | tf_op jit(solution)/shard_map/ppermute | solution.py:297
  28.8 12.4 %collective-permute-start.4 = (bf16[128,1024]{1,0:T(8,128)(2,1)S(1)}, bf16[128,1024]{1,0:T(8,128)(2,1)S(1)}, u32[]{:S(2)}, u32[]{:S(2)}) collective-permute-start(bf16[128,1024]{1,0:T(8,128)(2,1)S(1)} %get-tuple-element.17), channel_id=1, source_target_pairs={{0,4},{2,6},{4,0},{6,2},{1,5},{3,7},{5,1},{7,3},{8,12},{10,14},{12... | collective-permute-start | bytes 786440 | tf_op jit(solution)/shard_map/ppermute | solution.py:297
  29.4 11.8 %collective-permute-start.5 = (bf16[128,1024]{1,0:T(8,128)(2,1)S(1)}, bf16[128,1024]{1,0:T(8,128)(2,1)S(1)}, u32[]{:S(2)}, u32[]{:S(2)}) collective-permute-start(bf16[128,1024]{1,0:T(8,128)(2,1)S(1)} %get-tuple-element.18), channel_id=1, source_target_pairs={{0,6},{2,4},{4,2},{6,0},{1,7},{3,5},{5,3},{7,1},{8,14},{10,12},{12... | collective-permute-start | bytes 786440 | tf_op jit(solution)/shard_map/ppermute | solution.py:297

commit v4 on v3

--- a/solution.py
+++ b/solution.py
@@ -141,13 +141,23 @@
     return dot(high, high_ref[...]) + dot(low, high_ref[...]) + dot(high, low_ref[...])
 
 
+def order_of(what, parts):
+    near = list(range(1, parts))
+    return {"grad": near[-1:] + near[:-1], "input": near, "back": near[::-1]}[what]
+
+
+def places_of(what, parts):
+    me = lax.axis_index("ctx")
+    return [me ^ k for k in [0, *order_of(what, parts)]]
+
+
 def put(work_ref, at, row, re, im):
     rows = pl.ds(at * TILE + row, HALF_TILE)
     work_ref[rows, 0:LANES] = re
     work_ref[rows, LANES : 2 * LANES] = im
 
 
-def spectrum_kernel(me_ref, taps_ref, ahead_high, ahead_low, twiddle_ref, *refs, outer, parts, pencil):
+def spectrum_kernel(taps_ref, ahead_high, ahead_low, twiddle_ref, *refs, outer, parts, pencil):
     *moved, spec_ref = refs[:-6]
     taps_here, high_here, low_here, twiddle_here, work_ref, sems = refs[-6:]
     count = outer // 2
@@ -165,9 +175,10 @@
     later = []
     if moved:
         input_ref, grad_ref, *slices, own_grad = moved
-        moves = [(input_ref, k, ref) for k, ref in enumerate(slices)] + [(grad_ref, 0, own_grad)]
-        for at, (source, k, ref) in enumerate(moves):
-            rows = pl.ds((me_ref[0] ^ k) * pencil, pencil)
+        places = places_of("input", parts)
+        moves = [(input_ref, *move) for move in zip(places, slices)] + [(grad_ref, places[0], own_grad)]
+        for at, (source, place, ref) in enumerate(moves):
+            rows = pl.ds(place * pencil, pencil)
             later.append(pltpu.make_async_copy(source.at[rows, :], ref, sems.at[steps + 3 + at]))
     fetch(0).start()
     for copy in reversed(copies):
@@ -196,13 +207,13 @@
         copy.wait()
 
 
-def correlate(step, piece_refs, me, mate_ref, keep_ref, signal_is_grad, tables, fill_ref, work_ref, out_ref, outer):
+def correlate(step, piece_refs, places, mate_ref, keep_ref, signal_is_grad, tables, fill_ref, work_ref, out_ref, outer):
     ahead_high, ahead_low, back_high, back_low, twiddle_ref = tables
     count = outer // 2
     per_piece = outer // len(piece_refs)
     rows = pl.ds(pl.multiple_of(step * TILE, TILE), TILE)
-    for k, ref in enumerate(piece_refs):
-        first = (me ^ k) * per_piece
+    for place, ref in zip(places, piece_refs):
+        first = place * per_piece
         for i in range(per_piece):
             fill_ref[first + i] = ref[rows, i * LANES : (i + 1) * LANES].astype(jnp.float32)
 
@@ -228,26 +239,27 @@
         outer_inverse(work_ref, twiddle_ref, out_ref, outer, half)
 
 
-def input_kernel(me_ref, *refs, outer, parts):
+def input_kernel(*refs, outer, parts):
     pieces, (mate_ref, *tables) = refs[:parts], refs[parts : parts + 6]
     keep_ref, *sends = refs[parts + 6 : 2 * parts + 7]
     fill_ref, work_ref, out_ref = refs[2 * parts + 7 :]
-    me = me_ref[0]
+    places, send_places = places_of("grad", parts), places_of("back", parts)
     per_piece = outer // parts
 
     @pl.loop(0, pieces[0].shape[0] // TILE)
     def _(step):
-        correlate(step, pieces, me, mate_ref, keep_ref, True, tables, fill_ref, work_ref, out_ref, outer)
+        correlate(step, pieces, places, mate_ref, keep_ref, True, tables, fill_ref, work_ref, out_ref, outer)
         rows = pl.ds(pl.multiple_of(step * TILE, TILE), TILE)
-        for k, ref in enumerate(sends):
-            first = (me ^ k) * per_piece
+        for place, ref in zip(send_places, sends):
+            first = place * per_piece
             for i in range(per_piece):
                 ref[rows, i * LANES : (i + 1) * LANES] = out_ref[first + i].astype(jnp.bfloat16)
 
 
-def filter_kernel(me_ref, *refs, outer, parts):
+def filter_kernel(*refs, outer, parts):
     pieces, (mate_ref, *tables) = refs[:parts], refs[parts : parts + 6]
     result_ref, fill_ref, work_ref, out_ref, result_here, sems = refs[parts + 6 :]
+    places = places_of("input", parts)
     steps = pieces[0].shape[0] // TILE
 
     def flush(step):
@@ -256,7 +268,7 @@
 
     @pl.loop(0, steps)
     def _(step):
-        correlate(step, pieces, me_ref[0], mate_ref, None, False, tables, fill_ref, work_ref, out_ref, outer)
+        correlate(step, pieces, places, mate_ref, None, False, tables, fill_ref, work_ref, out_ref, outer)
         rows = pl.ds(pl.multiple_of(step * TILE, TILE), TILE)
         for n in range(outer):
             result_here[rows, n * LANES : (n + 1) * LANES] = out_ref[n]
@@ -267,22 +279,32 @@
         flush(step).wait()
 
 
-def gather_kernel(*refs, pencil):
-    *pieces, out_ref, sems = refs
-    me = lax.axis_index("ctx")
+def slice_kernel(source_ref, *refs, parts, pencil):
+    *blocks, sems = refs
     copies = []
-    for k, ref in enumerate(pieces):
-        rows = pl.ds((me ^ k) * pencil, pencil)
-        copies.append(pltpu.make_async_copy(ref, out_ref.at[rows, :], sems.at[k]))
+    for place, ref in zip(places_of("grad", parts)[2:], blocks):
+        rows = pl.ds(place * pencil, pencil)
+        copies.append(pltpu.make_async_copy(source_ref.at[rows, :], ref, sems.at[len(copies)]))
     for copy in copies:
         copy.start()
     for copy in copies:
         copy.wait()
 
 
+def gather_kernel(*refs, pencil):
+    *pieces, out_ref, sems = refs
+    copies = []
+    for place, ref in zip(places_of("back", len(pieces)), pieces):
+        rows = pl.ds(place * pencil, pencil)
+        copies.append(pltpu.make_async_copy(ref, out_ref.at[rows, :], sems.at[len(copies)]))
+    for copy in copies:
+        copy.start()
+    for copy in copies:
+        copy.wait()
+
+
 def shards(layer_input, grad_output, filter_taps):
     parts = lax.axis_size("ctx")
-    me = lax.axis_index("ctx")
     pencil, piece = layer_input.shape[0] // parts, layer_input.shape[1]
     length = piece * parts
     outer = length // LANES
@@ -290,20 +312,17 @@
     rows = -(-pencil // TILE) * TILE
     steps = rows // TILE
     ahead, back, back_scaled, twiddle = dft_tables(length)
-    me_array = me.astype(jnp.int32).reshape(1)
-    others = sorted(range(1, parts), reverse=True)
-
-    def swap(block, k):
-        return lax.ppermute(block, "ctx", [(i, i ^ k) for i in range(parts)])
-
-    def pick(array, k):
+    def exchange(what, blocks):
+        pairs = [[(i, i ^ k) for i in range(parts)] for k in order_of(what, parts)]
+        return [lax.ppermute(block, "ctx", pair) for block, pair in zip(blocks, pairs)]
+
+    def pick(array, place):
         blocks = array.reshape(parts, pencil, piece)
-        return lax.dynamic_index_in_dim(blocks, me ^ k, 0, keepdims=False)
+        return lax.dynamic_index_in_dim(blocks, place, 0, keepdims=False)
 
     def pad(block):
         return block if aligned else jnp.pad(block, ((0, rows - pencil), (0, 0)))
 
-    scalar = pl.BlockSpec(memory_space=pltpu.SMEM)
     here = pl.BlockSpec(memory_space=pltpu.VMEM)
     there = pl.BlockSpec(memory_space=pl.ANY)
     spec_shape = jax.ShapeDtypeStruct((steps, outer * TILE, 2 * LANES), jnp.float32)
@@ -320,16 +339,27 @@
     def in_hbm(array):
         return pltpu.with_memory_space_constraint(array, pltpu.HBM)
 
-    grad_pieces = [None] * parts
-    for k in others:
-        grad_pieces[k] = swap(pick(grad_output, k), k)
+    own, *others = places_of("grad", parts)
+    if aligned:
+        blocks = pl.pallas_call(
+            functools.partial(slice_kernel, parts=parts, pencil=pencil),
+            in_specs=[there],
+            out_specs=[here] * (parts - 2),
+            out_shape=[slice_shape] * (parts - 2),
+            scratch_shapes=[pltpu.SemaphoreType.DMA((parts - 2,))],
+            cost_estimate=cost(0, 2 * (parts - 2) * pencil * piece * 2),
+            name="slice_grad",
+        )(in_hbm(grad_output))
+    else:
+        blocks = [pick(grad_output, place) for place in others[1:]]
+    grad_pieces = exchange("grad", [pick(grad_output, others[0]), *blocks])
 
     taps = filter_taps.reshape(pencil, length)
     tables = [*ahead, twiddle]
     slices = parts + 1 if aligned else 0
     results = pl.pallas_call(
         functools.partial(spectrum_kernel, outer=outer, parts=parts, pencil=pencil),
-        in_specs=[scalar] + [there] * (6 if aligned else 4),
+        in_specs=[there] * (6 if aligned else 4),
         out_specs=[here] * (slices + 1),
         out_shape=[slice_shape] * slices + [spec_shape],
         scratch_shapes=[
@@ -341,34 +371,31 @@
         compiler_params=params,
         cost_estimate=cost(1, 2 * spec_bytes),
         name="taps_spectrum",
-    )(me_array, in_hbm(pad(taps)), *map(in_hbm, map(jnp.asarray, tables)), *map(in_hbm, [layer_input, grad_output] if aligned else []))
+    )(*map(in_hbm, [pad(taps), *map(jnp.asarray, tables), *([layer_input, grad_output] if aligned else [])]))
     taps_spectrum = results[-1]
-    blocks = results[:parts] if aligned else [pick(layer_input, k) for k in range(parts)]
-    grad_pieces[0] = results[parts] if aligned else pick(grad_output, 0)
-    input_pieces = [blocks[0]] + [None] * (parts - 1)
-    for k in others:
-        input_pieces[k] = swap(blocks[k], k)
+    blocks = results[:parts] if aligned else [pick(layer_input, place) for place in places_of("input", parts)]
+    grad_pieces = [results[parts] if aligned else pick(grad_output, own), *grad_pieces]
+    input_pieces = [blocks[0], *exchange("input", blocks[1:])]
 
     tables = [*ahead, *back, twiddle]
     grad_spectrum, *outgoing = pl.pallas_call(
         functools.partial(input_kernel, outer=outer, parts=parts),
-        in_specs=[scalar] + [here] * (parts + 1 + len(tables)),
+        in_specs=[here] * (parts + 1 + len(tables)),
         out_specs=[here] * (parts + 1),
         out_shape=[spec_shape, *[slice_shape] * parts],
         scratch_shapes=[lane_tiles, work, lane_tiles],
         compiler_params=params,
         cost_estimate=cost(2, 2 * spec_bytes),
         name="grad_input",
-    )(me_array, *map(pad, grad_pieces), taps_spectrum, *tables)
-
-    incoming = [outgoing[0][:pencil]] + [None] * (parts - 1)
-    for k in others:
-        incoming[k] = swap(outgoing[k][:pencil], k)
+    )(*map(pad, grad_pieces), taps_spectrum, *tables)
+
+    outgoing = [block[:pencil] for block in outgoing]
+    incoming = [outgoing[0], *exchange("back", outgoing[1:])]
 
     tables = [*ahead, *back_scaled, twiddle]
     grad_filter = pl.pallas_call(
         functools.partial(filter_kernel, outer=outer, parts=parts),
-        in_specs=[scalar] + [here] * (parts + 1 + len(tables)),
+        in_specs=[here] * (parts + 1 + len(tables)),
         out_specs=there,
         out_shape=jax.ShapeDtypeStruct((rows, length), jnp.float32),
         scratch_shapes=[
@@ -381,7 +408,7 @@
         compiler_params=params,
         cost_estimate=cost(2, 2 * spec_bytes),
         name="grad_filter",
-    )(me_array, *map(pad, input_pieces), grad_spectrum, *tables)
+    )(*map(pad, input_pieces), grad_spectrum, *tables)
 
     if aligned:
         grad_input = pl.pallas_call(
@@ -393,10 +420,10 @@
             name="gather_pieces",
         )(*[pltpu.with_memory_space_constraint(block, pltpu.VMEM) for block in incoming])
     else:
-        slots = jnp.zeros((parts, pencil, piece), jnp.bfloat16)
-        for k, block in enumerate(incoming):
-            slots = lax.dynamic_update_index_in_dim(slots, block, me ^ k, 0)
-        grad_input = slots.reshape(parts * pencil, piece)
+        grad_input = jnp.zeros((parts, pencil, piece), jnp.bfloat16)
+        for place, block in zip(places_of("back", parts), incoming):
+            grad_input = lax.dynamic_update_index_in_dim(grad_input, block, place, 0)
+        grad_input = grad_input.reshape(parts * pencil, piece)
     return (grad_input, grad_filter[:pencil].reshape(1, pencil, length))
 
 

time: 42.3 us -> 42 us (level)
  Pallas kernels: 23.1 us -> 24.9 us
  waiting for transfers between devices: 4.93 us -> 3.3 us
    pallas_call x0 -> x1, Pallas kernels: none -> 1.83 us  [shards(): pl.pallas_call(functools.partial(slice_kernel, parts=parts, pencil=pencil...]
    ppermute x9, waiting for transfers between devices: 4.93 us -> 3.3 us  [exchange(): lax.ppermute(block, 'ctx', pair)]
  transfers between devices with their start and end apart: 9 -> 9, of which waited for: 3 -> 3; matrix products, arithmetic and copies ran while one was open for 0% -> 0% of each run, Pallas kernels for 52% -> 57%
where the time goes in v4:
time: 42 us; the launch traced here: 41.8 us
  Pallas kernels  24.9 us (59%)
  starting transfers between devices  11.7 us (28%)
  waiting for transfers between devices  3.3 us (8%)
  local copies, waits for them, and re-layouts  1.11 us (3%)
  between operations  0.78 us (2%)
    ppermute x9, starting transfers between devices, exchange(): lax.ppermute(block, 'ctx', pair)  11.7 us
    pallas_call x1, Pallas kernels, shards(): pl.pallas_call(functools.partial(filter_kernel, outer=outer, parts=parts)...  8.54 us
    pallas_call x1, Pallas kernels, shards(): pl.pallas_call(functools.partial(input_kernel, outer=outer, parts=parts),...  8.01 us
    pallas_call x1, Pallas kernels, shards(): pl.pallas_call(functools.partial(spectrum_kernel, outer=outer, parts=part...  5.53 us
    ppermute x9, waiting for transfers between devices, exchange(): lax.ppermute(block, 'ctx', pair)  3.3 us
    pallas_call x1, Pallas kernels, shards(): pl.pallas_call(functools.partial(slice_kernel, parts=parts, pencil=pencil...  1.83 us
    squeeze x1, local copies, waits for them, and re-layouts, pick(): return lax.dynamic_index_in_dim(blocks, place, 0, keepdims=False)  1.06 us
    pallas_call x1, Pallas kernels, shards(): pl.pallas_call(functools.partial(gather_kernel, pencil=pencil), in_specs=...  0.99 us
  transfers between devices with their start and end apart: 9, of which 3 were waited for; matrix products, arithmetic and copies ran while one was open for 0% of the time, Pallas kernels for 57%

profile of v4, /device:TPU:0, one launch (start us, length us, event | category | flops | bytes accessed | tf_op | source)
XLA Modules:
  0.0 41.8 jit_solution(15071791673840544606)
XLA Ops:
  0.6 0.0 copy-start.6
  0.6 0.0 copy-start
  0.7 0.0 copy-start.1
  0.7 0.0 copy-start.4
  0.7 0.0 copy-start.5
  0.7 1.1 %dynamic-slice_bitcast_fusion = bf16[128,1024]{1,0:T(8,128)(2,1)S(1)} fusion(bf16[4,128,1024]{2,1,0:T(8,128)(2,1)} %bitcast.5, s32[]{:T(128)S(6)} %select_n.4), kind=kLoop, calls=%fused_computation | loop fusion | bytes 524292 | tf_op jit(solution)/shard_map/jit(dynamic_index_in_dim)/squeeze | solution.py:321
  1.8 4.0 %collective-permute-start = (bf16[128,1024]{1,0:T(8,128)(2,1)S(1)}, bf16[128,1024]{1,0:T(8,128)(2,1)S(1)}, u32[]{:S(2)}, u32[]{:S(2)}) collective-permute-start(bf16[128,1024]{1,0:T(8,128)(2,1)S(1)} %dynamic-slice_bitcast_fusion), channel_id=1, source_target_pairs={{0,6},{2,4},{4,2},{6,0},{1,7},{3,5},{5,3},{7,1},{8,14},{10,12},{12... | collective-permute-start | bytes 786440 | tf_op jit(solution)/shard_map/ppermute | solution.py:317
  5.7 1.8 %slice_grad.1 = (bf16[128,1024]{1,0:T(8,128)(2,1)}, bf16[128,1024]{1,0:T(8,128)(2,1)}) custom-call(bf16[512,1024]{1,0:T(8,128)(2,1)} %source_ref.1), custom_call_target="tpu_custom_call" | custom-call | bytes 1048576 | tf_op jit(solution)/shard_map/slice_grad/pallas_call | solution.py:344
  7.6 0.6 %collective-permute-start.1 = (bf16[128,1024]{1,0:T(8,128)(2,1)}, bf16[128,1024]{1,0:T(8,128)(2,1)S(1)}, u32[]{:S(2)}, u32[]{:S(2)}) collective-permute-start(bf16[128,1024]{1,0:T(8,128)(2,1)} %get-tuple-element.16), channel_id=1, source_target_pairs={{0,2},{2,0},{4,6},{6,4},{1,3},{3,1},{5,7},{7,5},{8,10},{10,8},{12,... | collective-permute-start | bytes 786440 | tf_op jit(solution)/shard_map/ppermute | solution.py:317
  8.2 0.1 collective-permute-start.2
  8.2 5.5 %taps_spectrum.1 = (bf16[128,1024]{1,0:T(8,128)(2,1)S(1)}, bf16[128,1024]{1,0:T(8,128)(2,1)S(1)}, bf16[128,1024]{1,0:T(8,128)(2,1)S(1)}, bf16[128,1024]{1,0:T(8,...) custom-call(f32[128,4096]{1,0:T(8,128)} %bitcast.6, ...), custom_call_target="tpu_custom_call" | custom-call | flops 1610612736 | bytes 8388608 | tf_op jit(solution)/shard_map/taps_spectrum/pallas_call | solution.py:360
  13.8 2.0 %collective-permute-start.6 = (bf16[128,1024]{1,0:T(8,128)(2,1)S(1)}, bf16[128,1024]{1,0:T(8,128)(2,1)S(1)}, u32[]{:S(2)}, u32[]{:S(2)}) collective-permute-start(bf16[128,1024]{1,0:T(8,128)(2,1)S(1)} %get-tuple-element.24), channel_id=1, source_target_pairs={{0,2},{2,0},{4,6},{6,4},{1,3},{3,1},{5,7},{7,5},{8,10},{10,8},{12,... | collective-permute-start | bytes 786440 | tf_op jit(solution)/shard_map/ppermute | solution.py:317
  15.8 1.5 %collective-permute-start.7 = (bf16[128,1024]{1,0:T(8,128)(2,1)S(1)}, bf16[128,1024]{1,0:T(8,128)(2,1)S(1)}, u32[]{:S(2)}, u32[]{:S(2)}) collective-permute-start(bf16[128,1024]{1,0:T(8,128)(2,1)S(1)} %get-tuple-element.25), channel_id=1, source_target_pairs={{0,4},{2,6},{4,0},{6,2},{1,5},{3,7},{5,1},{7,3},{8,12},{10,14},{12... | collective-permute-start | bytes 786440 | tf_op jit(solution)/shard_map/ppermute | solution.py:317
  17.3 0.0 collective-permute-done.refs_1_
  17.3 0.0 collective-permute-start.8
  17.3 1.8 %collective-permute-done.1.refs_2_ = bf16[128,1024]{1,0:T(8,128)(2,1)S(1)} collective-permute-done((bf16[128,1024]{1,0:T(8,128)(2,1)}, bf16[128,1024]{1,0:T(8,128)(2,1)S(1)}, u32[]{:S(2)}, u32[]{:S(2)}) %collective-permute-start.1) | collective-permute-done | bytes 262176 | tf_op jit(solution)/shard_map/ppermute | solution.py:317
  19.1 0.0 collective-permute-done.2.refs_3_
  19.1 0.0 copy-done.6
  19.1 0.0 copy-done
  19.1 0.0 copy-done.1
  19.1 0.0 copy-done.4
  19.1 0.0 copy-done.5
  19.1 0.0 copy-start.2
  19.1 0.0 copy-start.3
  19.2 8.0 %grad_input.1 = (f32[8,512,256]{2,1,0:T(8,128)S(1)}, bf16[128,1024]{1,0:T(8,128)(2,1)S(1)}, bf16[128,1024]{1,0:T(8,128)(2,1)S(1)}, bf16[128,1024]{1,0:T(8,128)(2,1)S(1)}, bf16[128,1024]{1,0:T(8,128)(2,1)S(1)}) custom-call(bf16[128,1024]{1,0:T(8,128)(2,1)S(1)} %get-tuple-element.15.refs_0_, bf16[128,1024]{1,0:T(8,128)(2,1)S(1)} %collective-permute-done.refs_1_, ...), custom_call_target="tpu_custom_call" | custom-call | flops 3221225472 | bytes 8388608 | tf_op jit(solution)/shard_map/grad_input/pallas_call | solution.py:381
  27.2 1.4 %collective-permute-start.3 = (bf16[128,1024]{1,0:T(8,128)(2,1)S(1)}, bf16[128,1024]{1,0:T(8,128)(2,1)S(1)}, u32[]{:S(2)}, u32[]{:S(2)}) collective-permute-start(bf16[128,1024]{1,0:T(8,128)(2,1)S(1)} %get-tuple-element.20), channel_id=1, source_target_pairs={{0,6},{2,4},{4,2},{6,0},{1,7},{3,5},{5,3},{7,1},{8,14},{10,12},{12... | collective-permute-start | bytes 786440 | tf_op jit(solution)/shard_map/ppermute | solution.py:317
  28.6 1.6 %collective-permute-start.4 = (bf16[128,1024]{1,0:T(8,128)(2,1)S(1)}, bf16[128,1024]{1,0:T(8,128)(2,1)S(1)}, u32[]{:S(2)}, u32[]{:S(2)}) collective-permute-start(bf16[128,1024]{1,0:T(8,128)(2,1)S(1)} %get-tuple-element.21), channel_id=1, source_target_pairs={{0,4},{2,6},{4,0},{6,2},{1,5},{3,7},{5,1},{7,3},{8,12},{10,14},{12... | collective-permute-start | bytes 786440 | tf_op jit(solution)/shard_map/ppermute | solution.py:317
  30.2 0.0 collective-permute-done.6.refs_1_
  30.2 0.5 %collective-permute-start.5 = (bf16[128,1024]{1,0:T(8,128)(2,1)S(1)}, bf16[128,1024]{1,0:T(8,128)(2,1)S(1)}, u32[]{:S(2)}, u32[]{:S(2)}) collective-permute-start(bf16[128,1024]{1,0:T(8,128)(2,1)S(1)} %get-tuple-element.22), channel_id=1, source_target_pairs={{0,2},{2,0},{4,6},{6,4},{1,3},{3,1},{5,7},{7,5},{8,10},{10,8},{12,... | collective-permute-start | bytes 786440 | tf_op jit(solution)/shard_map/ppermute | solution.py:317
  30.7 0.0 collective-permute-done.7.refs_2_
  30.7 0.0 collective-permute-done.8.refs_3_
  30.7 0.0 copy-done.2
  30.7 0.0 copy-done.3
  30.7 8.5 %grad_filter.1 = f32[128,4096]{1,0:T(8,128)} custom-call(bf16[128,1024]{1,0:T(8,128)(2,1)S(1)} %get-tuple-element.23.refs_0_, bf16[128,1024]{1,0:T(8,128)(2,1)S(1)} %collective-permute-done.6.refs_1_, bf16[128,1024]{1,0:T(8,128)(2,1)S(1)} %collective-permute-done.7.refs_2_, bf16[128,1024]{1,0:T(8,128)(2,1)S(1)} %collective-permute-done.8.refs_3_, ...), custom_call_target="tpu_custom_call" | custom-call | flops 3221225472 | bytes 8388608 | tf_op jit(solution)/shard_map/grad_filter/pallas_call | solution.py:396
  39.3 0.0 collective-permute-done.3.refs_1_
  39.3 1.3 %collective-permute-done.4.refs_2_ = bf16[128,1024]{1,0:T(8,128)(2,1)S(1)} collective-permute-done((bf16[128,1024]{1,0:T(8,128)(2,1)S(1)}, bf16[128,1024]{1,0:T(8,128)(2,1)S(1)}, u32[]{:S(2)}, u32[]{:S(2)}) %collective-permute-start.4) | collective-permute-done | bytes 262176 | tf_op jit(solution)/shard_map/ppermute | solution.py:317
  40.6 0.3 collective-permute-done.5.refs_3_
  40.8 1.0 %gather_pieces.1 = bf16[512,1024]{1,0:T(8,128)(2,1)} custom-call(bf16[128,1024]{1,0:T(8,128)(2,1)S(1)} %get-tuple-element.19.refs_0_, bf16[128,1024]{1,0:T(8,128)(2,1)S(1)} %collective-permute-done.3.refs_1_, bf16[128,1024]{1,0:T(8,128)(2,1)S(1)} %collective-permute-done.4.refs_2_, bf16[128,1024]{1,0:T(8,128)(2,1)S(1)} %collective-permute-done.5.refs_3_), custom_call_target="tpu_custom_call" | custom-call | tf_op jit(solution)/shard_map/gather_pieces/pallas_call | solution.py:414
Async XLA Ops:
  0.6 18.5 %copy-start.6 = (f32[32,2,128]{2,1,0:T(2,128)S(1)}, f32[32,2,128]{2,1,0:T(2,128)}, u32[]{:S(2)}) copy-start(f32[32,2,128]{2,1,0:T(2,128)} %constant.30.clone.twiddle_ref.refs_9_) | copy-start | bytes 98308
  0.6 18.5 %copy-start = (bf16[256,256]{1,0:T(8,128)(2,1)S(1)}, bf16[256,256]{1,0:T(8,128)(2,1)}, u32[]{:S(2)}) copy-start(bf16[256,256]{1,0:T(8,128)(2,1)} %constant.29.clone.ahead_low.refs_6_) | copy-start | bytes 393220
  0.7 18.4 %copy-start.1 = (bf16[256,256]{1,0:T(8,128)(2,1)S(1)}, bf16[256,256]{1,0:T(8,128)(2,1)}, u32[]{:S(2)}) copy-start(bf16[256,256]{1,0:T(8,128)(2,1)} %constant.28.clone.ahead_high.refs_5_) | copy-start | bytes 393220
  0.7 18.4 %copy-start.4 = (bf16[256,256]{1,0:T(8,128)(2,1)S(1)}, bf16[256,256]{1,0:T(8,128)(2,1)}, u32[]{:S(2)}) copy-start(bf16[256,256]{1,0:T(8,128)(2,1)} %constant.32.clone.refs_8_) | copy-start | bytes 393220
  0.7 18.4 %copy-start.5 = (bf16[256,256]{1,0:T(8,128)(2,1)S(1)}, bf16[256,256]{1,0:T(8,128)(2,1)}, u32[]{:S(2)}) copy-start(bf16[256,256]{1,0:T(8,128)(2,1)} %constant.31.clone.refs_7_) | copy-start | bytes 393220
  1.8 15.5 %collective-permute-start = (bf16[128,1024]{1,0:T(8,128)(2,1)S(1)}, bf16[128,1024]{1,0:T(8,128)(2,1)S(1)}, u32[]{:S(2)}, u32[]{:S(2)}) collective-permute-start(bf16[128,1024]{1,0:T(8,128)(2,1)S(1)} %dynamic-slice_bitcast_fusion), channel_id=1, source_target_pairs={{0,6},{2,4},{4,2},{6,0},{1,7},{3,5},{5,3},{7,1},{8,14},{10,12},{12... | collective-permute-start | bytes 786440 | tf_op jit(solution)/shard_map/ppermute | solution.py:317
  7.6 11.5 %collective-permute-start.1 = (bf16[128,1024]{1,0:T(8,128)(2,1)}, bf16[128,1024]{1,0:T(8,128)(2,1)S(1)}, u32[]{:S(2)}, u32[]{:S(2)}) collective-permute-start(bf16[128,1024]{1,0:T(8,128)(2,1)} %get-tuple-element.16), channel_id=1, source_target_pairs={{0,2},{2,0},{4,6},{6,4},{1,3},{3,1},{5,7},{7,5},{8,10},{10,8},{12,... | collective-permute-start | bytes 786440 | tf_op jit(solution)/shard_map/ppermute | solution.py:317
  8.2 10.9 %collective-permute-start.2 = (bf16[128,1024]{1,0:T(8,128)(2,1)}, bf16[128,1024]{1,0:T(8,128)(2,1)S(1)}, u32[]{:S(2)}, u32[]{:S(2)}) collective-permute-start(bf16[128,1024]{1,0:T(8,128)(2,1)} %get-tuple-element.17), channel_id=1, source_target_pairs={{0,4},{2,6},{4,0},{6,2},{1,5},{3,7},{5,1},{7,3},{8,12},{10,14},{12... | collective-permute-start | bytes 786440 | tf_op jit(solution)/shard_map/ppermute | solution.py:317
  13.8 16.4 %collective-permute-start.6 = (bf16[128,1024]{1,0:T(8,128)(2,1)S(1)}, bf16[128,1024]{1,0:T(8,128)(2,1)S(1)}, u32[]{:S(2)}, u32[]{:S(2)}) collective-permute-start(bf16[128,1024]{1,0:T(8,128)(2,1)S(1)} %get-tuple-element.24), channel_id=1, source_target_pairs={{0,2},{2,0},{4,6},{6,4},{1,3},{3,1},{5,7},{7,5},{8,10},{10,8},{12,... | collective-permute-start | bytes 786440 | tf_op jit(solution)/shard_map/ppermute | solution.py:317
  15.8 15.0 %collective-permute-start.7 = (bf16[128,1024]{1,0:T(8,128)(2,1)S(1)}, bf16[128,1024]{1,0:T(8,128)(2,1)S(1)}, u32[]{:S(2)}, u32[]{:S(2)}) collective-permute-start(bf16[128,1024]{1,0:T(8,128)(2,1)S(1)} %get-tuple-element.25), channel_id=1, source_target_pairs={{0,4},{2,6},{4,0},{6,2},{1,5},{3,7},{5,1},{7,3},{8,12},{10,14},{12... | collective-permute-start | bytes 786440 | tf_op jit(solution)/shard_map/ppermute | solution.py:317
  17.3 13.4 %collective-permute-start.8 = (bf16[128,1024]{1,0:T(8,128)(2,1)S(1)}, bf16[128,1024]{1,0:T(8,128)(2,1)S(1)}, u32[]{:S(2)}, u32[]{:S(2)}) collective-permute-start(bf16[128,1024]{1,0:T(8,128)(2,1)S(1)} %get-tuple-element.26), channel_id=1, source_target_pairs={{0,6},{2,4},{4,2},{6,0},{1,7},{3,5},{5,3},{7,1},{8,14},{10,12},{12... | collective-permute-start | bytes 786440 | tf_op jit(solution)/shard_map/ppermute | solution.py:317
  19.1 11.6 %copy-start.2 = (bf16[256,256]{1,0:T(8,128)(2,1)S(1)}, bf16[256,256]{1,0:T(8,128)(2,1)}, u32[]{:S(2)}) copy-start(bf16[256,256]{1,0:T(8,128)(2,1)} %constant.34.clone.refs_8_) | copy-start | bytes 393220
  19.1 11.6 %copy-start.3 = (bf16[256,256]{1,0:T(8,128)(2,1)S(1)}, bf16[256,256]{1,0:T(8,128)(2,1)}, u32[]{:S(2)}) copy-start(bf16[256,256]{1,0:T(8,128)(2,1)} %constant.33.clone.refs_7_) | copy-start | bytes 393220
  27.2 12.1 %collective-permute-start.3 = (bf16[128,1024]{1,0:T(8,128)(2,1)S(1)}, bf16[128,1024]{1,0:T(8,128)(2,1)S(1)}, u32[]{:S(2)}, u32[]{:S(2)}) collective-permute-start(bf16[128,1024]{1,0:T(8,128)(2,1)S(1)} %get-tuple-element.20), channel_id=1, source_target_pairs={{0,6},{2,4},{4,2},{6,0},{1,7},{3,5},{5,3},{7,1},{8,14},{10,12},{12... | collective-permute-start | bytes 786440 | tf_op jit(solution)/shard_map/ppermute | solution.py:317
  28.6 12.0 %collective-permute-start.4 = (bf16[128,1024]{1,0:T(8,128)(2,1)S(1)}, bf16[128,1024]{1,0:T(8,128)(2,1)S(1)}, u32[]{:S(2)}, u32[]{:S(2)}) collective-permute-start(bf16[128,1024]{1,0:T(8,128)(2,1)S(1)} %get-tuple-element.21), channel_id=1, source_target_pairs={{0,4},{2,6},{4,0},{6,2},{1,5},{3,7},{5,1},{7,3},{8,12},{10,14},{12... | collective-permute-start | bytes 786440 | tf_op jit(solution)/shard_map/ppermute | solution.py:317
  30.2 10.6 %collective-permute-start.5 = (bf16[128,1024]{1,0:T(8,128)(2,1)S(1)}, bf16[128,1024]{1,0:T(8,128)(2,1)S(1)}, u32[]{:S(2)}, u32[]{:S(2)}) collective-permute-start(bf16[128,1024]{1,0:T(8,128)(2,1)S(1)} %get-tuple-element.22), channel_id=1, source_target_pairs={{0,2},{2,0},{4,6},{6,4},{1,3},{3,1},{5,7},{7,5},{8,10},{10,8},{12,... | collective-permute-start | bytes 786440 | tf_op jit(solution)/shard_map/ppermute | solution.py:317

commit v5 on v4

--- a/solution.py
+++ b/solution.py
@@ -138,7 +138,9 @@
     high = values.astype(jnp.bfloat16)
     low = (values - high.astype(jnp.float32)).astype(jnp.bfloat16)
     dot = functools.partial(jnp.dot, preferred_element_type=jnp.float32)
-    return dot(high, high_ref[...]) + dot(low, high_ref[...]) + dot(high, low_ref[...])
+    both = dot(jnp.concatenate([high, low], axis=0), high_ref[...])
+    count = high.shape[0]
+    return both[:count] + both[count:] + dot(high, low_ref[...])
 
 
 def order_of(what, parts):

time: 42 us -> 41.9 us (level)
  Pallas kernels: 24.9 us -> 24.4 us
  transfers between devices with their start and end apart: 9 -> 9, of which waited for: 3 -> 3; matrix products, arithmetic and copies ran while one was open for 0% -> 0% of each run, Pallas kernels for 57% -> 56%
where the time goes in v5:
time: 41.9 us; the launch traced here: 41.7 us
  Pallas kernels  24.4 us (58%)
  starting transfers between devices  11.7 us (28%)
  waiting for transfers between devices  3.66 us (9%)
  local copies, waits for them, and re-layouts  1.11 us (3%)
  between operations  0.78 us (2%)
    ppermute x9, starting transfers between devices, exchange(): lax.ppermute(block, 'ctx', pair)  11.7 us
    pallas_call x1, Pallas kernels, shards(): pl.pallas_call(functools.partial(filter_kernel, outer=outer, parts=parts)...  8.46 us
    pallas_call x1, Pallas kernels, shards(): pl.pallas_call(functools.partial(input_kernel, outer=outer, parts=parts),...  7.9 us
    pallas_call x1, Pallas kernels, shards(): pl.pallas_call(functools.partial(spectrum_kernel, outer=outer, parts=part...  5.25 us
    ppermute x9, waiting for transfers between devices, exchange(): lax.ppermute(block, 'ctx', pair)  3.66 us
    pallas_call x1, Pallas kernels, shards(): pl.pallas_call(functools.partial(slice_kernel, parts=parts, pencil=pencil...  1.83 us
    squeeze x1, local copies, waits for them, and re-layouts, pick(): return lax.dynamic_index_in_dim(blocks, place, 0, keepdims=False)  1.06 us
    pallas_call x1, Pallas kernels, shards(): pl.pallas_call(functools.partial(gather_kernel, pencil=pencil), in_specs=...  0.99 us
  transfers between devices with their start and end apart: 9, of which 3 were waited for; matrix products, arithmetic and copies ran while one was open for 0% of the time, Pallas kernels for 56%

profile of v5, /device:TPU:0, one launch (start us, length us, event | category | flops | bytes accessed | tf_op | source)
XLA Modules:
  0.0 41.7 jit_solution(2347168664248647186)
XLA Ops:
  0.6 0.0 copy-start.6
  0.6 0.0 copy-start
  0.7 0.0 copy-start.1
  0.7 0.0 copy-start.4
  0.7 0.0 copy-start.5
  0.7 1.1 %dynamic-slice_bitcast_fusion = bf16[128,1024]{1,0:T(8,128)(2,1)S(1)} fusion(bf16[4,128,1024]{2,1,0:T(8,128)(2,1)} %bitcast.5, s32[]{:T(128)S(6)} %select_n.4), kind=kLoop, calls=%fused_computation | loop fusion | bytes 524292 | tf_op jit(solution)/shard_map/jit(dynamic_index_in_dim)/squeeze | solution.py:323
  1.8 4.0 %collective-permute-start = (bf16[128,1024]{1,0:T(8,128)(2,1)S(1)}, bf16[128,1024]{1,0:T(8,128)(2,1)S(1)}, u32[]{:S(2)}, u32[]{:S(2)}) collective-permute-start(bf16[128,1024]{1,0:T(8,128)(2,1)S(1)} %dynamic-slice_bitcast_fusion), channel_id=1, source_target_pairs={{0,6},{2,4},{4,2},{6,0},{1,7},{3,5},{5,3},{7,1},{8,14},{10,12},{12... | collective-permute-start | bytes 786440 | tf_op jit(solution)/shard_map/ppermute | solution.py:319
  5.7 1.8 %slice_grad.1 = (bf16[128,1024]{1,0:T(8,128)(2,1)}, bf16[128,1024]{1,0:T(8,128)(2,1)}) custom-call(bf16[512,1024]{1,0:T(8,128)(2,1)} %source_ref.1), custom_call_target="tpu_custom_call" | custom-call | bytes 1048576 | tf_op jit(solution)/shard_map/slice_grad/pallas_call | solution.py:346
  7.6 0.6 %collective-permute-start.1 = (bf16[128,1024]{1,0:T(8,128)(2,1)}, bf16[128,1024]{1,0:T(8,128)(2,1)S(1)}, u32[]{:S(2)}, u32[]{:S(2)}) collective-permute-start(bf16[128,1024]{1,0:T(8,128)(2,1)} %get-tuple-element.16), channel_id=1, source_target_pairs={{0,2},{2,0},{4,6},{6,4},{1,3},{3,1},{5,7},{7,5},{8,10},{10,8},{12,... | collective-permute-start | bytes 786440 | tf_op jit(solution)/shard_map/ppermute | solution.py:319
  8.2 0.1 collective-permute-start.2
  8.2 5.2 %taps_spectrum.1 = (bf16[128,1024]{1,0:T(8,128)(2,1)S(1)}, bf16[128,1024]{1,0:T(8,128)(2,1)S(1)}, bf16[128,1024]{1,0:T(8,128)(2,1)S(1)}, bf16[128,1024]{1,0:T(8,...) custom-call(f32[128,4096]{1,0:T(8,128)} %bitcast.6, ...), custom_call_target="tpu_custom_call" | custom-call | flops 1610612736 | bytes 8388608 | tf_op jit(solution)/shard_map/taps_spectrum/pallas_call | solution.py:362
  13.5 2.0 %collective-permute-start.6 = (bf16[128,1024]{1,0:T(8,128)(2,1)S(1)}, bf16[128,1024]{1,0:T(8,128)(2,1)S(1)}, u32[]{:S(2)}, u32[]{:S(2)}) collective-permute-start(bf16[128,1024]{1,0:T(8,128)(2,1)S(1)} %get-tuple-element.24), channel_id=1, source_target_pairs={{0,2},{2,0},{4,6},{6,4},{1,3},{3,1},{5,7},{7,5},{8,10},{10,8},{12,... | collective-permute-start | bytes 786440 | tf_op jit(solution)/shard_map/ppermute | solution.py:319
  15.5 1.5 %collective-permute-start.7 = (bf16[128,1024]{1,0:T(8,128)(2,1)S(1)}, bf16[128,1024]{1,0:T(8,128)(2,1)S(1)}, u32[]{:S(2)}, u32[]{:S(2)}) collective-permute-start(bf16[128,1024]{1,0:T(8,128)(2,1)S(1)} %get-tuple-element.25), channel_id=1, source_target_pairs={{0,4},{2,6},{4,0},{6,2},{1,5},{3,7},{5,1},{7,3},{8,12},{10,14},{12... | collective-permute-start | bytes 786440 | tf_op jit(solution)/shard_map/ppermute | solution.py:319
  17.0 0.0 collective-permute-done.refs_1_
  17.0 0.0 collective-permute-start.8
  17.0 2.1 %collective-permute-done.1.refs_2_ = bf16[128,1024]{1,0:T(8,128)(2,1)S(1)} collective-permute-done((bf16[128,1024]{1,0:T(8,128)(2,1)}, bf16[128,1024]{1,0:T(8,128)(2,1)S(1)}, u32[]{:S(2)}, u32[]{:S(2)}) %collective-permute-start.1) | collective-permute-done | bytes 262176 | tf_op jit(solution)/shard_map/ppermute | solution.py:319
  19.1 0.0 collective-permute-done.2.refs_3_
  19.1 0.0 copy-done.6
  19.1 0.0 copy-done
  19.1 0.0 copy-done.1
  19.1 0.0 copy-done.4
  19.1 0.0 copy-done.5
  19.1 0.0 copy-start.2
  19.1 0.0 copy-start.3
  19.2 7.9 %grad_input.1 = (f32[8,512,256]{2,1,0:T(8,128)S(1)}, bf16[128,1024]{1,0:T(8,128)(2,1)S(1)}, bf16[128,1024]{1,0:T(8,128)(2,1)S(1)}, bf16[128,1024]{1,0:T(8,128)(2,1)S(1)}, bf16[128,1024]{1,0:T(8,128)(2,1)S(1)}) custom-call(bf16[128,1024]{1,0:T(8,128)(2,1)S(1)} %get-tuple-element.15.refs_0_, bf16[128,1024]{1,0:T(8,128)(2,1)S(1)} %collective-permute-done.refs_1_, ...), custom_call_target="tpu_custom_call" | custom-call | flops 3221225472 | bytes 8388608 | tf_op jit(solution)/shard_map/grad_input/pallas_call | solution.py:383
  27.1 1.5 %collective-permute-start.3 = (bf16[128,1024]{1,0:T(8,128)(2,1)S(1)}, bf16[128,1024]{1,0:T(8,128)(2,1)S(1)}, u32[]{:S(2)}, u32[]{:S(2)}) collective-permute-start(bf16[128,1024]{1,0:T(8,128)(2,1)S(1)} %get-tuple-element.20), channel_id=1, source_target_pairs={{0,6},{2,4},{4,2},{6,0},{1,7},{3,5},{5,3},{7,1},{8,14},{10,12},{12... | collective-permute-start | bytes 786440 | tf_op jit(solution)/shard_map/ppermute | solution.py:319
  28.6 1.5 %collective-permute-start.4 = (bf16[128,1024]{1,0:T(8,128)(2,1)S(1)}, bf16[128,1024]{1,0:T(8,128)(2,1)S(1)}, u32[]{:S(2)}, u32[]{:S(2)}) collective-permute-start(bf16[128,1024]{1,0:T(8,128)(2,1)S(1)} %get-tuple-element.21), channel_id=1, source_target_pairs={{0,4},{2,6},{4,0},{6,2},{1,5},{3,7},{5,1},{7,3},{8,12},{10,14},{12... | collective-permute-start | bytes 786440 | tf_op jit(solution)/shard_map/ppermute | solution.py:319
  30.1 0.0 collective-permute-done.6.refs_1_
  30.1 0.5 %collective-permute-start.5 = (bf16[128,1024]{1,0:T(8,128)(2,1)S(1)}, bf16[128,1024]{1,0:T(8,128)(2,1)S(1)}, u32[]{:S(2)}, u32[]{:S(2)}) collective-permute-start(bf16[128,1024]{1,0:T(8,128)(2,1)S(1)} %get-tuple-element.22), channel_id=1, source_target_pairs={{0,2},{2,0},{4,6},{6,4},{1,3},{3,1},{5,7},{7,5},{8,10},{10,8},{12,... | collective-permute-start | bytes 786440 | tf_op jit(solution)/shard_map/ppermute | solution.py:319
  30.6 0.0 collective-permute-done.7.refs_2_
  30.6 0.0 collective-permute-done.8.refs_3_
  30.6 0.0 copy-done.2
  30.6 0.0 copy-done.3
  30.6 8.5 %grad_filter.1 = f32[128,4096]{1,0:T(8,128)} custom-call(bf16[128,1024]{1,0:T(8,128)(2,1)S(1)} %get-tuple-element.23.refs_0_, bf16[128,1024]{1,0:T(8,128)(2,1)S(1)} %collective-permute-done.6.refs_1_, bf16[128,1024]{1,0:T(8,128)(2,1)S(1)} %collective-permute-done.7.refs_2_, bf16[128,1024]{1,0:T(8,128)(2,1)S(1)} %collective-permute-done.8.refs_3_, ...), custom_call_target="tpu_custom_call" | custom-call | flops 3221225472 | bytes 8388608 | tf_op jit(solution)/shard_map/grad_filter/pallas_call | solution.py:398
  39.1 0.0 collective-permute-done.3.refs_1_
  39.1 1.3 %collective-permute-done.4.refs_2_ = bf16[128,1024]{1,0:T(8,128)(2,1)S(1)} collective-permute-done((bf16[128,1024]{1,0:T(8,128)(2,1)S(1)}, bf16[128,1024]{1,0:T(8,128)(2,1)S(1)}, u32[]{:S(2)}, u32[]{:S(2)}) %collective-permute-start.4) | collective-permute-done | bytes 262176 | tf_op jit(solution)/shard_map/ppermute | solution.py:319
  40.5 0.2 collective-permute-done.5.refs_3_
  40.7 1.0 %gather_pieces.1 = bf16[512,1024]{1,0:T(8,128)(2,1)} custom-call(bf16[128,1024]{1,0:T(8,128)(2,1)S(1)} %get-tuple-element.19.refs_0_, bf16[128,1024]{1,0:T(8,128)(2,1)S(1)} %collective-permute-done.3.refs_1_, bf16[128,1024]{1,0:T(8,128)(2,1)S(1)} %collective-permute-done.4.refs_2_, bf16[128,1024]{1,0:T(8,128)(2,1)S(1)} %collective-permute-done.5.refs_3_), custom_call_target="tpu_custom_call" | custom-call | tf_op jit(solution)/shard_map/gather_pieces/pallas_call | solution.py:416
Async XLA Ops:
  0.6 18.5 %copy-start.6 = (f32[32,2,128]{2,1,0:T(2,128)S(1)}, f32[32,2,128]{2,1,0:T(2,128)}, u32[]{:S(2)}) copy-start(f32[32,2,128]{2,1,0:T(2,128)} %constant.30.clone.twiddle_ref.refs_9_) | copy-start | bytes 98308
  0.6 18.5 %copy-start = (bf16[256,256]{1,0:T(8,128)(2,1)S(1)}, bf16[256,256]{1,0:T(8,128)(2,1)}, u32[]{:S(2)}) copy-start(bf16[256,256]{1,0:T(8,128)(2,1)} %constant.29.clone.ahead_low.refs_6_) | copy-start | bytes 393220
  0.7 18.4 %copy-start.1 = (bf16[256,256]{1,0:T(8,128)(2,1)S(1)}, bf16[256,256]{1,0:T(8,128)(2,1)}, u32[]{:S(2)}) copy-start(bf16[256,256]{1,0:T(8,128)(2,1)} %constant.28.clone.ahead_high.refs_5_) | copy-start | bytes 393220
  0.7 18.4 %copy-start.4 = (bf16[256,256]{1,0:T(8,128)(2,1)S(1)}, bf16[256,256]{1,0:T(8,128)(2,1)}, u32[]{:S(2)}) copy-start(bf16[256,256]{1,0:T(8,128)(2,1)} %constant.32.clone.refs_8_) | copy-start | bytes 393220
  0.7 18.4 %copy-start.5 = (bf16[256,256]{1,0:T(8,128)(2,1)S(1)}, bf16[256,256]{1,0:T(8,128)(2,1)}, u32[]{:S(2)}) copy-start(bf16[256,256]{1,0:T(8,128)(2,1)} %constant.31.clone.refs_7_) | copy-start | bytes 393220
  1.8 15.2 %collective-permute-start = (bf16[128,1024]{1,0:T(8,128)(2,1)S(1)}, bf16[128,1024]{1,0:T(8,128)(2,1)S(1)}, u32[]{:S(2)}, u32[]{:S(2)}) collective-permute-start(bf16[128,1024]{1,0:T(8,128)(2,1)S(1)} %dynamic-slice_bitcast_fusion), channel_id=1, source_target_pairs={{0,6},{2,4},{4,2},{6,0},{1,7},{3,5},{5,3},{7,1},{8,14},{10,12},{12... | collective-permute-start | bytes 786440 | tf_op jit(solution)/shard_map/ppermute | solution.py:319
  7.6 11.5 %collective-permute-start.1 = (bf16[128,1024]{1,0:T(8,128)(2,1)}, bf16[128,1024]{1,0:T(8,128)(2,1)S(1)}, u32[]{:S(2)}, u32[]{:S(2)}) collective-permute-start(bf16[128,1024]{1,0:T(8,128)(2,1)} %get-tuple-element.16), channel_id=1, source_target_pairs={{0,2},{2,0},{4,6},{6,4},{1,3},{3,1},{5,7},{7,5},{8,10},{10,8},{12,... | collective-permute-start | bytes 786440 | tf_op jit(solution)/shard_map/ppermute | solution.py:319
  8.2 10.9 %collective-permute-start.2 = (bf16[128,1024]{1,0:T(8,128)(2,1)}, bf16[128,1024]{1,0:T(8,128)(2,1)S(1)}, u32[]{:S(2)}, u32[]{:S(2)}) collective-permute-start(bf16[128,1024]{1,0:T(8,128)(2,1)} %get-tuple-element.17), channel_id=1, source_target_pairs={{0,4},{2,6},{4,0},{6,2},{1,5},{3,7},{5,1},{7,3},{8,12},{10,14},{12... | collective-permute-start | bytes 786440 | tf_op jit(solution)/shard_map/ppermute | solution.py:319
  13.5 16.6 %collective-permute-start.6 = (bf16[128,1024]{1,0:T(8,128)(2,1)S(1)}, bf16[128,1024]{1,0:T(8,128)(2,1)S(1)}, u32[]{:S(2)}, u32[]{:S(2)}) collective-permute-start(bf16[128,1024]{1,0:T(8,128)(2,1)S(1)} %get-tuple-element.24), channel_id=1, source_target_pairs={{0,2},{2,0},{4,6},{6,4},{1,3},{3,1},{5,7},{7,5},{8,10},{10,8},{12,... | collective-permute-start | bytes 786440 | tf_op jit(solution)/shard_map/ppermute | solution.py:319
  15.5 15.1 %collective-permute-start.7 = (bf16[128,1024]{1,0:T(8,128)(2,1)S(1)}, bf16[128,1024]{1,0:T(8,128)(2,1)S(1)}, u32[]{:S(2)}, u32[]{:S(2)}) collective-permute-start(bf16[128,1024]{1,0:T(8,128)(2,1)S(1)} %get-tuple-element.25), channel_id=1, source_target_pairs={{0,4},{2,6},{4,0},{6,2},{1,5},{3,7},{5,1},{7,3},{8,12},{10,14},{12... | collective-permute-start | bytes 786440 | tf_op jit(solution)/shard_map/ppermute | solution.py:319
  17.0 13.6 %collective-permute-start.8 = (bf16[128,1024]{1,0:T(8,128)(2,1)S(1)}, bf16[128,1024]{1,0:T(8,128)(2,1)S(1)}, u32[]{:S(2)}, u32[]{:S(2)}) collective-permute-start(bf16[128,1024]{1,0:T(8,128)(2,1)S(1)} %get-tuple-element.26), channel_id=1, source_target_pairs={{0,6},{2,4},{4,2},{6,0},{1,7},{3,5},{5,3},{7,1},{8,14},{10,12},{12... | collective-permute-start | bytes 786440 | tf_op jit(solution)/shard_map/ppermute | solution.py:319
  19.1 11.5 %copy-start.2 = (bf16[256,256]{1,0:T(8,128)(2,1)S(1)}, bf16[256,256]{1,0:T(8,128)(2,1)}, u32[]{:S(2)}) copy-start(bf16[256,256]{1,0:T(8,128)(2,1)} %constant.34.clone.refs_8_) | copy-start | bytes 393220
  19.1 11.5 %copy-start.3 = (bf16[256,256]{1,0:T(8,128)(2,1)S(1)}, bf16[256,256]{1,0:T(8,128)(2,1)}, u32[]{:S(2)}) copy-start(bf16[256,256]{1,0:T(8,128)(2,1)} %constant.33.clone.refs_7_) | copy-start | bytes 393220
  27.1 12.1 %collective-permute-start.3 = (bf16[128,1024]{1,0:T(8,128)(2,1)S(1)}, bf16[128,1024]{1,0:T(8,128)(2,1)S(1)}, u32[]{:S(2)}, u32[]{:S(2)}) collective-permute-start(bf16[128,1024]{1,0:T(8,128)(2,1)S(1)} %get-tuple-element.20), channel_id=1, source_target_pairs={{0,6},{2,4},{4,2},{6,0},{1,7},{3,5},{5,3},{7,1},{8,14},{10,12},{12... | collective-permute-start | bytes 786440 | tf_op jit(solution)/shard_map/ppermute | solution.py:319
  28.6 11.9 %collective-permute-start.4 = (bf16[128,1024]{1,0:T(8,128)(2,1)S(1)}, bf16[128,1024]{1,0:T(8,128)(2,1)S(1)}, u32[]{:S(2)}, u32[]{:S(2)}) collective-permute-start(bf16[128,1024]{1,0:T(8,128)(2,1)S(1)} %get-tuple-element.21), channel_id=1, source_target_pairs={{0,4},{2,6},{4,0},{6,2},{1,5},{3,7},{5,1},{7,3},{8,12},{10,14},{12... | collective-permute-start | bytes 786440 | tf_op jit(solution)/shard_map/ppermute | solution.py:319
  30.1 10.6 %collective-permute-start.5 = (bf16[128,1024]{1,0:T(8,128)(2,1)S(1)}, bf16[128,1024]{1,0:T(8,128)(2,1)S(1)}, u32[]{:S(2)}, u32[]{:S(2)}) collective-permute-start(bf16[128,1024]{1,0:T(8,128)(2,1)S(1)} %get-tuple-element.22), channel_id=1, source_target_pairs={{0,2},{2,0},{4,6},{6,4},{1,3},{3,1},{5,7},{7,5},{8,10},{10,8},{12,... | collective-permute-start | bytes 786440 | tf_op jit(solution)/shard_map/ppermute | solution.py:319

commit v6 on v5

--- a/solution.py
+++ b/solution.py
@@ -159,9 +159,11 @@
     work_ref[rows, LANES : 2 * LANES] = im
 
 
-def spectrum_kernel(taps_ref, ahead_high, ahead_low, twiddle_ref, *refs, outer, parts, pencil):
-    *moved, spec_ref = refs[:-6]
-    taps_here, high_here, low_here, twiddle_here, work_ref, sems = refs[-6:]
+def spectrum_kernel(taps_ref, *refs, outer, parts, pencil, tables):
+    table_refs, refs = refs[:tables], refs[tables:]
+    *moved, spec_ref = refs[: -3 - tables]
+    tables_here, (taps_here, work_ref, sems) = refs[-3 - tables : -3], refs[-3:]
+    high_here, low_here, twiddle_here = tables_here[:3]
     count = outer // 2
     steps = taps_ref.shape[0] // TILE
 
@@ -170,18 +172,17 @@
         return pltpu.make_async_copy(taps_ref.at[rows, :], taps_here.at[rows, :], sems.at[step])
 
     copies = [
-        pltpu.make_async_copy(ahead_high, high_here, sems.at[steps]),
-        pltpu.make_async_copy(ahead_low, low_here, sems.at[steps + 1]),
-        pltpu.make_async_copy(twiddle_ref, twiddle_here, sems.at[steps + 2]),
+        pltpu.make_async_copy(table_ref, here, sems.at[steps + at])
+        for at, (table_ref, here) in enumerate(zip(table_refs, tables_here))
     ]
-    later = []
+    copies, later = copies[:3], copies[3:]
     if moved:
         input_ref, grad_ref, *slices, own_grad = moved
         places = places_of("input", parts)
         moves = [(input_ref, *move) for move in zip(places, slices)] + [(grad_ref, places[0], own_grad)]
         for at, (source, place, ref) in enumerate(moves):
             rows = pl.ds(place * pencil, pencil)
-            later.append(pltpu.make_async_copy(source.at[rows, :], ref, sems.at[steps + 3 + at]))
+            later.append(pltpu.make_async_copy(source.at[rows, :], ref, sems.at[steps + tables + at]))
     fetch(0).start()
     for copy in reversed(copies):
         copy.start()
@@ -260,9 +261,14 @@
 
 def filter_kernel(*refs, outer, parts):
     pieces, (mate_ref, *tables) = refs[:parts], refs[parts : parts + 6]
-    result_ref, fill_ref, work_ref, out_ref, result_here, sems = refs[parts + 6 :]
+    *moved, fill_ref, work_ref, out_ref, result_here, sems = refs[parts + 6 :]
+    own_ref, result_ref, whole_ref = moved if len(moved) == 3 else (None, *moved, None)
     places = places_of("input", parts)
     steps = pieces[0].shape[0] // TILE
+    if own_ref is not None:
+        rows = pl.ds(places[0] * own_ref.shape[0], own_ref.shape[0])
+        own_copy = pltpu.make_async_copy(own_ref, whole_ref.at[rows, :], sems.at[steps])
+        own_copy.start()
 
     def flush(step):
         rows = pl.ds(pl.multiple_of(step * TILE, TILE), TILE)
@@ -279,6 +285,9 @@
     @pl.loop(0, steps)
     def _(step):
         flush(step).wait()
+
+    if own_ref is not None:
+        own_copy.wait()
 
 
 def slice_kernel(source_ref, *refs, parts, pencil):
@@ -293,10 +302,10 @@
         copy.wait()
 
 
-def gather_kernel(*refs, pencil):
+def gather_kernel(held_ref, *refs, pencil):
     *pieces, out_ref, sems = refs
     copies = []
-    for place, ref in zip(places_of("back", len(pieces)), pieces):
+    for place, ref in zip(places_of("back", len(pieces) + 1)[1:], pieces):
         rows = pl.ds(place * pencil, pencil)
         copies.append(pltpu.make_async_copy(ref, out_ref.at[rows, :], sems.at[len(copies)]))
     for copy in copies:
@@ -357,24 +366,24 @@
     grad_pieces = exchange("grad", [pick(grad_output, others[0]), *blocks])
 
     taps = filter_taps.reshape(pencil, length)
-    tables = [*ahead, twiddle]
+    tables = [*ahead, twiddle, *back, *back_scaled]
     slices = parts + 1 if aligned else 0
     results = pl.pallas_call(
-        functools.partial(spectrum_kernel, outer=outer, parts=parts, pencil=pencil),
-        in_specs=[there] * (6 if aligned else 4),
-        out_specs=[here] * (slices + 1),
-        out_shape=[slice_shape] * slices + [spec_shape],
+        functools.partial(spectrum_kernel, outer=outer, parts=parts, pencil=pencil, tables=len(tables)),
+        in_specs=[there] * (1 + len(tables) + (2 if aligned else 0)),
+        out_specs=[here] * (slices + 1 + len(tables)),
+        out_shape=[slice_shape] * slices + [spec_shape] + [jax.ShapeDtypeStruct(table.shape, table.dtype) for table in tables],
         scratch_shapes=[
             pltpu.VMEM((rows, length), jnp.float32),
-            *[pltpu.VMEM(table.shape, table.dtype) for table in tables],
             work,
-            pltpu.SemaphoreType.DMA((steps + 3 + slices,)),
+            pltpu.SemaphoreType.DMA((steps + len(tables) + slices,)),
         ],
         compiler_params=params,
         cost_estimate=cost(1, 2 * spec_bytes),
         name="taps_spectrum",
     )(*map(in_hbm, [pad(taps), *map(jnp.asarray, tables), *([layer_input, grad_output] if aligned else [])]))
-    taps_spectrum = results[-1]
+    taps_spectrum, *tables = results[slices:]
+    ahead, twiddle, back, back_scaled = tables[:2], tables[2], tables[3:5], tables[5:]
     blocks = results[:parts] if aligned else [pick(layer_input, place) for place in places_of("input", parts)]
     grad_pieces = [results[parts] if aligned else pick(grad_output, own), *grad_pieces]
     input_pieces = [blocks[0], *exchange("input", blocks[1:])]
@@ -395,32 +404,35 @@
     incoming = [outgoing[0], *exchange("back", outgoing[1:])]
 
     tables = [*ahead, *back_scaled, twiddle]
-    grad_filter = pl.pallas_call(
+    filter_shape = jax.ShapeDtypeStruct((rows, length), jnp.float32)
+    whole_shape = jax.ShapeDtypeStruct((parts * pencil, piece), jnp.bfloat16)
+    grad_filter, *whole = pl.pallas_call(
         functools.partial(filter_kernel, outer=outer, parts=parts),
-        in_specs=[here] * (parts + 1 + len(tables)),
-        out_specs=there,
-        out_shape=jax.ShapeDtypeStruct((rows, length), jnp.float32),
+        in_specs=[here] * (parts + 1 + len(tables) + aligned),
+        out_specs=[there] * (1 + aligned),
+        out_shape=[filter_shape, whole_shape][: 1 + aligned],
         scratch_shapes=[
             lane_tiles,
             work,
             lane_tiles,
             pltpu.VMEM((rows, length), jnp.float32),
-            pltpu.SemaphoreType.DMA((steps,)),
+            pltpu.SemaphoreType.DMA((steps + aligned,)),
         ],
         compiler_params=params,
         cost_estimate=cost(2, 2 * spec_bytes),
         name="grad_filter",
-    )(*map(pad, input_pieces), grad_spectrum, *tables)
+    )(*map(pad, input_pieces), grad_spectrum, *tables, *incoming[:aligned])
 
     if aligned:
         grad_input = pl.pallas_call(
             functools.partial(gather_kernel, pencil=pencil),
             in_specs=[there] * parts,
             out_specs=there,
-            out_shape=jax.ShapeDtypeStruct((parts * pencil, piece), jnp.bfloat16),
-            scratch_shapes=[pltpu.SemaphoreType.DMA((parts,))],
+            out_shape=whole_shape,
+            input_output_aliases={0: 0},
+            scratch_shapes=[pltpu.SemaphoreType.DMA((parts - 1,))],
             name="gather_pieces",
-        )(*[pltpu.with_memory_space_constraint(block, pltpu.VMEM) for block in incoming])
+        )(*whole, *[pltpu.with_memory_space_constraint(block, pltpu.VMEM) for block in incoming[1:]])
     else:
         grad_input = jnp.zeros((parts, pencil, piece), jnp.bfloat16)
         for place, block in zip(places_of("back", parts), incoming):

time: 41.9 us -> 41.6 us (level)
  transfers between devices with their start and end apart: 9 -> 9, of which waited for: 3 -> 3; matrix products, arithmetic and copies ran while one was open for 0% -> 0% of each run, Pallas kernels for 56% -> 57%
where the time goes in v6:
time: 41.6 us; the launch traced here: 41.4 us
  Pallas kernels  24.4 us (59%)
  starting transfers between devices  11.7 us (28%)
  waiting for transfers between devices  3.59 us (9%)
  local copies, waits for them, and re-layouts  0.97 us (2%)
  between operations  0.69 us (2%)
    ppermute x9, starting transfers between devices, exchange(): lax.ppermute(block, 'ctx', pair)  11.7 us
    pallas_call x1, Pallas kernels, shards(): pl.pallas_call(functools.partial(filter_kernel, outer=outer, parts=parts)...  8.46 us
    pallas_call x1, Pallas kernels, shards(): pl.pallas_call(functools.partial(input_kernel, outer=outer, parts=parts),...  7.88 us
    pallas_call x1, Pallas kernels, shards(): pl.pallas_call(functools.partial(spectrum_kernel, outer=outer, parts=part...  5.34 us
    ppermute x9, waiting for transfers between devices, exchange(): lax.ppermute(block, 'ctx', pair)  3.59 us
    pallas_call x1, Pallas kernels, shards(): pl.pallas_call(functools.partial(slice_kernel, parts=parts, pencil=pencil...  1.83 us
    squeeze x1, local copies, waits for them, and re-layouts, pick(): return lax.dynamic_index_in_dim(blocks, place, 0, keepdims=False)  0.97 us
    pallas_call x1, Pallas kernels, shards(): pl.pallas_call(functools.partial(gather_kernel, pencil=pencil), in_specs=...  0.9 us
  transfers between devices with their start and end apart: 9, of which 3 were waited for; matrix products, arithmetic and copies ran while one was open for 0% of the time, Pallas kernels for 57%

profile of v6, /device:TPU:0, one launch (start us, length us, event | category | flops | bytes accessed | tf_op | source)
XLA Modules:
  0.0 41.4 jit_solution(13930134319968927716)
XLA Ops:
  0.6 1.0 %dynamic-slice_bitcast_fusion = bf16[128,1024]{1,0:T(8,128)(2,1)S(1)} fusion(bf16[4,128,1024]{2,1,0:T(8,128)(2,1)} %bitcast.5, s32[]{:T(128)S(6)} %select_n.4), kind=kLoop, calls=%fused_computation | loop fusion | bytes 524292 | tf_op jit(solution)/shard_map/jit(dynamic_index_in_dim)/squeeze | solution.py:332
  1.6 4.0 %collective-permute-start.3 = (bf16[128,1024]{1,0:T(8,128)(2,1)S(1)}, bf16[128,1024]{1,0:T(8,128)(2,1)S(1)}, u32[]{:S(2)}, u32[]{:S(2)}) collective-permute-start(bf16[128,1024]{1,0:T(8,128)(2,1)S(1)} %dynamic-slice_bitcast_fusion), channel_id=1, source_target_pairs={{0,6},{2,4},{4,2},{6,0},{1,7},{3,5},{5,3},{7,1},{8,14},{10,12},{12... | collective-permute-start | bytes 786440 | tf_op jit(solution)/shard_map/ppermute | solution.py:328
  5.6 1.8 %slice_grad.1 = (bf16[128,1024]{1,0:T(8,128)(2,1)}, bf16[128,1024]{1,0:T(8,128)(2,1)}) custom-call(bf16[512,1024]{1,0:T(8,128)(2,1)} %source_ref.1), custom_call_target="tpu_custom_call" | custom-call | bytes 1048576 | tf_op jit(solution)/shard_map/slice_grad/pallas_call | solution.py:355
  7.4 0.6 %collective-permute-start.4 = (bf16[128,1024]{1,0:T(8,128)(2,1)}, bf16[128,1024]{1,0:T(8,128)(2,1)S(1)}, u32[]{:S(2)}, u32[]{:S(2)}) collective-permute-start(bf16[128,1024]{1,0:T(8,128)(2,1)} %get-tuple-element.29), channel_id=1, source_target_pairs={{0,2},{2,0},{4,6},{6,4},{1,3},{3,1},{5,7},{7,5},{8,10},{10,8},{12,... | collective-permute-start | bytes 786440 | tf_op jit(solution)/shard_map/ppermute | solution.py:328
  8.0 0.1 collective-permute-start.5
  8.1 5.3 %taps_spectrum.1 = (bf16[128,1024]{1,0:T(8,128)(2,1)S(1)}, bf16[128,1024]{1,0:T(8,128)(2,1)S(1)}, bf16[128,1024]{1,0:T(8,128)(2,1)S(1)}, bf16[128,1024]{1,0:T(8,...) custom-call(f32[128,4096]{1,0:T(8,128)} %bitcast.6, ...), custom_call_target="tpu_custom_call" | custom-call | flops 1610612736 | bytes 8388608 | tf_op jit(solution)/shard_map/taps_spectrum/pallas_call | solution.py:371
  13.4 2.0 %collective-permute-start = (bf16[128,1024]{1,0:T(8,128)(2,1)S(1)}, bf16[128,1024]{1,0:T(8,128)(2,1)S(1)}, u32[]{:S(2)}, u32[]{:S(2)}) collective-permute-start(bf16[128,1024]{1,0:T(8,128)(2,1)S(1)} %get-tuple-element.25), channel_id=1, source_target_pairs={{0,2},{2,0},{4,6},{6,4},{1,3},{3,1},{5,7},{7,5},{8,10},{10,8},{12,... | collective-permute-start | bytes 786440 | tf_op jit(solution)/shard_map/ppermute | solution.py:328
  15.4 1.5 %collective-permute-start.1 = (bf16[128,1024]{1,0:T(8,128)(2,1)S(1)}, bf16[128,1024]{1,0:T(8,128)(2,1)S(1)}, u32[]{:S(2)}, u32[]{:S(2)}) collective-permute-start(bf16[128,1024]{1,0:T(8,128)(2,1)S(1)} %get-tuple-element.26), channel_id=1, source_target_pairs={{0,4},{2,6},{4,0},{6,2},{1,5},{3,7},{5,1},{7,3},{8,12},{10,14},{12... | collective-permute-start | bytes 786440 | tf_op jit(solution)/shard_map/ppermute | solution.py:328
  16.9 0.0 collective-permute-done.3.refs_1_
  16.9 0.0 collective-permute-start.2
  17.0 2.0 %collective-permute-done.4.refs_2_ = bf16[128,1024]{1,0:T(8,128)(2,1)S(1)} collective-permute-done((bf16[128,1024]{1,0:T(8,128)(2,1)}, bf16[128,1024]{1,0:T(8,128)(2,1)S(1)}, u32[]{:S(2)}, u32[]{:S(2)}) %collective-permute-start.4) | collective-permute-done | bytes 262176 | tf_op jit(solution)/shard_map/ppermute | solution.py:328
  18.9 0.0 collective-permute-done.5.refs_3_
  18.9 7.9 %grad_input.1 = (f32[8,512,256]{2,1,0:T(8,128)S(1)}, bf16[128,1024]{1,0:T(8,128)(2,1)S(1)}, bf16[128,1024]{1,0:T(8,128)(2,1)S(1)}, bf16[128,1024]{1,0:T(8,128)(2,1)S(1)}, bf16[128,1024]{1,0:T(8,128)(2,1)S(1)}) custom-call(bf16[128,1024]{1,0:T(8,128)(2,1)S(1)} %get-tuple-element.28.refs_0_, bf16[128,1024]{1,0:T(8,128)(2,1)S(1)} %collective-permute-done.3.refs_1_, ...), custom_call_target="tpu_custom_call" | custom-call | flops 3221225472 | bytes 8388608 | tf_op jit(solution)/shard_map/grad_input/pallas_call | solution.py:392
  26.8 1.5 %collective-permute-start.6 = (bf16[128,1024]{1,0:T(8,128)(2,1)S(1)}, bf16[128,1024]{1,0:T(8,128)(2,1)S(1)}, u32[]{:S(2)}, u32[]{:S(2)}) collective-permute-start(bf16[128,1024]{1,0:T(8,128)(2,1)S(1)} %get-tuple-element.42), channel_id=1, source_target_pairs={{0,6},{2,4},{4,2},{6,0},{1,7},{3,5},{5,3},{7,1},{8,14},{10,12},{12... | collective-permute-start | bytes 786440 | tf_op jit(solution)/shard_map/ppermute | solution.py:328
  28.3 1.5 %collective-permute-start.7 = (bf16[128,1024]{1,0:T(8,128)(2,1)S(1)}, bf16[128,1024]{1,0:T(8,128)(2,1)S(1)}, u32[]{:S(2)}, u32[]{:S(2)}) collective-permute-start(bf16[128,1024]{1,0:T(8,128)(2,1)S(1)} %get-tuple-element.43), channel_id=1, source_target_pairs={{0,4},{2,6},{4,0},{6,2},{1,5},{3,7},{5,1},{7,3},{8,12},{10,14},{12... | collective-permute-start | bytes 786440 | tf_op jit(solution)/shard_map/ppermute | solution.py:328
  29.9 0.0 collective-permute-done.refs_1_
  29.9 0.5 %collective-permute-start.8 = (bf16[128,1024]{1,0:T(8,128)(2,1)S(1)}, bf16[128,1024]{1,0:T(8,128)(2,1)S(1)}, u32[]{:S(2)}, u32[]{:S(2)}) collective-permute-start(bf16[128,1024]{1,0:T(8,128)(2,1)S(1)} %get-tuple-element.44), channel_id=1, source_target_pairs={{0,2},{2,0},{4,6},{6,4},{1,3},{3,1},{5,7},{7,5},{8,10},{10,8},{12,... | collective-permute-start | bytes 786440 | tf_op jit(solution)/shard_map/ppermute | solution.py:328
  30.4 0.0 collective-permute-done.1.refs_2_
  30.4 0.0 collective-permute-done.2.refs_3_
  30.4 8.5 %grad_filter.1 = (f32[128,4096]{1,0:T(8,128)}, bf16[512,1024]{1,0:T(8,128)(2,1)}) custom-call(bf16[128,1024]{1,0:T(8,128)(2,1)S(1)} %get-tuple-element.24.refs_0_, bf16[128,1024]{1,0:T(8,128)(2,1)S(1)} %collective-permute-done.refs_1_, bf16[128,1024]{1,0:T(8,128)(2,1)S(1)} %collective-permute-done.1.refs_2_, ...), custom_call_target="tpu_custom_call" | custom-call | flops 3221225472 | bytes 8388608 | tf_op jit(solution)/shard_map/grad_filter/pallas_call | solution.py:409
  38.9 0.0 collective-permute-done.6.refs_0_
  38.9 1.4 %collective-permute-done.7.refs_1_ = bf16[128,1024]{1,0:T(8,128)(2,1)S(1)} collective-permute-done((bf16[128,1024]{1,0:T(8,128)(2,1)S(1)}, bf16[128,1024]{1,0:T(8,128)(2,1)S(1)}, u32[]{:S(2)}, u32[]{:S(2)}) %collective-permute-start.7) | collective-permute-done | bytes 262176 | tf_op jit(solution)/shard_map/ppermute | solution.py:328
  40.2 0.2 collective-permute-done.8.refs_2_
  40.5 0.9 %gather_pieces.1 = bf16[512,1024]{1,0:T(8,128)(2,1)} custom-call(bf16[512,1024]{1,0:T(8,128)(2,1)} %get-tuple-element.41.held_ref, bf16[128,1024]{1,0:T(8,128)(2,1)S(1)} %collective-permute-done.6.refs_0_, bf16[128,1024]{1,0:T(8,128)(2,1)S(1)} %collective-permute-done.7.refs_1_, ...), custom_call_target="tpu_custom_call", output_to_operand_aliasing={{}: (0, {})} | custom-call | tf_op jit(solution)/shard_map/gather_pieces/pallas_call | solution.py:427
Async XLA Ops:
  1.6 15.3 %collective-permute-start.3 = (bf16[128,1024]{1,0:T(8,128)(2,1)S(1)}, bf16[128,1024]{1,0:T(8,128)(2,1)S(1)}, u32[]{:S(2)}, u32[]{:S(2)}) collective-permute-start(bf16[128,1024]{1,0:T(8,128)(2,1)S(1)} %dynamic-slice_bitcast_fusion), channel_id=1, source_target_pairs={{0,6},{2,4},{4,2},{6,0},{1,7},{3,5},{5,3},{7,1},{8,14},{10,12},{12... | collective-permute-start | bytes 786440 | tf_op jit(solution)/shard_map/ppermute | solution.py:328
  7.4 11.5 %collective-permute-start.4 = (bf16[128,1024]{1,0:T(8,128)(2,1)}, bf16[128,1024]{1,0:T(8,128)(2,1)S(1)}, u32[]{:S(2)}, u32[]{:S(2)}) collective-permute-start(bf16[128,1024]{1,0:T(8,128)(2,1)} %get-tuple-element.29), channel_id=1, source_target_pairs={{0,2},{2,0},{4,6},{6,4},{1,3},{3,1},{5,7},{7,5},{8,10},{10,8},{12,... | collective-permute-start | bytes 786440 | tf_op jit(solution)/shard_map/ppermute | solution.py:328
  8.0 10.9 %collective-permute-start.5 = (bf16[128,1024]{1,0:T(8,128)(2,1)}, bf16[128,1024]{1,0:T(8,128)(2,1)S(1)}, u32[]{:S(2)}, u32[]{:S(2)}) collective-permute-start(bf16[128,1024]{1,0:T(8,128)(2,1)} %get-tuple-element.30), channel_id=1, source_target_pairs={{0,4},{2,6},{4,0},{6,2},{1,5},{3,7},{5,1},{7,3},{8,12},{10,14},{12... | collective-permute-start | bytes 786440 | tf_op jit(solution)/shard_map/ppermute | solution.py:328
  13.4 16.4 %collective-permute-start = (bf16[128,1024]{1,0:T(8,128)(2,1)S(1)}, bf16[128,1024]{1,0:T(8,128)(2,1)S(1)}, u32[]{:S(2)}, u32[]{:S(2)}) collective-permute-start(bf16[128,1024]{1,0:T(8,128)(2,1)S(1)} %get-tuple-element.25), channel_id=1, source_target_pairs={{0,2},{2,0},{4,6},{6,4},{1,3},{3,1},{5,7},{7,5},{8,10},{10,8},{12,... | collective-permute-start | bytes 786440 | tf_op jit(solution)/shard_map/ppermute | solution.py:328
  15.4 15.0 %collective-permute-start.1 = (bf16[128,1024]{1,0:T(8,128)(2,1)S(1)}, bf16[128,1024]{1,0:T(8,128)(2,1)S(1)}, u32[]{:S(2)}, u32[]{:S(2)}) collective-permute-start(bf16[128,1024]{1,0:T(8,128)(2,1)S(1)} %get-tuple-element.26), channel_id=1, source_target_pairs={{0,4},{2,6},{4,0},{6,2},{1,5},{3,7},{5,1},{7,3},{8,12},{10,14},{12... | collective-permute-start | bytes 786440 | tf_op jit(solution)/shard_map/ppermute | solution.py:328
  16.9 13.4 %collective-permute-start.2 = (bf16[128,1024]{1,0:T(8,128)(2,1)S(1)}, bf16[128,1024]{1,0:T(8,128)(2,1)S(1)}, u32[]{:S(2)}, u32[]{:S(2)}) collective-permute-start(bf16[128,1024]{1,0:T(8,128)(2,1)S(1)} %get-tuple-element.27), channel_id=1, source_target_pairs={{0,6},{2,4},{4,2},{6,0},{1,7},{3,5},{5,3},{7,1},{8,14},{10,12},{12... | collective-permute-start | bytes 786440 | tf_op jit(solution)/shard_map/ppermute | solution.py:328
  26.8 12.0 %collective-permute-start.6 = (bf16[128,1024]{1,0:T(8,128)(2,1)S(1)}, bf16[128,1024]{1,0:T(8,128)(2,1)S(1)}, u32[]{:S(2)}, u32[]{:S(2)}) collective-permute-start(bf16[128,1024]{1,0:T(8,128)(2,1)S(1)} %get-tuple-element.42), channel_id=1, source_target_pairs={{0,6},{2,4},{4,2},{6,0},{1,7},{3,5},{5,3},{7,1},{8,14},{10,12},{12... | collective-permute-start | bytes 786440 | tf_op jit(solution)/shard_map/ppermute | solution.py:328
  28.3 11.9 %collective-permute-start.7 = (bf16[128,1024]{1,0:T(8,128)(2,1)S(1)}, bf16[128,1024]{1,0:T(8,128)(2,1)S(1)}, u32[]{:S(2)}, u32[]{:S(2)}) collective-permute-start(bf16[128,1024]{1,0:T(8,128)(2,1)S(1)} %get-tuple-element.43), channel_id=1, source_target_pairs={{0,4},{2,6},{4,0},{6,2},{1,5},{3,7},{5,1},{7,3},{8,12},{10,14},{12... | collective-permute-start | bytes 786440 | tf_op jit(solution)/shard_map/ppermute | solution.py:328
  29.9 10.6 %collective-permute-start.8 = (bf16[128,1024]{1,0:T(8,128)(2,1)S(1)}, bf16[128,1024]{1,0:T(8,128)(2,1)S(1)}, u32[]{:S(2)}, u32[]{:S(2)}) collective-permute-start(bf16[128,1024]{1,0:T(8,128)(2,1)S(1)} %get-tuple-element.44), channel_id=1, source_target_pairs={{0,2},{2,0},{4,6},{6,4},{1,3},{3,1},{5,7},{7,5},{8,10},{10,8},{12,... | collective-permute-start | bytes 786440 | tf_op jit(solution)/shard_map/ppermute | solution.py:328

commit v7 on v6

--- a/solution.py
+++ b/solution.py
@@ -159,10 +159,9 @@
     work_ref[rows, LANES : 2 * LANES] = im
 
 
-def spectrum_kernel(taps_ref, *refs, outer, parts, pencil, tables):
-    table_refs, refs = refs[:tables], refs[tables:]
-    *moved, spec_ref = refs[: -3 - tables]
-    tables_here, (taps_here, work_ref, sems) = refs[-3 - tables : -3], refs[-3:]
+def spectrum_kernel(taps_ref, *refs, outer, tables):
+    table_refs, spec_ref, tables_here = refs[:tables], refs[tables], refs[tables + 1 : -3]
+    taps_here, work_ref, sems = refs[-3:]
     high_here, low_here, twiddle_here = tables_here[:3]
     count = outer // 2
     steps = taps_ref.shape[0] // TILE
@@ -176,13 +175,6 @@
         for at, (table_ref, here) in enumerate(zip(table_refs, tables_here))
     ]
     copies, later = copies[:3], copies[3:]
-    if moved:
-        input_ref, grad_ref, *slices, own_grad = moved
-        places = places_of("input", parts)
-        moves = [(input_ref, *move) for move in zip(places, slices)] + [(grad_ref, places[0], own_grad)]
-        for at, (source, place, ref) in enumerate(moves):
-            rows = pl.ds(place * pencil, pencil)
-            later.append(pltpu.make_async_copy(source.at[rows, :], ref, sems.at[steps + tables + at]))
     fetch(0).start()
     for copy in reversed(copies):
         copy.start()
@@ -290,10 +282,13 @@
         own_copy.wait()
 
 
-def slice_kernel(source_ref, *refs, parts, pencil):
+def slice_kernel(grad_ref, input_ref, *refs, parts, pencil):
     *blocks, sems = refs
+    grad_places, input_places = places_of("grad", parts), places_of("input", parts)
+    moves = [(grad_ref, place) for place in grad_places[2:] + grad_places[:1]]
+    moves += [(input_ref, place) for place in input_places]
     copies = []
-    for place, ref in zip(places_of("grad", parts)[2:], blocks):
+    for (source_ref, place), ref in zip(moves, blocks):
         rows = pl.ds(place * pencil, pencil)
         copies.append(pltpu.make_async_copy(source_ref.at[rows, :], ref, sems.at[len(copies)]))
     for copy in copies:
@@ -302,10 +297,10 @@
         copy.wait()
 
 
-def gather_kernel(held_ref, *refs, pencil):
+def gather_kernel(held_ref, *refs, first, parts, pencil):
     *pieces, out_ref, sems = refs
     copies = []
-    for place, ref in zip(places_of("back", len(pieces) + 1)[1:], pieces):
+    for place, ref in zip(places_of("back", parts)[first:], pieces):
         rows = pl.ds(place * pencil, pencil)
         copies.append(pltpu.make_async_copy(ref, out_ref.at[rows, :], sems.at[len(copies)]))
     for copy in copies:
@@ -352,42 +347,41 @@
 
     own, *others = places_of("grad", parts)
     if aligned:
+        count = 2 * parts - 1
         blocks = pl.pallas_call(
             functools.partial(slice_kernel, parts=parts, pencil=pencil),
-            in_specs=[there],
-            out_specs=[here] * (parts - 2),
-            out_shape=[slice_shape] * (parts - 2),
-            scratch_shapes=[pltpu.SemaphoreType.DMA((parts - 2,))],
-            cost_estimate=cost(0, 2 * (parts - 2) * pencil * piece * 2),
-            name="slice_grad",
-        )(in_hbm(grad_output))
+            in_specs=[there] * 2,
+            out_specs=[here] * count,
+            out_shape=[slice_shape] * count,
+            scratch_shapes=[pltpu.SemaphoreType.DMA((count,))],
+            cost_estimate=cost(0, 2 * count * pencil * piece * 2),
+            name="slice_blocks",
+        )(in_hbm(grad_output), in_hbm(layer_input))
     else:
-        blocks = [pick(grad_output, place) for place in others[1:]]
-    grad_pieces = exchange("grad", [pick(grad_output, others[0]), *blocks])
+        blocks = [pick(grad_output, place) for place in [*others[1:], own]]
+        blocks += [pick(layer_input, place) for place in places_of("input", parts)]
+    grad_blocks, input_blocks = blocks[: parts - 1], blocks[parts - 1 :]
+    grad_pieces = [grad_blocks[-1], *exchange("grad", [pick(grad_output, others[0]), *grad_blocks[:-1]])]
+    input_pieces = [input_blocks[0], *exchange("input", input_blocks[1:])]
 
     taps = filter_taps.reshape(pencil, length)
     tables = [*ahead, twiddle, *back, *back_scaled]
-    slices = parts + 1 if aligned else 0
     results = pl.pallas_call(
-        functools.partial(spectrum_kernel, outer=outer, parts=parts, pencil=pencil, tables=len(tables)),
-        in_specs=[there] * (1 + len(tables) + (2 if aligned else 0)),
-        out_specs=[here] * (slices + 1 + len(tables)),
-        out_shape=[slice_shape] * slices + [spec_shape] + [jax.ShapeDtypeStruct(table.shape, table.dtype) for table in tables],
+        functools.partial(spectrum_kernel, outer=outer, tables=len(tables)),
+        in_specs=[there] * (1 + len(tables)),
+        out_specs=[here] * (1 + len(tables)),
+        out_shape=[spec_shape] + [jax.ShapeDtypeStruct(table.shape, table.dtype) for table in tables],
         scratch_shapes=[
             pltpu.VMEM((rows, length), jnp.float32),
             work,
-            pltpu.SemaphoreType.DMA((steps + len(tables) + slices,)),
+            pltpu.SemaphoreType.DMA((steps + len(tables),)),
         ],
         compiler_params=params,
         cost_estimate=cost(1, 2 * spec_bytes),
         name="taps_spectrum",
-    )(*map(in_hbm, [pad(taps), *map(jnp.asarray, tables), *([layer_input, grad_output] if aligned else [])]))
-    taps_spectrum, *tables = results[slices:]
+    )(*map(in_hbm, [pad(taps), *map(jnp.asarray, tables)]))
+    taps_spectrum, *tables = results
     ahead, twiddle, back, back_scaled = tables[:2], tables[2], tables[3:5], tables[5:]
-    blocks = results[:parts] if aligned else [pick(layer_input, place) for place in places_of("input", parts)]
-    grad_pieces = [results[parts] if aligned else pick(grad_output, own), *grad_pieces]
-    input_pieces = [blocks[0], *exchange("input", blocks[1:])]
-
     tables = [*ahead, *back, twiddle]
     grad_spectrum, *outgoing = pl.pallas_call(
         functools.partial(input_kernel, outer=outer, parts=parts),
@@ -424,15 +418,18 @@
     )(*map(pad, input_pieces), grad_spectrum, *tables, *incoming[:aligned])
 
     if aligned:
-        grad_input = pl.pallas_call(
-            functools.partial(gather_kernel, pencil=pencil),
-            in_specs=[there] * parts,
-            out_specs=there,
-            out_shape=whole_shape,
-            input_output_aliases={0: 0},
-            scratch_shapes=[pltpu.SemaphoreType.DMA((parts - 1,))],
-            name="gather_pieces",
-        )(*whole, *[pltpu.with_memory_space_constraint(block, pltpu.VMEM) for block in incoming[1:]])
+        (grad_input,) = whole
+        for first, last in ((1, 2), (2, parts)):
+            blocks = [pltpu.with_memory_space_constraint(block, pltpu.VMEM) for block in incoming[first:last]]
+            grad_input = pl.pallas_call(
+                functools.partial(gather_kernel, first=first, parts=parts, pencil=pencil),
+                in_specs=[there] * (1 + len(blocks)),
+                out_specs=there,
+                out_shape=whole_shape,
+                input_output_aliases={0: 0},
+                scratch_shapes=[pltpu.SemaphoreType.DMA((len(blocks),))],
+                name="gather_pieces",
+            )(grad_input, *blocks)
     else:
         grad_input = jnp.zeros((parts, pencil, piece), jnp.bfloat16)
         for place, block in zip(places_of("back", parts), incoming):

time: 41.6 us -> 41.4 us (level)
  waiting for transfers between devices: 3.59 us -> 1.86 us
  Pallas kernels: 24.4 us -> 25.9 us
    ppermute x9, waiting for transfers between devices: 3.59 us -> 1.86 us  [exchange(): lax.ppermute(block, 'ctx', pair)]
    pallas_call x1, Pallas kernels: 1.83 us -> 2.72 us  [shards(): pl.pallas_call(functools.partial(slice_kernel, parts=parts, pencil=pencil...]
    pallas_call x2 -> x3, Pallas kernels: 6.24 us -> 6.8 us  [the longest x1 5.27 us: shards(): pl.pallas_call(functools.partial(spectrum_kernel, outer=outer, tables=len...]
  transfers between devices with their start and end apart: 9 -> 9, of which waited for: 3 -> 3; matrix products, arithmetic and copies ran while one was open for 0% -> 0% of each run, Pallas kernels for 57% -> 61%
where the time goes in v7:
time: 41.4 us; the launch traced here: 41.2 us
  Pallas kernels  25.9 us (63%)
  starting transfers between devices  11.7 us (28%)
  waiting for transfers between devices  1.86 us (4%)
  local copies, waits for them, and re-layouts  0.98 us (2%)
  between operations  0.74 us (2%)
    ppermute x9, starting transfers between devices, exchange(): lax.ppermute(block, 'ctx', pair)  11.7 us
    pallas_call x1, Pallas kernels, shards(): pl.pallas_call(functools.partial(filter_kernel, outer=outer, parts=parts)...  8.48 us
    pallas_call x1, Pallas kernels, shards(): pl.pallas_call(functools.partial(input_kernel, outer=outer, parts=parts),...  7.89 us
    pallas_call x1, Pallas kernels, shards(): pl.pallas_call(functools.partial(spectrum_kernel, outer=outer, tables=len...  5.27 us
    pallas_call x1, Pallas kernels, shards(): pl.pallas_call(functools.partial(slice_kernel, parts=parts, pencil=pencil...  2.72 us
    ppermute x9, waiting for transfers between devices, exchange(): lax.ppermute(block, 'ctx', pair)  1.86 us
    pallas_call x2, Pallas kernels, shards(): pl.pallas_call(functools.partial(gather_kernel, first=first, parts=parts,...  1.53 us
    squeeze x1, local copies, waits for them, and re-layouts, pick(): return lax.dynamic_index_in_dim(blocks, place, 0, keepdims=False)  0.97 us
  transfers between devices with their start and end apart: 9, of which 3 were waited for; matrix products, arithmetic and copies ran while one was open for 0% of the time, Pallas kernels for 61%

profile of v7, /device:TPU:0, one launch (start us, length us, event | category | flops | bytes accessed | tf_op | source)
XLA Modules:
  0.0 41.2 jit_solution(12729437854214125723)
XLA Ops:
  0.6 1.0 %dynamic-slice_bitcast_fusion = bf16[128,1024]{1,0:T(8,128)(2,1)S(1)} fusion(bf16[4,128,1024]{2,1,0:T(8,128)(2,1)} %bitcast.5, s32[]{:T(128)S(6)} %select_n.4), kind=kLoop, calls=%fused_computation | loop fusion | bytes 524292 | tf_op jit(solution)/shard_map/jit(dynamic_index_in_dim)/squeeze | solution.py:327
  1.6 4.0 %collective-permute-start.3 = (bf16[128,1024]{1,0:T(8,128)(2,1)S(1)}, bf16[128,1024]{1,0:T(8,128)(2,1)S(1)}, u32[]{:S(2)}, u32[]{:S(2)}) collective-permute-start(bf16[128,1024]{1,0:T(8,128)(2,1)S(1)} %dynamic-slice_bitcast_fusion), channel_id=1, source_target_pairs={{0,6},{2,4},{4,2},{6,0},{1,7},{3,5},{5,3},{7,1},{8,14},{10,12},{12... | collective-permute-start | bytes 786440 | tf_op jit(solution)/shard_map/ppermute | solution.py:323
  5.6 2.7 %slice_blocks.1 = (bf16[128,1024]{1,0:T(8,128)(2,1)}, bf16[128,1024]{1,0:T(8,128)(2,1)}, bf16[128,1024]{1,0:T(8,128)(2,1)}, bf16[128,1024]{1,0:T(8,128)(2,1)}, b...) custom-call(bf16[512,1024]{1,0:T(8,128)(2,1)} %grad_ref.1, bf16[512,1024]{1,0:T(8,128)(2,1)} %input_ref.1), custom_call_target="tpu_custom_call" | custom-call | bytes 3670016 | tf_op jit(solution)/shard_map/slice_blocks/pallas_call | solution.py:351
  8.3 0.0 copy-start.2
  8.3 0.0 copy-start.1
  8.3 0.6 %collective-permute-start.4 = (bf16[128,1024]{1,0:T(8,128)(2,1)}, bf16[128,1024]{1,0:T(8,128)(2,1)S(1)}, u32[]{:S(2)}, u32[]{:S(2)}) collective-permute-start(bf16[128,1024]{1,0:T(8,128)(2,1)} %get-tuple-element.29), channel_id=1, source_target_pairs={{0,2},{2,0},{4,6},{6,4},{1,3},{3,1},{5,7},{7,5},{8,10},{10,8},{12,... | collective-permute-start | bytes 786440 | tf_op jit(solution)/shard_map/ppermute | solution.py:323
  8.9 0.1 collective-permute-start.5
  9.0 1.9 %collective-permute-start = (bf16[128,1024]{1,0:T(8,128)(2,1)}, bf16[128,1024]{1,0:T(8,128)(2,1)S(1)}, u32[]{:S(2)}, u32[]{:S(2)}) collective-permute-start(bf16[128,1024]{1,0:T(8,128)(2,1)} %get-tuple-element.25), channel_id=1, source_target_pairs={{0,2},{2,0},{4,6},{6,4},{1,3},{3,1},{5,7},{7,5},{8,10},{10,8},{12,... | collective-permute-start | bytes 786440 | tf_op jit(solution)/shard_map/ppermute | solution.py:323
  10.9 1.5 %collective-permute-start.1 = (bf16[128,1024]{1,0:T(8,128)(2,1)}, bf16[128,1024]{1,0:T(8,128)(2,1)S(1)}, u32[]{:S(2)}, u32[]{:S(2)}) collective-permute-start(bf16[128,1024]{1,0:T(8,128)(2,1)} %get-tuple-element.26), channel_id=1, source_target_pairs={{0,4},{2,6},{4,0},{6,2},{1,5},{3,7},{5,1},{7,3},{8,12},{10,14},{12... | collective-permute-start | bytes 786440 | tf_op jit(solution)/shard_map/ppermute | solution.py:323
  12.4 5.3 %taps_spectrum.1 = (f32[8,512,256]{2,1,0:T(8,128)S(1)}, bf16[256,256]{1,0:T(8,128)(2,1)S(1)}, bf16[256,256]{1,0:T(8,128)(2,1)S(1)}, f32[32,2,128]{2,1,0:T(2,128)...) custom-call(f32[128,4096]{1,0:T(8,128)} %bitcast.6, ...), custom_call_target="tpu_custom_call" | custom-call | flops 1610612736 | bytes 8388608 | tf_op jit(solution)/shard_map/taps_spectrum/pallas_call | solution.py:369
  17.7 0.0 collective-permute-done.3.refs_1_
  17.7 0.0 copy-done.2
  17.7 0.1 collective-permute-start.2
  17.8 1.1 %collective-permute-done.4.refs_2_ = bf16[128,1024]{1,0:T(8,128)(2,1)S(1)} collective-permute-done((bf16[128,1024]{1,0:T(8,128)(2,1)}, bf16[128,1024]{1,0:T(8,128)(2,1)S(1)}, u32[]{:S(2)}, u32[]{:S(2)}) %collective-permute-start.4) | collective-permute-done | bytes 262176 | tf_op jit(solution)/shard_map/ppermute | solution.py:323
  18.9 0.0 collective-permute-done.5.refs_3_
  18.9 0.0 copy-done.1
  18.9 0.0 copy-start
  18.9 7.9 %grad_input.1 = (f32[8,512,256]{2,1,0:T(8,128)S(1)}, bf16[128,1024]{1,0:T(8,128)(2,1)S(1)}, bf16[128,1024]{1,0:T(8,128)(2,1)S(1)}, bf16[128,1024]{1,0:T(8,128)(2,1)S(1)}, bf16[128,1024]{1,0:T(8,128)(2,1)S(1)}) custom-call(bf16[128,1024]{1,0:T(8,128)(2,1)S(1)} %copy-done.1, bf16[128,1024]{1,0:T(8,128)(2,1)S(1)} %collective-permute-done.3.refs_1_, ...), custom_call_target="tpu_custom_call" | custom-call | flops 3221225472 | bytes 8388608 | tf_op jit(solution)/shard_map/grad_input/pallas_call | solution.py:386
  26.8 1.9 %collective-permute-start.6 = (bf16[128,1024]{1,0:T(8,128)(2,1)S(1)}, bf16[128,1024]{1,0:T(8,128)(2,1)S(1)}, u32[]{:S(2)}, u32[]{:S(2)}) collective-permute-start(bf16[128,1024]{1,0:T(8,128)(2,1)S(1)} %get-tuple-element.42), channel_id=1, source_target_pairs={{0,6},{2,4},{4,2},{6,0},{1,7},{3,5},{5,3},{7,1},{8,14},{10,12},{12... | collective-permute-start | bytes 786440 | tf_op jit(solution)/shard_map/ppermute | solution.py:323
  28.8 1.1 %collective-permute-start.7 = (bf16[128,1024]{1,0:T(8,128)(2,1)S(1)}, bf16[128,1024]{1,0:T(8,128)(2,1)S(1)}, u32[]{:S(2)}, u32[]{:S(2)}) collective-permute-start(bf16[128,1024]{1,0:T(8,128)(2,1)S(1)} %get-tuple-element.43), channel_id=1, source_target_pairs={{0,4},{2,6},{4,0},{6,2},{1,5},{3,7},{5,1},{7,3},{8,12},{10,14},{12... | collective-permute-start | bytes 786440 | tf_op jit(solution)/shard_map/ppermute | solution.py:323
  29.8 0.0 collective-permute-done.refs_1_
  29.8 0.5 %collective-permute-start.8 = (bf16[128,1024]{1,0:T(8,128)(2,1)S(1)}, bf16[128,1024]{1,0:T(8,128)(2,1)S(1)}, u32[]{:S(2)}, u32[]{:S(2)}) collective-permute-start(bf16[128,1024]{1,0:T(8,128)(2,1)S(1)} %get-tuple-element.44), channel_id=1, source_target_pairs={{0,2},{2,0},{4,6},{6,4},{1,3},{3,1},{5,7},{7,5},{8,10},{10,8},{12,... | collective-permute-start | bytes 786440 | tf_op jit(solution)/shard_map/ppermute | solution.py:323
  30.4 0.0 collective-permute-done.1.refs_2_
  30.4 0.0 collective-permute-done.2.refs_3_
  30.4 0.0 copy-done
  30.4 8.5 %grad_filter.1 = (f32[128,4096]{1,0:T(8,128)}, bf16[512,1024]{1,0:T(8,128)(2,1)}) custom-call(bf16[128,1024]{1,0:T(8,128)(2,1)S(1)} %copy-done, bf16[128,1024]{1,0:T(8,128)(2,1)S(1)} %collective-permute-done.refs_1_, bf16[128,1024]{1,0:T(8,128)(2,1)S(1)} %collective-permute-done.1.refs_2_, bf16[128,1024]{1,0:T(8,128)(2,1)S(1)} %collective-permute-done.2.refs_3_, ...), custom_call_target="tpu_custom_call" | custom-call | flops 3221225472 | bytes 8388608 | tf_op jit(solution)/shard_map/grad_filter/pallas_call | solution.py:403
  38.9 0.0 collective-permute-done.6.refs_0_
  38.9 0.7 %gather_pieces.2.held_ref = bf16[512,1024]{1,0:T(8,128)(2,1)} custom-call(bf16[512,1024]{1,0:T(8,128)(2,1)} %get-tuple-element.41.held_ref, bf16[128,1024]{1,0:T(8,128)(2,1)S(1)} %collective-permute-done.6.refs_0_), custom_call_target="tpu_custom_call", output_to_operand_aliasing={{}: (0, {})} | custom-call | tf_op jit(solution)/shard_map/gather_pieces/pallas_call | solution.py:424
  39.6 0.4 collective-permute-done.7.refs_0_
  40.0 0.4 %collective-permute-done.8.refs_1_ = bf16[128,1024]{1,0:T(8,128)(2,1)S(1)} collective-permute-done((bf16[128,1024]{1,0:T(8,128)(2,1)S(1)}, bf16[128,1024]{1,0:T(8,128)(2,1)S(1)}, u32[]{:S(2)}, u32[]{:S(2)}) %collective-permute-start.8) | collective-permute-done | bytes 262176 | tf_op jit(solution)/shard_map/ppermute | solution.py:323
  40.4 0.8 %gather_pieces.3 = bf16[512,1024]{1,0:T(8,128)(2,1)} custom-call(bf16[512,1024]{1,0:T(8,128)(2,1)} %gather_pieces.2.held_ref, bf16[128,1024]{1,0:T(8,128)(2,1)S(1)} %collective-permute-done.7.refs_0_, bf16[128,1024]{1,0:T(8,128)(2,1)S(1)} %collective-permute-done.8.refs_1_), custom_call_target="tpu_custom_call", output_to_operand_aliasing={{}: (0, {})} | custom-call | tf_op jit(solution)/shard_map/gather_pieces/pallas_call | solution.py:424
Async XLA Ops:
  1.6 16.1 %collective-permute-start.3 = (bf16[128,1024]{1,0:T(8,128)(2,1)S(1)}, bf16[128,1024]{1,0:T(8,128)(2,1)S(1)}, u32[]{:S(2)}, u32[]{:S(2)}) collective-permute-start(bf16[128,1024]{1,0:T(8,128)(2,1)S(1)} %dynamic-slice_bitcast_fusion), channel_id=1, source_target_pairs={{0,6},{2,4},{4,2},{6,0},{1,7},{3,5},{5,3},{7,1},{8,14},{10,12},{12... | collective-permute-start | bytes 786440 | tf_op jit(solution)/shard_map/ppermute | solution.py:323
  8.3 9.4 %copy-start.2 = (bf16[128,1024]{1,0:T(8,128)(2,1)S(1)}, bf16[128,1024]{1,0:T(8,128)(2,1)}, u32[]{:S(2)}) copy-start(bf16[128,1024]{1,0:T(8,128)(2,1)} %get-tuple-element.27) | copy-start | bytes 786436
  8.3 10.6 %copy-start.1 = (bf16[128,1024]{1,0:T(8,128)(2,1)S(1)}, bf16[128,1024]{1,0:T(8,128)(2,1)}, u32[]{:S(2)}) copy-start(bf16[128,1024]{1,0:T(8,128)(2,1)} %get-tuple-element.28.refs_0_) | copy-start | bytes 786436
  8.3 10.6 %collective-permute-start.4 = (bf16[128,1024]{1,0:T(8,128)(2,1)}, bf16[128,1024]{1,0:T(8,128)(2,1)S(1)}, u32[]{:S(2)}, u32[]{:S(2)}) collective-permute-start(bf16[128,1024]{1,0:T(8,128)(2,1)} %get-tuple-element.29), channel_id=1, source_target_pairs={{0,2},{2,0},{4,6},{6,4},{1,3},{3,1},{5,7},{7,5},{8,10},{10,8},{12,... | collective-permute-start | bytes 786440 | tf_op jit(solution)/shard_map/ppermute | solution.py:323
  8.9 10.0 %collective-permute-start.5 = (bf16[128,1024]{1,0:T(8,128)(2,1)}, bf16[128,1024]{1,0:T(8,128)(2,1)S(1)}, u32[]{:S(2)}, u32[]{:S(2)}) collective-permute-start(bf16[128,1024]{1,0:T(8,128)(2,1)} %get-tuple-element.30), channel_id=1, source_target_pairs={{0,4},{2,6},{4,0},{6,2},{1,5},{3,7},{5,1},{7,3},{8,12},{10,14},{12... | collective-permute-start | bytes 786440 | tf_op jit(solution)/shard_map/ppermute | solution.py:323
  9.0 20.9 %collective-permute-start = (bf16[128,1024]{1,0:T(8,128)(2,1)}, bf16[128,1024]{1,0:T(8,128)(2,1)S(1)}, u32[]{:S(2)}, u32[]{:S(2)}) collective-permute-start(bf16[128,1024]{1,0:T(8,128)(2,1)} %get-tuple-element.25), channel_id=1, source_target_pairs={{0,2},{2,0},{4,6},{6,4},{1,3},{3,1},{5,7},{7,5},{8,10},{10,8},{12,... | collective-permute-start | bytes 786440 | tf_op jit(solution)/shard_map/ppermute | solution.py:323
  10.9 19.5 %collective-permute-start.1 = (bf16[128,1024]{1,0:T(8,128)(2,1)}, bf16[128,1024]{1,0:T(8,128)(2,1)S(1)}, u32[]{:S(2)}, u32[]{:S(2)}) collective-permute-start(bf16[128,1024]{1,0:T(8,128)(2,1)} %get-tuple-element.26), channel_id=1, source_target_pairs={{0,4},{2,6},{4,0},{6,2},{1,5},{3,7},{5,1},{7,3},{8,12},{10,14},{12... | collective-permute-start | bytes 786440 | tf_op jit(solution)/shard_map/ppermute | solution.py:323
  17.7 12.6 %collective-permute-start.2 = (bf16[128,1024]{1,0:T(8,128)(2,1)S(1)}, bf16[128,1024]{1,0:T(8,128)(2,1)S(1)}, u32[]{:S(2)}, u32[]{:S(2)}) collective-permute-start(bf16[128,1024]{1,0:T(8,128)(2,1)S(1)} %copy-done.2), channel_id=1, source_target_pairs={{0,6},{2,4},{4,2},{6,0},{1,7},{3,5},{5,3},{7,1},{8,14},{10,12},{12... | collective-permute-start | bytes 786440 | tf_op jit(solution)/shard_map/ppermute | solution.py:323
  18.9 11.5 %copy-start = (bf16[128,1024]{1,0:T(8,128)(2,1)S(1)}, bf16[128,1024]{1,0:T(8,128)(2,1)}, u32[]{:S(2)}) copy-start(bf16[128,1024]{1,0:T(8,128)(2,1)} %get-tuple-element.24.refs_0_) | copy-start | bytes 786436
  26.8 12.1 %collective-permute-start.6 = (bf16[128,1024]{1,0:T(8,128)(2,1)S(1)}, bf16[128,1024]{1,0:T(8,128)(2,1)S(1)}, u32[]{:S(2)}, u32[]{:S(2)}) collective-permute-start(bf16[128,1024]{1,0:T(8,128)(2,1)S(1)} %get-tuple-element.42), channel_id=1, source_target_pairs={{0,6},{2,4},{4,2},{6,0},{1,7},{3,5},{5,3},{7,1},{8,14},{10,12},{12... | collective-permute-start | bytes 786440 | tf_op jit(solution)/shard_map/ppermute | solution.py:323
  28.8 11.2 %collective-permute-start.7 = (bf16[128,1024]{1,0:T(8,128)(2,1)S(1)}, bf16[128,1024]{1,0:T(8,128)(2,1)S(1)}, u32[]{:S(2)}, u32[]{:S(2)}) collective-permute-start(bf16[128,1024]{1,0:T(8,128)(2,1)S(1)} %get-tuple-element.43), channel_id=1, source_target_pairs={{0,4},{2,6},{4,0},{6,2},{1,5},{3,7},{5,1},{7,3},{8,12},{10,14},{12... | collective-permute-start | bytes 786440 | tf_op jit(solution)/shard_map/ppermute | solution.py:323
  29.8 10.6 %collective-permute-start.8 = (bf16[128,1024]{1,0:T(8,128)(2,1)S(1)}, bf16[128,1024]{1,0:T(8,128)(2,1)S(1)}, u32[]{:S(2)}, u32[]{:S(2)}) collective-permute-start(bf16[128,1024]{1,0:T(8,128)(2,1)S(1)} %get-tuple-element.44), channel_id=1, source_target_pairs={{0,2},{2,0},{4,6},{6,4},{1,3},{3,1},{5,7},{7,5},{8,10},{10,8},{12,... | collective-permute-start | bytes 786440 | tf_op jit(solution)/shard_map/ppermute | solution.py:323

commit v8 on v7

--- a/solution.py
+++ b/solution.py
@@ -145,7 +145,8 @@
 
 def order_of(what, parts):
     near = list(range(1, parts))
-    return {"grad": near[-1:] + near[:-1], "input": near, "back": near[::-1]}[what]
+    middle = near[:-1][::-1] + near[-1:]
+    return {"grad": near[-1:] + near[:-1], "input": middle, "back": near[::-1]}[what]
 
 
 def places_of(what, parts):

time: 41.4 us -> 41.4 us (level)
  no operation moved by 1% of the time
where the time goes in v8:
time: 41.4 us; the launch traced here: 41.2 us
  Pallas kernels  25.9 us (63%)
  starting transfers between devices  11.7 us (28%)
  waiting for transfers between devices  1.86 us (4%)
  local copies, waits for them, and re-layouts  0.98 us (2%)
  between operations  0.74 us (2%)
    ppermute x9, starting transfers between devices, exchange(): lax.ppermute(block, 'ctx', pair)  11.7 us
    pallas_call x1, Pallas kernels, shards(): pl.pallas_call(functools.partial(filter_kernel, outer=outer, parts=parts)...  8.48 us
    pallas_call x1, Pallas kernels, shards(): pl.pallas_call(functools.partial(input_kernel, outer=outer, parts=parts),...  7.89 us
    pallas_call x1, Pallas kernels, shards(): pl.pallas_call(functools.partial(spectrum_kernel, outer=outer, tables=len...  5.27 us
    pallas_call x1, Pallas kernels, shards(): pl.pallas_call(functools.partial(slice_kernel, parts=parts, pencil=pencil...  2.72 us
    ppermute x9, waiting for transfers between devices, exchange(): lax.ppermute(block, 'ctx', pair)  1.86 us
    pallas_call x2, Pallas kernels, shards(): pl.pallas_call(functools.partial(gather_kernel, first=first, parts=parts,...  1.53 us
    squeeze x1, local copies, waits for them, and re-layouts, pick(): return lax.dynamic_index_in_dim(blocks, place, 0, keepdims=False)  0.97 us
  transfers between devices with their start and end apart: 9, of which 3 were waited for; matrix products, arithmetic and copies ran while one was open for 0% of the time, Pallas kernels for 61%

profile of v8, /device:TPU:0, one launch (start us, length us, event | category | flops | bytes accessed | tf_op | source)
XLA Modules:
  0.0 41.2 jit_solution(16873729105467364664)
XLA Ops:
  0.6 1.0 %dynamic-slice_bitcast_fusion = bf16[128,1024]{1,0:T(8,128)(2,1)S(1)} fusion(bf16[4,128,1024]{2,1,0:T(8,128)(2,1)} %bitcast.5, s32[]{:T(128)S(6)} %select_n.4), kind=kLoop, calls=%fused_computation | loop fusion | bytes 524292 | tf_op jit(solution)/shard_map/jit(dynamic_index_in_dim)/squeeze | solution.py:328
  1.6 4.0 %collective-permute-start.3 = (bf16[128,1024]{1,0:T(8,128)(2,1)S(1)}, bf16[128,1024]{1,0:T(8,128)(2,1)S(1)}, u32[]{:S(2)}, u32[]{:S(2)}) collective-permute-start(bf16[128,1024]{1,0:T(8,128)(2,1)S(1)} %dynamic-slice_bitcast_fusion), channel_id=1, source_target_pairs={{0,6},{2,4},{4,2},{6,0},{1,7},{3,5},{5,3},{7,1},{8,14},{10,12},{12... | collective-permute-start | bytes 786440 | tf_op jit(solution)/shard_map/ppermute | solution.py:324
  5.6 2.7 %slice_blocks.1 = (bf16[128,1024]{1,0:T(8,128)(2,1)}, bf16[128,1024]{1,0:T(8,128)(2,1)}, bf16[128,1024]{1,0:T(8,128)(2,1)}, bf16[128,1024]{1,0:T(8,128)(2,1)}, b...) custom-call(bf16[512,1024]{1,0:T(8,128)(2,1)} %grad_ref.1, bf16[512,1024]{1,0:T(8,128)(2,1)} %input_ref.1), custom_call_target="tpu_custom_call" | custom-call | bytes 3670016 | tf_op jit(solution)/shard_map/slice_blocks/pallas_call | solution.py:352
  8.3 0.0 copy-start.2
  8.3 0.0 copy-start.1
  8.3 0.6 %collective-permute-start.4 = (bf16[128,1024]{1,0:T(8,128)(2,1)}, bf16[128,1024]{1,0:T(8,128)(2,1)S(1)}, u32[]{:S(2)}, u32[]{:S(2)}) collective-permute-start(bf16[128,1024]{1,0:T(8,128)(2,1)} %get-tuple-element.29), channel_id=1, source_target_pairs={{0,2},{2,0},{4,6},{6,4},{1,3},{3,1},{5,7},{7,5},{8,10},{10,8},{12,... | collective-permute-start | bytes 786440 | tf_op jit(solution)/shard_map/ppermute | solution.py:324
  8.9 0.1 collective-permute-start.5
  9.0 2.0 %collective-permute-start = (bf16[128,1024]{1,0:T(8,128)(2,1)}, bf16[128,1024]{1,0:T(8,128)(2,1)S(1)}, u32[]{:S(2)}, u32[]{:S(2)}) collective-permute-start(bf16[128,1024]{1,0:T(8,128)(2,1)} %get-tuple-element.25), channel_id=1, source_target_pairs={{0,4},{2,6},{4,0},{6,2},{1,5},{3,7},{5,1},{7,3},{8,12},{10,14},{12... | collective-permute-start | bytes 786440 | tf_op jit(solution)/shard_map/ppermute | solution.py:324
  10.9 1.5 %collective-permute-start.1 = (bf16[128,1024]{1,0:T(8,128)(2,1)}, bf16[128,1024]{1,0:T(8,128)(2,1)S(1)}, u32[]{:S(2)}, u32[]{:S(2)}) collective-permute-start(bf16[128,1024]{1,0:T(8,128)(2,1)} %get-tuple-element.26), channel_id=1, source_target_pairs={{0,2},{2,0},{4,6},{6,4},{1,3},{3,1},{5,7},{7,5},{8,10},{10,8},{12,... | collective-permute-start | bytes 786440 | tf_op jit(solution)/shard_map/ppermute | solution.py:324
  12.4 5.3 %taps_spectrum.1 = (f32[8,512,256]{2,1,0:T(8,128)S(1)}, bf16[256,256]{1,0:T(8,128)(2,1)S(1)}, bf16[256,256]{1,0:T(8,128)(2,1)S(1)}, f32[32,2,128]{2,1,0:T(2,128)...) custom-call(f32[128,4096]{1,0:T(8,128)} %bitcast.6, ...), custom_call_target="tpu_custom_call" | custom-call | flops 1610612736 | bytes 8388608 | tf_op jit(solution)/shard_map/taps_spectrum/pallas_call | solution.py:370
  17.7 0.0 collective-permute-done.3.refs_1_
  17.7 0.0 copy-done.2
  17.7 0.1 collective-permute-start.2
  17.8 1.1 %collective-permute-done.4.refs_2_ = bf16[128,1024]{1,0:T(8,128)(2,1)S(1)} collective-permute-done((bf16[128,1024]{1,0:T(8,128)(2,1)}, bf16[128,1024]{1,0:T(8,128)(2,1)S(1)}, u32[]{:S(2)}, u32[]{:S(2)}) %collective-permute-start.4) | collective-permute-done | bytes 262176 | tf_op jit(solution)/shard_map/ppermute | solution.py:324
  18.9 0.0 collective-permute-done.5.refs_3_
  18.9 0.0 copy-done.1
  18.9 0.0 copy-start
  18.9 7.9 %grad_input.1 = (f32[8,512,256]{2,1,0:T(8,128)S(1)}, bf16[128,1024]{1,0:T(8,128)(2,1)S(1)}, bf16[128,1024]{1,0:T(8,128)(2,1)S(1)}, bf16[128,1024]{1,0:T(8,128)(2,1)S(1)}, bf16[128,1024]{1,0:T(8,128)(2,1)S(1)}) custom-call(bf16[128,1024]{1,0:T(8,128)(2,1)S(1)} %copy-done.1, bf16[128,1024]{1,0:T(8,128)(2,1)S(1)} %collective-permute-done.3.refs_1_, ...), custom_call_target="tpu_custom_call" | custom-call | flops 3221225472 | bytes 8388608 | tf_op jit(solution)/shard_map/grad_input/pallas_call | solution.py:387
  26.8 1.9 %collective-permute-start.6 = (bf16[128,1024]{1,0:T(8,128)(2,1)S(1)}, bf16[128,1024]{1,0:T(8,128)(2,1)S(1)}, u32[]{:S(2)}, u32[]{:S(2)}) collective-permute-start(bf16[128,1024]{1,0:T(8,128)(2,1)S(1)} %get-tuple-element.42), channel_id=1, source_target_pairs={{0,6},{2,4},{4,2},{6,0},{1,7},{3,5},{5,3},{7,1},{8,14},{10,12},{12... | collective-permute-start | bytes 786440 | tf_op jit(solution)/shard_map/ppermute | solution.py:324
  28.8 1.1 %collective-permute-start.7 = (bf16[128,1024]{1,0:T(8,128)(2,1)S(1)}, bf16[128,1024]{1,0:T(8,128)(2,1)S(1)}, u32[]{:S(2)}, u32[]{:S(2)}) collective-permute-start(bf16[128,1024]{1,0:T(8,128)(2,1)S(1)} %get-tuple-element.43), channel_id=1, source_target_pairs={{0,4},{2,6},{4,0},{6,2},{1,5},{3,7},{5,1},{7,3},{8,12},{10,14},{12... | collective-permute-start | bytes 786440 | tf_op jit(solution)/shard_map/ppermute | solution.py:324
  29.8 0.0 collective-permute-done.refs_1_
  29.8 0.5 %collective-permute-start.8 = (bf16[128,1024]{1,0:T(8,128)(2,1)S(1)}, bf16[128,1024]{1,0:T(8,128)(2,1)S(1)}, u32[]{:S(2)}, u32[]{:S(2)}) collective-permute-start(bf16[128,1024]{1,0:T(8,128)(2,1)S(1)} %get-tuple-element.44), channel_id=1, source_target_pairs={{0,2},{2,0},{4,6},{6,4},{1,3},{3,1},{5,7},{7,5},{8,10},{10,8},{12,... | collective-permute-start | bytes 786440 | tf_op jit(solution)/shard_map/ppermute | solution.py:324
  30.4 0.0 collective-permute-done.1.refs_2_
  30.4 0.0 collective-permute-done.2.refs_3_
  30.4 0.0 copy-done
  30.4 8.5 %grad_filter.1 = (f32[128,4096]{1,0:T(8,128)}, bf16[512,1024]{1,0:T(8,128)(2,1)}) custom-call(bf16[128,1024]{1,0:T(8,128)(2,1)S(1)} %copy-done, bf16[128,1024]{1,0:T(8,128)(2,1)S(1)} %collective-permute-done.refs_1_, bf16[128,1024]{1,0:T(8,128)(2,1)S(1)} %collective-permute-done.1.refs_2_, bf16[128,1024]{1,0:T(8,128)(2,1)S(1)} %collective-permute-done.2.refs_3_, ...), custom_call_target="tpu_custom_call" | custom-call | flops 3221225472 | bytes 8388608 | tf_op jit(solution)/shard_map/grad_filter/pallas_call | solution.py:404
  38.9 0.0 collective-permute-done.6.refs_0_
  38.9 0.7 %gather_pieces.2.held_ref = bf16[512,1024]{1,0:T(8,128)(2,1)} custom-call(bf16[512,1024]{1,0:T(8,128)(2,1)} %get-tuple-element.41.held_ref, bf16[128,1024]{1,0:T(8,128)(2,1)S(1)} %collective-permute-done.6.refs_0_), custom_call_target="tpu_custom_call", output_to_operand_aliasing={{}: (0, {})} | custom-call | tf_op jit(solution)/shard_map/gather_pieces/pallas_call | solution.py:425
  39.6 0.4 collective-permute-done.7.refs_0_
  40.0 0.4 %collective-permute-done.8.refs_1_ = bf16[128,1024]{1,0:T(8,128)(2,1)S(1)} collective-permute-done((bf16[128,1024]{1,0:T(8,128)(2,1)S(1)}, bf16[128,1024]{1,0:T(8,128)(2,1)S(1)}, u32[]{:S(2)}, u32[]{:S(2)}) %collective-permute-start.8) | collective-permute-done | bytes 262176 | tf_op jit(solution)/shard_map/ppermute | solution.py:324
  40.4 0.8 %gather_pieces.3 = bf16[512,1024]{1,0:T(8,128)(2,1)} custom-call(bf16[512,1024]{1,0:T(8,128)(2,1)} %gather_pieces.2.held_ref, bf16[128,1024]{1,0:T(8,128)(2,1)S(1)} %collective-permute-done.7.refs_0_, bf16[128,1024]{1,0:T(8,128)(2,1)S(1)} %collective-permute-done.8.refs_1_), custom_call_target="tpu_custom_call", output_to_operand_aliasing={{}: (0, {})} | custom-call | tf_op jit(solution)/shard_map/gather_pieces/pallas_call | solution.py:425
Async XLA Ops:
  1.6 16.1 %collective-permute-start.3 = (bf16[128,1024]{1,0:T(8,128)(2,1)S(1)}, bf16[128,1024]{1,0:T(8,128)(2,1)S(1)}, u32[]{:S(2)}, u32[]{:S(2)}) collective-permute-start(bf16[128,1024]{1,0:T(8,128)(2,1)S(1)} %dynamic-slice_bitcast_fusion), channel_id=1, source_target_pairs={{0,6},{2,4},{4,2},{6,0},{1,7},{3,5},{5,3},{7,1},{8,14},{10,12},{12... | collective-permute-start | bytes 786440 | tf_op jit(solution)/shard_map/ppermute | solution.py:324
  8.3 9.4 %copy-start.2 = (bf16[128,1024]{1,0:T(8,128)(2,1)S(1)}, bf16[128,1024]{1,0:T(8,128)(2,1)}, u32[]{:S(2)}) copy-start(bf16[128,1024]{1,0:T(8,128)(2,1)} %get-tuple-element.27) | copy-start | bytes 786436
  8.3 10.6 %copy-start.1 = (bf16[128,1024]{1,0:T(8,128)(2,1)S(1)}, bf16[128,1024]{1,0:T(8,128)(2,1)}, u32[]{:S(2)}) copy-start(bf16[128,1024]{1,0:T(8,128)(2,1)} %get-tuple-element.28.refs_0_) | copy-start | bytes 786436
  8.3 10.6 %collective-permute-start.4 = (bf16[128,1024]{1,0:T(8,128)(2,1)}, bf16[128,1024]{1,0:T(8,128)(2,1)S(1)}, u32[]{:S(2)}, u32[]{:S(2)}) collective-permute-start(bf16[128,1024]{1,0:T(8,128)(2,1)} %get-tuple-element.29), channel_id=1, source_target_pairs={{0,2},{2,0},{4,6},{6,4},{1,3},{3,1},{5,7},{7,5},{8,10},{10,8},{12,... | collective-permute-start | bytes 786440 | tf_op jit(solution)/shard_map/ppermute | solution.py:324
  8.9 10.0 %collective-permute-start.5 = (bf16[128,1024]{1,0:T(8,128)(2,1)}, bf16[128,1024]{1,0:T(8,128)(2,1)S(1)}, u32[]{:S(2)}, u32[]{:S(2)}) collective-permute-start(bf16[128,1024]{1,0:T(8,128)(2,1)} %get-tuple-element.30), channel_id=1, source_target_pairs={{0,4},{2,6},{4,0},{6,2},{1,5},{3,7},{5,1},{7,3},{8,12},{10,14},{12... | collective-permute-start | bytes 786440 | tf_op jit(solution)/shard_map/ppermute | solution.py:324
  9.0 20.9 %collective-permute-start = (bf16[128,1024]{1,0:T(8,128)(2,1)}, bf16[128,1024]{1,0:T(8,128)(2,1)S(1)}, u32[]{:S(2)}, u32[]{:S(2)}) collective-permute-start(bf16[128,1024]{1,0:T(8,128)(2,1)} %get-tuple-element.25), channel_id=1, source_target_pairs={{0,4},{2,6},{4,0},{6,2},{1,5},{3,7},{5,1},{7,3},{8,12},{10,14},{12... | collective-permute-start | bytes 786440 | tf_op jit(solution)/shard_map/ppermute | solution.py:324
  10.9 19.4 %collective-permute-start.1 = (bf16[128,1024]{1,0:T(8,128)(2,1)}, bf16[128,1024]{1,0:T(8,128)(2,1)S(1)}, u32[]{:S(2)}, u32[]{:S(2)}) collective-permute-start(bf16[128,1024]{1,0:T(8,128)(2,1)} %get-tuple-element.26), channel_id=1, source_target_pairs={{0,2},{2,0},{4,6},{6,4},{1,3},{3,1},{5,7},{7,5},{8,10},{10,8},{12,... | collective-permute-start | bytes 786440 | tf_op jit(solution)/shard_map/ppermute | solution.py:324
  17.7 12.6 %collective-permute-start.2 = (bf16[128,1024]{1,0:T(8,128)(2,1)S(1)}, bf16[128,1024]{1,0:T(8,128)(2,1)S(1)}, u32[]{:S(2)}, u32[]{:S(2)}) collective-permute-start(bf16[128,1024]{1,0:T(8,128)(2,1)S(1)} %copy-done.2), channel_id=1, source_target_pairs={{0,6},{2,4},{4,2},{6,0},{1,7},{3,5},{5,3},{7,1},{8,14},{10,12},{12... | collective-permute-start | bytes 786440 | tf_op jit(solution)/shard_map/ppermute | solution.py:324
  18.9 11.5 %copy-start = (bf16[128,1024]{1,0:T(8,128)(2,1)S(1)}, bf16[128,1024]{1,0:T(8,128)(2,1)}, u32[]{:S(2)}) copy-start(bf16[128,1024]{1,0:T(8,128)(2,1)} %get-tuple-element.24.refs_0_) | copy-start | bytes 786436
  26.8 12.1 %collective-permute-start.6 = (bf16[128,1024]{1,0:T(8,128)(2,1)S(1)}, bf16[128,1024]{1,0:T(8,128)(2,1)S(1)}, u32[]{:S(2)}, u32[]{:S(2)}) collective-permute-start(bf16[128,1024]{1,0:T(8,128)(2,1)S(1)} %get-tuple-element.42), channel_id=1, source_target_pairs={{0,6},{2,4},{4,2},{6,0},{1,7},{3,5},{5,3},{7,1},{8,14},{10,12},{12... | collective-permute-start | bytes 786440 | tf_op jit(solution)/shard_map/ppermute | solution.py:324
  28.8 11.2 %collective-permute-start.7 = (bf16[128,1024]{1,0:T(8,128)(2,1)S(1)}, bf16[128,1024]{1,0:T(8,128)(2,1)S(1)}, u32[]{:S(2)}, u32[]{:S(2)}) collective-permute-start(bf16[128,1024]{1,0:T(8,128)(2,1)S(1)} %get-tuple-element.43), channel_id=1, source_target_pairs={{0,4},{2,6},{4,0},{6,2},{1,5},{3,7},{5,1},{7,3},{8,12},{10,14},{12... | collective-permute-start | bytes 786440 | tf_op jit(solution)/shard_map/ppermute | solution.py:324
  29.8 10.6 %collective-permute-start.8 = (bf16[128,1024]{1,0:T(8,128)(2,1)S(1)}, bf16[128,1024]{1,0:T(8,128)(2,1)S(1)}, u32[]{:S(2)}, u32[]{:S(2)}) collective-permute-start(bf16[128,1024]{1,0:T(8,128)(2,1)S(1)} %get-tuple-element.44), channel_id=1, source_target_pairs={{0,2},{2,0},{4,6},{6,4},{1,3},{3,1},{5,7},{7,5},{8,10},{10,8},{12,... | collective-permute-start | bytes 786440 | tf_op jit(solution)/shard_map/ppermute | solution.py:324

commit v9 on v7

--- a/solution.py
+++ b/solution.py
@@ -145,7 +145,7 @@
 
 def order_of(what, parts):
     near = list(range(1, parts))
-    return {"grad": near[-1:] + near[:-1], "input": near, "back": near[::-1]}[what]
+    return {"grad": near[-1:] + near[:-1], "input": near, "back": near[-1:] + near[:-1]}[what]
 
 
 def places_of(what, parts):

time: 41.4 us -> 41.4 us (level)
  transfers between devices with their start and end apart: 9 -> 9, of which waited for: 3 -> 2; matrix products, arithmetic and copies ran while one was open for 0% -> 0% of each run, Pallas kernels for 61% -> 61%
where the time goes in v9:
time: 41.4 us; the launch traced here: 41.2 us
  Pallas kernels  25.9 us (63%)
  starting transfers between devices  11.7 us (28%)
  waiting for transfers between devices  1.91 us (5%)
  local copies, waits for them, and re-layouts  0.98 us (2%)
  between operations  0.74 us (2%)
    ppermute x9, starting transfers between devices, exchange(): lax.ppermute(block, 'ctx', pair)  11.7 us
    pallas_call x1, Pallas kernels, shards(): pl.pallas_call(functools.partial(filter_kernel, outer=outer, parts=parts)...  8.48 us
    pallas_call x1, Pallas kernels, shards(): pl.pallas_call(functools.partial(input_kernel, outer=outer, parts=parts),...  7.89 us
    pallas_call x1, Pallas kernels, shards(): pl.pallas_call(functools.partial(spectrum_kernel, outer=outer, tables=len...  5.27 us
    pallas_call x1, Pallas kernels, shards(): pl.pallas_call(functools.partial(slice_kernel, parts=parts, pencil=pencil...  2.72 us
    ppermute x9, waiting for transfers between devices, exchange(): lax.ppermute(block, 'ctx', pair)  1.91 us
    pallas_call x2, Pallas kernels, shards(): pl.pallas_call(functools.partial(gather_kernel, first=first, parts=parts,...  1.53 us
    squeeze x1, local copies, waits for them, and re-layouts, pick(): return lax.dynamic_index_in_dim(blocks, place, 0, keepdims=False)  0.97 us
  transfers between devices with their start and end apart: 9, of which 2 were waited for; matrix products, arithmetic and copies ran while one was open for 0% of the time, Pallas kernels for 61%

profile of v9, /device:TPU:0, one launch (start us, length us, event | category | flops | bytes accessed | tf_op | source)
XLA Modules:
  0.0 41.2 jit_solution(1536725611366626839)
XLA Ops:
  0.6 1.0 %dynamic-slice_bitcast_fusion = bf16[128,1024]{1,0:T(8,128)(2,1)S(1)} fusion(bf16[4,128,1024]{2,1,0:T(8,128)(2,1)} %bitcast.5, s32[]{:T(128)S(6)} %select_n.4), kind=kLoop, calls=%fused_computation | loop fusion | bytes 524292 | tf_op jit(solution)/shard_map/jit(dynamic_index_in_dim)/squeeze | solution.py:327
  1.6 4.0 %collective-permute-start.3 = (bf16[128,1024]{1,0:T(8,128)(2,1)S(1)}, bf16[128,1024]{1,0:T(8,128)(2,1)S(1)}, u32[]{:S(2)}, u32[]{:S(2)}) collective-permute-start(bf16[128,1024]{1,0:T(8,128)(2,1)S(1)} %dynamic-slice_bitcast_fusion), channel_id=1, source_target_pairs={{0,6},{2,4},{4,2},{6,0},{1,7},{3,5},{5,3},{7,1},{8,14},{10,12},{12... | collective-permute-start | bytes 786440 | tf_op jit(solution)/shard_map/ppermute | solution.py:323
  5.6 2.7 %slice_blocks.1 = (bf16[128,1024]{1,0:T(8,128)(2,1)}, bf16[128,1024]{1,0:T(8,128)(2,1)}, bf16[128,1024]{1,0:T(8,128)(2,1)}, bf16[128,1024]{1,0:T(8,128)(2,1)}, b...) custom-call(bf16[512,1024]{1,0:T(8,128)(2,1)} %grad_ref.1, bf16[512,1024]{1,0:T(8,128)(2,1)} %input_ref.1), custom_call_target="tpu_custom_call" | custom-call | bytes 3670016 | tf_op jit(solution)/shard_map/slice_blocks/pallas_call | solution.py:351
  8.3 0.0 copy-start.2
  8.3 0.0 copy-start.1
  8.3 0.6 %collective-permute-start.4 = (bf16[128,1024]{1,0:T(8,128)(2,1)}, bf16[128,1024]{1,0:T(8,128)(2,1)S(1)}, u32[]{:S(2)}, u32[]{:S(2)}) collective-permute-start(bf16[128,1024]{1,0:T(8,128)(2,1)} %get-tuple-element.29), channel_id=1, source_target_pairs={{0,2},{2,0},{4,6},{6,4},{1,3},{3,1},{5,7},{7,5},{8,10},{10,8},{12,... | collective-permute-start | bytes 786440 | tf_op jit(solution)/shard_map/ppermute | solution.py:323
  8.9 0.1 collective-permute-start.5
  9.0 1.9 %collective-permute-start = (bf16[128,1024]{1,0:T(8,128)(2,1)}, bf16[128,1024]{1,0:T(8,128)(2,1)S(1)}, u32[]{:S(2)}, u32[]{:S(2)}) collective-permute-start(bf16[128,1024]{1,0:T(8,128)(2,1)} %get-tuple-element.25), channel_id=1, source_target_pairs={{0,2},{2,0},{4,6},{6,4},{1,3},{3,1},{5,7},{7,5},{8,10},{10,8},{12,... | collective-permute-start | bytes 786440 | tf_op jit(solution)/shard_map/ppermute | solution.py:323
  10.9 1.5 %collective-permute-start.1 = (bf16[128,1024]{1,0:T(8,128)(2,1)}, bf16[128,1024]{1,0:T(8,128)(2,1)S(1)}, u32[]{:S(2)}, u32[]{:S(2)}) collective-permute-start(bf16[128,1024]{1,0:T(8,128)(2,1)} %get-tuple-element.26), channel_id=1, source_target_pairs={{0,4},{2,6},{4,0},{6,2},{1,5},{3,7},{5,1},{7,3},{8,12},{10,14},{12... | collective-permute-start | bytes 786440 | tf_op jit(solution)/shard_map/ppermute | solution.py:323
  12.4 5.3 %taps_spectrum.1 = (f32[8,512,256]{2,1,0:T(8,128)S(1)}, bf16[256,256]{1,0:T(8,128)(2,1)S(1)}, bf16[256,256]{1,0:T(8,128)(2,1)S(1)}, f32[32,2,128]{2,1,0:T(2,128)...) custom-call(f32[128,4096]{1,0:T(8,128)} %bitcast.6, ...), custom_call_target="tpu_custom_call" | custom-call | flops 1610612736 | bytes 8388608 | tf_op jit(solution)/shard_map/taps_spectrum/pallas_call | solution.py:369
  17.7 0.0 collective-permute-done.3.refs_1_
  17.7 0.0 copy-done.2
  17.7 0.1 collective-permute-start.2
  17.8 1.1 %collective-permute-done.4.refs_2_ = bf16[128,1024]{1,0:T(8,128)(2,1)S(1)} collective-permute-done((bf16[128,1024]{1,0:T(8,128)(2,1)}, bf16[128,1024]{1,0:T(8,128)(2,1)S(1)}, u32[]{:S(2)}, u32[]{:S(2)}) %collective-permute-start.4) | collective-permute-done | bytes 262176 | tf_op jit(solution)/shard_map/ppermute | solution.py:323
  18.9 0.0 collective-permute-done.5.refs_3_
  18.9 0.0 copy-done.1
  18.9 0.0 copy-start
  18.9 7.9 %grad_input.1 = (f32[8,512,256]{2,1,0:T(8,128)S(1)}, bf16[128,1024]{1,0:T(8,128)(2,1)S(1)}, bf16[128,1024]{1,0:T(8,128)(2,1)S(1)}, bf16[128,1024]{1,0:T(8,128)(2,1)S(1)}, bf16[128,1024]{1,0:T(8,128)(2,1)S(1)}) custom-call(bf16[128,1024]{1,0:T(8,128)(2,1)S(1)} %copy-done.1, bf16[128,1024]{1,0:T(8,128)(2,1)S(1)} %collective-permute-done.3.refs_1_, ...), custom_call_target="tpu_custom_call" | custom-call | flops 3221225472 | bytes 8388608 | tf_op jit(solution)/shard_map/grad_input/pallas_call | solution.py:386
  26.8 1.9 %collective-permute-start.6 = (bf16[128,1024]{1,0:T(8,128)(2,1)S(1)}, bf16[128,1024]{1,0:T(8,128)(2,1)S(1)}, u32[]{:S(2)}, u32[]{:S(2)}) collective-permute-start(bf16[128,1024]{1,0:T(8,128)(2,1)S(1)} %get-tuple-element.42), channel_id=1, source_target_pairs={{0,6},{2,4},{4,2},{6,0},{1,7},{3,5},{5,3},{7,1},{8,14},{10,12},{12... | collective-permute-start | bytes 786440 | tf_op jit(solution)/shard_map/ppermute | solution.py:323
  28.8 0.5 %collective-permute-start.7 = (bf16[128,1024]{1,0:T(8,128)(2,1)S(1)}, bf16[128,1024]{1,0:T(8,128)(2,1)S(1)}, u32[]{:S(2)}, u32[]{:S(2)}) collective-permute-start(bf16[128,1024]{1,0:T(8,128)(2,1)S(1)} %get-tuple-element.43), channel_id=1, source_target_pairs={{0,2},{2,0},{4,6},{6,4},{1,3},{3,1},{5,7},{7,5},{8,10},{10,8},{12,... | collective-permute-start | bytes 786440 | tf_op jit(solution)/shard_map/ppermute | solution.py:323
  29.2 0.0 collective-permute-done.refs_1_
  29.2 1.1 %collective-permute-start.8 = (bf16[128,1024]{1,0:T(8,128)(2,1)S(1)}, bf16[128,1024]{1,0:T(8,128)(2,1)S(1)}, u32[]{:S(2)}, u32[]{:S(2)}) collective-permute-start(bf16[128,1024]{1,0:T(8,128)(2,1)S(1)} %get-tuple-element.44), channel_id=1, source_target_pairs={{0,4},{2,6},{4,0},{6,2},{1,5},{3,7},{5,1},{7,3},{8,12},{10,14},{12... | collective-permute-start | bytes 786440 | tf_op jit(solution)/shard_map/ppermute | solution.py:323
  30.4 0.0 collective-permute-done.1.refs_2_
  30.4 0.0 collective-permute-done.2.refs_3_
  30.4 0.0 copy-done
  30.4 8.5 %grad_filter.1 = (f32[128,4096]{1,0:T(8,128)}, bf16[512,1024]{1,0:T(8,128)(2,1)}) custom-call(bf16[128,1024]{1,0:T(8,128)(2,1)S(1)} %copy-done, bf16[128,1024]{1,0:T(8,128)(2,1)S(1)} %collective-permute-done.refs_1_, bf16[128,1024]{1,0:T(8,128)(2,1)S(1)} %collective-permute-done.1.refs_2_, bf16[128,1024]{1,0:T(8,128)(2,1)S(1)} %collective-permute-done.2.refs_3_, ...), custom_call_target="tpu_custom_call" | custom-call | flops 3221225472 | bytes 8388608 | tf_op jit(solution)/shard_map/grad_filter/pallas_call | solution.py:403
  38.9 0.0 collective-permute-done.6.refs_0_
  38.9 0.7 %gather_pieces.2.held_ref = bf16[512,1024]{1,0:T(8,128)(2,1)} custom-call(bf16[512,1024]{1,0:T(8,128)(2,1)} %get-tuple-element.41.held_ref, bf16[128,1024]{1,0:T(8,128)(2,1)S(1)} %collective-permute-done.6.refs_0_), custom_call_target="tpu_custom_call", output_to_operand_aliasing={{}: (0, {})} | custom-call | tf_op jit(solution)/shard_map/gather_pieces/pallas_call | solution.py:424
  39.6 0.8 %collective-permute-done.7.refs_0_ = bf16[128,1024]{1,0:T(8,128)(2,1)S(1)} collective-permute-done((bf16[128,1024]{1,0:T(8,128)(2,1)S(1)}, bf16[128,1024]{1,0:T(8,128)(2,1)S(1)}, u32[]{:S(2)}, u32[]{:S(2)}) %collective-permute-start.7) | collective-permute-done | bytes 262176 | tf_op jit(solution)/shard_map/ppermute | solution.py:323
  40.4 0.0 collective-permute-done.8.refs_1_
  40.4 0.8 %gather_pieces.3 = bf16[512,1024]{1,0:T(8,128)(2,1)} custom-call(bf16[512,1024]{1,0:T(8,128)(2,1)} %gather_pieces.2.held_ref, bf16[128,1024]{1,0:T(8,128)(2,1)S(1)} %collective-permute-done.7.refs_0_, bf16[128,1024]{1,0:T(8,128)(2,1)S(1)} %collective-permute-done.8.refs_1_), custom_call_target="tpu_custom_call", output_to_operand_aliasing={{}: (0, {})} | custom-call | tf_op jit(solution)/shard_map/gather_pieces/pallas_call | solution.py:424
Async XLA Ops:
  1.6 16.1 %collective-permute-start.3 = (bf16[128,1024]{1,0:T(8,128)(2,1)S(1)}, bf16[128,1024]{1,0:T(8,128)(2,1)S(1)}, u32[]{:S(2)}, u32[]{:S(2)}) collective-permute-start(bf16[128,1024]{1,0:T(8,128)(2,1)S(1)} %dynamic-slice_bitcast_fusion), channel_id=1, source_target_pairs={{0,6},{2,4},{4,2},{6,0},{1,7},{3,5},{5,3},{7,1},{8,14},{10,12},{12... | collective-permute-start | bytes 786440 | tf_op jit(solution)/shard_map/ppermute | solution.py:323
  8.3 9.4 %copy-start.2 = (bf16[128,1024]{1,0:T(8,128)(2,1)S(1)}, bf16[128,1024]{1,0:T(8,128)(2,1)}, u32[]{:S(2)}) copy-start(bf16[128,1024]{1,0:T(8,128)(2,1)} %get-tuple-element.27) | copy-start | bytes 786436
  8.3 10.6 %copy-start.1 = (bf16[128,1024]{1,0:T(8,128)(2,1)S(1)}, bf16[128,1024]{1,0:T(8,128)(2,1)}, u32[]{:S(2)}) copy-start(bf16[128,1024]{1,0:T(8,128)(2,1)} %get-tuple-element.28.refs_0_) | copy-start | bytes 786436
  8.3 10.6 %collective-permute-start.4 = (bf16[128,1024]{1,0:T(8,128)(2,1)}, bf16[128,1024]{1,0:T(8,128)(2,1)S(1)}, u32[]{:S(2)}, u32[]{:S(2)}) collective-permute-start(bf16[128,1024]{1,0:T(8,128)(2,1)} %get-tuple-element.29), channel_id=1, source_target_pairs={{0,2},{2,0},{4,6},{6,4},{1,3},{3,1},{5,7},{7,5},{8,10},{10,8},{12,... | collective-permute-start | bytes 786440 | tf_op jit(solution)/shard_map/ppermute | solution.py:323
  8.9 10.0 %collective-permute-start.5 = (bf16[128,1024]{1,0:T(8,128)(2,1)}, bf16[128,1024]{1,0:T(8,128)(2,1)S(1)}, u32[]{:S(2)}, u32[]{:S(2)}) collective-permute-start(bf16[128,1024]{1,0:T(8,128)(2,1)} %get-tuple-element.30), channel_id=1, source_target_pairs={{0,4},{2,6},{4,0},{6,2},{1,5},{3,7},{5,1},{7,3},{8,12},{10,14},{12... | collective-permute-start | bytes 786440 | tf_op jit(solution)/shard_map/ppermute | solution.py:323
  9.0 20.3 %collective-permute-start = (bf16[128,1024]{1,0:T(8,128)(2,1)}, bf16[128,1024]{1,0:T(8,128)(2,1)S(1)}, u32[]{:S(2)}, u32[]{:S(2)}) collective-permute-start(bf16[128,1024]{1,0:T(8,128)(2,1)} %get-tuple-element.25), channel_id=1, source_target_pairs={{0,2},{2,0},{4,6},{6,4},{1,3},{3,1},{5,7},{7,5},{8,10},{10,8},{12,... | collective-permute-start | bytes 786440 | tf_op jit(solution)/shard_map/ppermute | solution.py:323
  10.9 19.5 %collective-permute-start.1 = (bf16[128,1024]{1,0:T(8,128)(2,1)}, bf16[128,1024]{1,0:T(8,128)(2,1)S(1)}, u32[]{:S(2)}, u32[]{:S(2)}) collective-permute-start(bf16[128,1024]{1,0:T(8,128)(2,1)} %get-tuple-element.26), channel_id=1, source_target_pairs={{0,4},{2,6},{4,0},{6,2},{1,5},{3,7},{5,1},{7,3},{8,12},{10,14},{12... | collective-permute-start | bytes 786440 | tf_op jit(solution)/shard_map/ppermute | solution.py:323
  17.7 12.6 %collective-permute-start.2 = (bf16[128,1024]{1,0:T(8,128)(2,1)S(1)}, bf16[128,1024]{1,0:T(8,128)(2,1)S(1)}, u32[]{:S(2)}, u32[]{:S(2)}) collective-permute-start(bf16[128,1024]{1,0:T(8,128)(2,1)S(1)} %copy-done.2), channel_id=1, source_target_pairs={{0,6},{2,4},{4,2},{6,0},{1,7},{3,5},{5,3},{7,1},{8,14},{10,12},{12... | collective-permute-start | bytes 786440 | tf_op jit(solution)/shard_map/ppermute | solution.py:323
  18.9 11.5 %copy-start = (bf16[128,1024]{1,0:T(8,128)(2,1)S(1)}, bf16[128,1024]{1,0:T(8,128)(2,1)}, u32[]{:S(2)}) copy-start(bf16[128,1024]{1,0:T(8,128)(2,1)} %get-tuple-element.24.refs_0_) | copy-start | bytes 786436
  26.8 12.1 %collective-permute-start.6 = (bf16[128,1024]{1,0:T(8,128)(2,1)S(1)}, bf16[128,1024]{1,0:T(8,128)(2,1)S(1)}, u32[]{:S(2)}, u32[]{:S(2)}) collective-permute-start(bf16[128,1024]{1,0:T(8,128)(2,1)S(1)} %get-tuple-element.42), channel_id=1, source_target_pairs={{0,6},{2,4},{4,2},{6,0},{1,7},{3,5},{5,3},{7,1},{8,14},{10,12},{12... | collective-permute-start | bytes 786440 | tf_op jit(solution)/shard_map/ppermute | solution.py:323
  28.8 11.7 %collective-permute-start.7 = (bf16[128,1024]{1,0:T(8,128)(2,1)S(1)}, bf16[128,1024]{1,0:T(8,128)(2,1)S(1)}, u32[]{:S(2)}, u32[]{:S(2)}) collective-permute-start(bf16[128,1024]{1,0:T(8,128)(2,1)S(1)} %get-tuple-element.43), channel_id=1, source_target_pairs={{0,2},{2,0},{4,6},{6,4},{1,3},{3,1},{5,7},{7,5},{8,10},{10,8},{12,... | collective-permute-start | bytes 786440 | tf_op jit(solution)/shard_map/ppermute | solution.py:323
  29.2 11.2 %collective-permute-start.8 = (bf16[128,1024]{1,0:T(8,128)(2,1)S(1)}, bf16[128,1024]{1,0:T(8,128)(2,1)S(1)}, u32[]{:S(2)}, u32[]{:S(2)}) collective-permute-start(bf16[128,1024]{1,0:T(8,128)(2,1)S(1)} %get-tuple-element.44), channel_id=1, source_target_pairs={{0,4},{2,6},{4,0},{6,2},{1,5},{3,7},{5,1},{7,3},{8,12},{10,14},{12... | collective-permute-start | bytes 786440 | tf_op jit(solution)/shard_map/ppermute | solution.py:323
